TPU v7x, 128 devices: a whole 4x4x4 slice. The times are simulated.
128 devices in a mesh: group: 16 (over x, z), lane: 8 (over y, core).
Axes of the slice: x: 4, y: 4, z: 4, core: 2. Of those that a mesh axis runs over, the one named last changes fastest.
Arguments:
- kv_latent: bfloat16 [1024, 128, 512], P(('group', 'lane')), may hold values from -6 to 6
- kv_rope: bfloat16 [1024, 64, 128], P(('group', 'lane')), may hold values from -6 to 6
- page_table: int32 [512, 2], P(('group', 'lane')), may hold values from 0 to 7, as said below
- seq_pages: int32 [64], replicated, may hold values from 1 to 16, 512 in all
- destiny: int32 [64], replicated, may hold values from 0 to 15, as said below
- q_latent: bfloat16 [64, 32, 512], P('group'), may hold values from -150 to 150
- q_rope: bfloat16 [64, 32, 64], P('group'), may hold values from -21 to 21
- new_latent: bfloat16 [64, 512], P('group'), may hold values from -6 to 6
- new_rope: bfloat16 [64, 64], P('group'), may hold values from -6 to 6
- residual_in: bfloat16 [64, 7168], P('group', 'lane'), may hold values from -0.75 to 0.75
- w_uv: bfloat16 [32, 512, 128], replicated, may hold values from -0.25 to 0.25
- w_out: bfloat16 [4096, 7168], P(None, 'lane'), may hold values from -0.09375 to 0.09375
- norm_gain: bfloat16 [7168], P('lane'), may hold values from 0.25 to 1.75
- w_gate: bfloat16 [16, 7168, 2048], P('group', 'lane'), may hold values from -0.0625 to 0.0625
- w_up: bfloat16 [16, 7168, 2048], P('group', 'lane'), may hold values from -0.0625 to 0.0625
- w_down: bfloat16 [16, 2048, 7168], P('group', None, 'lane'), may hold values from -0.125 to 0.125
- routes: int32 [128, 4], P('group'), may hold values from 0 to 15, all different within a row; in each aligned block of 8 rows (0 to 7, 8 to 15, ...) at most 2 rows name the same one
- route_gates: float32 [128, 4], P('group'), may hold values from 0.05 to 0.5
Outputs:
- layer_out: bfloat16 [128, 7168], P('group', 'lane')
- kept_latent: bfloat16 [2048, 128, 512], P(('group', 'lane'))
- kept_rope: bfloat16 [2048, 64, 128], P(('group', 'lane'))
Inputs may be any that keep to these rules, and one draw needn't show every extreme that they name: `destiny`: half of the groups are keepers and keep their sequences; each sequence of an emptied group goes to a keeper, the sequences of one emptied group to different keepers, and every keeper receives exactly 4 sequences. `page_table`: on each device, its 4 rows name every pool page of the device once. `routes`: in the rows of one group no expert is named by more than 2 rows.
All inputs are finite; a program needn't handle non-finite values.
Results may differ from a plain program's by a relative error of at most 0.027.
Values may be sent and summed in bfloat16 or wider, within the bound.
No kernel may reach another device: no remote copies, remote signals or barrier semaphores. Data moves between devices by JAX's collectives and lax.ppermute only.
A program may use at most 128 MiB of HBM per device.

v0:
```python
import jax
import jax.numpy as jnp
from jax import lax
from jax.sharding import PartitionSpec as P

D = 7168


MASKED = -1e30
EPSILON = 1e-06


def merged_2(value, axis, join):
    pieces = jax.tree.map(lambda part: lax.all_gather(part, axis), value)
    head = jax.tree.map(lambda part: part[0], pieces)
    tail = jax.tree.map(lambda part: part[1:], pieces)
    subtotal, _ = lax.scan(lambda subtotal, slab: (join(subtotal, slab), None), head, tail)
    return subtotal


def combine_parts(first, second):
    ceiling = jnp.maximum(first[0], second[0])
    first_weight = jnp.exp(first[0] - ceiling)
    second_weight = jnp.exp(second[0] - ceiling)
    normalizer = first[1] * first_weight + second[1] * second_weight
    summed = first[2] * first_weight[..., None] + second[2] * second_weight[..., None]
    return (ceiling, normalizer, summed)


def lane_merge(parts):
    return merged_2(parts, "lane", combine_parts)


def attend_pages(latent_pages, rotary_pages, query_latent, query_rotary, visible, score_scale):
    scores = jnp.einsum(
        "nhc,nptc->nhpt", query_latent, latent_pages, preferred_element_type=jnp.float32
    )
    scores = scores + jnp.einsum(
        "nhr,nprt->nhpt", query_rotary, rotary_pages, preferred_element_type=jnp.float32
    )
    scores = scores * score_scale
    shown = visible[:, None, :, None]
    highest = jnp.max(jnp.where(shown, scores, MASKED), axis=(2, 3))
    weights = jnp.exp(jnp.where(shown, scores - highest[:, :, None, None], MASKED))
    normalizer = jnp.sum(weights, axis=(2, 3))
    summed = jnp.einsum(
        "nhpt,nptc->nhc",
        weights.astype(jnp.bfloat16),
        latent_pages,
        preferred_element_type=jnp.float32,
    )
    return (highest, normalizer, summed)


def finish_softmax(parts, query_latent, query_rotary, fresh_latent, fresh_rotary, score_scale):
    highest, normalizer, summed = parts
    own_score = jnp.einsum(
        "nhc,nc->nh", query_latent, fresh_latent, preferred_element_type=jnp.float32
    )
    own_score = (
        own_score
        + jnp.einsum("nhr,nr->nh", query_rotary, fresh_rotary, preferred_element_type=jnp.float32)
    ) * score_scale
    ceiling = jnp.maximum(highest, own_score)
    old_weight = jnp.exp(highest - ceiling)
    own_weight = jnp.exp(own_score - ceiling)
    summed = (
        summed * old_weight[..., None]
        + own_weight[..., None] * fresh_latent.astype(jnp.float32)[:, None, :]
    )
    normalizer = normalizer * old_weight + own_weight
    return (summed / normalizer[..., None]).astype(jnp.bfloat16)


def outbound(values, index, present):
    picked = jnp.take(values, index, axis=0)
    shape = (present.shape[0],) + (1,) * (values.ndim - 1)
    return jnp.where(present.reshape(shape), picked, jnp.zeros_like(picked))


def keep_pages(pages, visible):
    masked = jnp.where(visible[:, :, None, None], pages, jnp.zeros_like(pages))
    return masked.reshape((-1,) + pages.shape[2:])


def per_device(
    kv_latent,
    kv_rope,
    page_table,
    seq_pages,
    destiny,
    q_latent,
    q_rope,
    new_latent,
    new_rope,
    residual_in,
    w_uv,
    w_out,
    norm_gain,
    w_gate,
    w_up,
    w_down,
    routes,
    route_gates,
):
    group_count = lax.axis_size("group")
    lane_count = lax.axis_size("lane")
    my_group = lax.axis_index("group")
    my_lane = lax.axis_index("lane")
    per_group = q_latent.shape[0]
    local_pages = page_table.shape[1]
    score_scale = (w_uv.shape[2] + q_rope.shape[2]) ** (-0.5)
    group_ids = jnp.arange(group_count, dtype=jnp.int32)
    slot_ids = jnp.arange(per_group, dtype=jnp.int32)
    dest_grid = destiny.reshape(group_count, per_group)
    leaving = dest_grid != group_ids[:, None]
    arrival = (dest_grid[None, :, :] == group_ids[:, None, None]) & leaving[None, :, :]
    arrives = jnp.any(arrival, axis=2)
    arrival_rank = jnp.cumsum(arrives.astype(jnp.int32), axis=1) - 1
    seq_choice = jnp.sum(arrival.astype(jnp.int32) * slot_ids[None, None, :], axis=2)
    length_grid = seq_pages.reshape(group_count, per_group)
    mine_arrives = lax.dynamic_index_in_dim(arrives, my_group, 0, keepdims=False)
    mine_rank = lax.dynamic_index_in_dim(arrival_rank, my_group, 0, keepdims=False)
    mine_choice = lax.dynamic_index_in_dim(seq_choice, my_group, 0, keepdims=False)
    picking = (mine_arrives[None, :] & (mine_rank[None, :] == slot_ids[:, None])).astype(jnp.int32)
    source_of = jnp.sum(picking * group_ids[None, :], axis=1)
    source_length = jnp.take_along_axis(length_grid, mine_choice[:, None], axis=1)[:, 0]
    incoming_length = jnp.sum(picking * source_length[None, :], axis=1)
    my_targets = lax.dynamic_index_in_dim(dest_grid, my_group, 0, keepdims=False)
    my_leaving = lax.dynamic_index_in_dim(leaving, my_group, 0, keepdims=False)
    bound_for = (my_targets[None, :] == group_ids[:, None]) & my_leaving[None, :]
    outbound_index = jnp.sum(bound_for.astype(jnp.int32) * slot_ids[None, :], axis=1)
    outbound_present = jnp.any(bound_for, axis=1)
    staying = jnp.logical_not(jnp.any(my_leaving))
    own_length = lax.dynamic_index_in_dim(length_grid, my_group, 0, keepdims=False)
    page_ids = jnp.arange(local_pages, dtype=jnp.int32) * lane_count + my_lane
    own_visible = page_ids[None, :] < own_length[:, None]
    incoming_visible = page_ids[None, :] < incoming_length[:, None]
    own_latent = jnp.take(kv_latent, page_table, axis=0)
    own_rotary = jnp.take(kv_rope, page_table, axis=0)
    arrived = (
        lax.all_to_all(
            outbound(own_latent, outbound_index, outbound_present),
            "group",
            split_axis=0,
            concat_axis=0,
            tiled=True,
        ),
        lax.all_to_all(
            outbound(own_rotary, outbound_index, outbound_present),
            "group",
            split_axis=0,
            concat_axis=0,
            tiled=True,
        ),
        lax.all_to_all(
            outbound(q_latent, outbound_index, outbound_present),
            "group",
            split_axis=0,
            concat_axis=0,
            tiled=True,
        ),
        lax.all_to_all(
            outbound(q_rope, outbound_index, outbound_present),
            "group",
            split_axis=0,
            concat_axis=0,
            tiled=True,
        ),
        lax.all_to_all(
            outbound(new_latent, outbound_index, outbound_present),
            "group",
            split_axis=0,
            concat_axis=0,
            tiled=True,
        ),
        lax.all_to_all(
            outbound(new_rope, outbound_index, outbound_present),
            "group",
            split_axis=0,
            concat_axis=0,
            tiled=True,
        ),
        lax.all_to_all(
            outbound(residual_in, outbound_index, outbound_present),
            "group",
            split_axis=0,
            concat_axis=0,
            tiled=True,
        ),
    )
    incoming = [jnp.take(values, source_of, axis=0) for values in arrived]
    own_parts = attend_pages(own_latent, own_rotary, q_latent, q_rope, own_visible, score_scale)
    incoming_parts = attend_pages(
        incoming[0], incoming[1], incoming[2], incoming[3], incoming_visible, score_scale
    )
    joined = tuple(
        (
            jnp.concatenate([first, second], axis=0)
            for first, second in zip(own_parts, incoming_parts)
        )
    )
    merged = lane_merge(joined)
    all_query_latent = jnp.concatenate([q_latent, incoming[2]], axis=0)
    all_query_rotary = jnp.concatenate([q_rope, incoming[3]], axis=0)
    all_fresh_latent = jnp.concatenate([new_latent, incoming[4]], axis=0)
    all_fresh_rotary = jnp.concatenate([new_rope, incoming[5]], axis=0)
    out_latent = finish_softmax(
        merged, all_query_latent, all_query_rotary, all_fresh_latent, all_fresh_rotary, score_scale
    )
    carried = jnp.concatenate([residual_in, incoming[6]], axis=0)
    landed_latent, landed_rotary = (incoming[0], incoming[1])
    kept_latent = jnp.concatenate(
        [keep_pages(own_latent, own_visible), keep_pages(landed_latent, incoming_visible)], axis=0
    )
    kept_rope = jnp.concatenate(
        [keep_pages(own_rotary, own_visible), keep_pages(landed_rotary, incoming_visible)], axis=0
    )
    kept_latent = jnp.where(staying, kept_latent, jnp.zeros_like(kept_latent))
    kept_rope = jnp.where(staying, kept_rope, jnp.zeros_like(kept_rope))
    slot_count = out_latent.shape[0]
    heads_out = jnp.einsum(
        "nhc,hcv->nhv", out_latent, w_uv, preferred_element_type=jnp.float32
    ).astype(jnp.bfloat16)
    heads_flat = heads_out.reshape(slot_count, -1)
    hidden = carried.astype(jnp.float32) + jnp.dot(
        heads_flat, w_out, preferred_element_type=jnp.float32
    )
    hidden = jnp.where(staying, hidden, jnp.zeros_like(hidden)).astype(jnp.bfloat16)
    route_count = routes.shape[1]
    capacity = max(2, (slot_count * route_count + group_count - 1) // group_count)
    expert_ids = jnp.arange(group_count, dtype=jnp.int32)
    capacity_ids = jnp.arange(capacity, dtype=jnp.int32)
    onehot = (routes[:, :, None] == expert_ids[None, None, :]).astype(jnp.int32)
    per_row = jnp.sum(onehot, axis=1)
    before = jnp.cumsum(per_row, axis=0) - per_row
    slot_of = jnp.sum(onehot * before[:, None, :], axis=2)
    placement = onehot[:, :, :, None] * (
        slot_of[:, :, None, None] == capacity_ids[None, None, None, :]
    ).astype(jnp.int32)
    placement = placement.astype(jnp.float32) * staying.astype(jnp.float32)
    dispatch_matrix = jnp.sum(placement, axis=1).reshape(slot_count, group_count * capacity)
    combine_weights = jnp.sum(placement * route_gates[:, :, None, None], axis=1).reshape(
        slot_count, group_count * capacity
    )
    outgoing = jnp.einsum(
        "rs,rd->sd",
        dispatch_matrix.astype(jnp.bfloat16),
        hidden,
        preferred_element_type=jnp.float32,
    )
    outgoing = outgoing.astype(jnp.bfloat16).reshape(group_count, capacity, -1)
    gain_slice = norm_gain.astype(jnp.float32)
    received = lax.all_to_all(outgoing, "group", split_axis=0, concat_axis=0, tiled=True)
    item_count = received.shape[1]
    row_block = received.reshape(group_count * item_count, -1)
    widened = row_block.astype(jnp.float32)
    squares = jnp.sum(widened * widened, axis=1)
    scaled = (widened * gain_slice[None, :]).astype(jnp.bfloat16)
    gate_part = jnp.dot(scaled, w_gate[0], preferred_element_type=jnp.float32)
    up_part = jnp.dot(scaled, w_up[0], preferred_element_type=jnp.float32)
    gate_total, up_total, square_total = lax.psum((gate_part, up_part, squares), "lane")
    factor = lax.rsqrt(square_total / D + EPSILON)[:, None]
    activated = (jax.nn.silu(gate_total * factor) * (up_total * factor)).astype(jnp.bfloat16)
    produced = jnp.dot(activated, w_down[0], preferred_element_type=jnp.float32).astype(
        jnp.bfloat16
    )
    produced = produced.reshape(group_count, item_count, -1)
    returned_rows = lax.all_to_all(produced, "group", split_axis=0, concat_axis=0, tiled=True)
    flat_returned = returned_rows.reshape(group_count * capacity, -1).astype(jnp.float32)
    mixed = hidden.astype(jnp.float32) + jnp.dot(
        combine_weights, flat_returned, precision=lax.Precision.HIGHEST
    )
    return (mixed.astype(jnp.bfloat16), kept_latent, kept_rope)


def solution(mesh):
    in_specs = (
        P(("group", "lane"), None, None),
        P(("group", "lane"), None, None),
        P(("group", "lane"), None),
        P(),
        P(),
        P("group", None, None),
        P("group", None, None),
        P("group", None),
        P("group", None),
        P("group", "lane"),
        P(),
        P(None, "lane"),
        P("lane"),
        P("group", "lane", None),
        P("group", "lane", None),
        P("group", None, "lane"),
        P("group", None),
        P("group", None),
    )
    out_specs = (
        P("group", "lane"),
        P(("group", "lane"), None, None),
        P(("group", "lane"), None, None),
    )
    return jax.shard_map(
        per_device, mesh=mesh, in_specs=in_specs, out_specs=out_specs, check_vma=False
    )
```

profile of v0, /device:TPU:0, one launch (start us, length us, event | category | flops | bytes accessed | tf_op | source)
XLA Modules:
  0.0 321.7 jit_solution(5392130020100848918)
XLA Ops:
  12.5 8.0 %all-to-all-start.3 = ((bf16[16,2,1024]{2,1,0:T(2,128)(2,1)}), bf16[16,2,1024]{2,1,0:T(2,128)(2,1)S(1)}, u32[]{:S(2)}, u32[]{:S(2)}) async-start(bf16[16,2,1024]{2,1,0:T(2,128)(2,1)} %reshape.659), calls=%async_computation.3 | async-start | bytes 131072 | tf_op jit(solution)/shard_map/all_to_all | solution.py:163
  28.3 7.3 %all-to-all-start.4 = ((bf16[16,2,64,128]{3,2,1,0:T(8,128)(2,1)}), bf16[16,2,64,128]{3,2,1,0:T(8,128)(2,1)}, u32[]{:S(2)}, u32[]{:S(2)}) async-start(bf16[16,2,64,128]{3,2,1,0:T(8,128)(2,1)} %select_select_fusion.2), calls=%async_computation.4 | async-start | bytes 1048576 | tf_op jit(solution)/shard_map/all_to_all | solution.py:149
  40.5 6.0 %all-to-all-done.4 = bf16[16,2,64,128]{3,2,1,0:T(8,128)(2,1)} async-done(((bf16[16,2,64,128]{3,2,1,0:T(8,128)(2,1)}), bf16[16,2,64,128]{3,2,1,0:T(8,128)(2,1)}, u32[]{:S(2)}, u32[]{:S(2)}) %all-to-all-start.4) | async-done | bytes 524320 | tf_op jit(solution)/shard_map/all_to_all | solution.py:149
  46.5 4.2 %all-to-all-start.1 = ((bf16[16,32,512]{2,1,0:T(8,128)(2,1)}), bf16[16,32,512]{2,1,0:T(8,128)(2,1)}, u32[]{:S(2)}, u32[]{:S(2)}) async-start(bf16[16,32,512]{2,1,0:T(8,128)(2,1)} %select_select_fusion.3), calls=%async_computation.1 | async-start | bytes 1048576 | tf_op jit(solution)/shard_map/all_to_all | solution.py:156
  50.8 4.7 %select_select_fusion = bf16[16,2,128,512]{3,2,1,0:T(8,128)(2,1)} fusion(bf16[16,2,128,512]{3,2,1,0:T(8,128)(2,1)} %gather_fusion.6, pred[16]{0:T(512)(128)(4,1)S(1)} %compare_and_fusion.1, pred[16]{0:T(512)(128)(4,1)S(1)} %fusion.70), kind=kLoop, calls=%fused_computation.25 | loop fusion | flops 4194304 | bytes 8388640 | tf_op jit(solution)/shard_map/jit(_where)/select_n | solution.py:78
  55.5 5.4 %all-to-all-done.1 = bf16[16,32,512]{2,1,0:T(8,128)(2,1)} async-done(((bf16[16,32,512]{2,1,0:T(8,128)(2,1)}), bf16[16,32,512]{2,1,0:T(8,128)(2,1)}, u32[]{:S(2)}, u32[]{:S(2)}) %all-to-all-start.1) | async-done | bytes 524320 | tf_op jit(solution)/shard_map/all_to_all | solution.py:156
  60.9 4.5 %all-to-all-start.2 = ((bf16[16,2,128,512]{3,2,1,0:T(8,128)(2,1)}), bf16[16,2,128,512]{3,2,1,0:T(8,128)(2,1)}, u32[]{:S(2)}, u32[]{:S(2)}) async-start(bf16[16,2,128,512]{3,2,1,0:T(8,128)(2,1)} %select_select_fusion), calls=%async_computation.2 | async-start | bytes 8388608 | tf_op jit(solution)/shard_map/all_to_all | solution.py:142
  83.6 31.5 %all-to-all-done.2 = bf16[16,2,128,512]{3,2,1,0:T(8,128)(2,1)} async-done(((bf16[16,2,128,512]{3,2,1,0:T(8,128)(2,1)}), bf16[16,2,128,512]{3,2,1,0:T(8,128)(2,1)}, u32[]{:S(2)}, u32[]{:S(2)}) %all-to-all-start.2) | async-done | bytes 4194336 | tf_op jit(solution)/shard_map/all_to_all | solution.py:142
  115.0 3.9 %gather_fusion.7 = bf16[4,2,128,512]{3,2,1,0:T(8,128)(2,1)} fusion(bf16[16,2,128,512]{3,2,1,0:T(8,128)(2,1)} %all-to-all-done.2, s32[1024]{0:T(1024)} %pad_clamp_fusion.1), kind=kCustom, calls=%fused_computation.7 | custom fusion | bytes 2097168 | tf_op jit(solution)/shard_map/jit(_take)/gather | solution.py:192
  124.9 7.1 %all-to-all-start.6 = ((bf16[16,1,64]{2,1,0:T(2,128)(2,1)}), bf16[16,1,64]{2,1,0:T(2,128)(2,1)S(1)}, u32[]{:S(2)}, u32[]{:S(2)}) async-start(bf16[16,1,64]{2,1,0:T(2,128)(2,1)} %copy.66), calls=%async_computation.6 | async-start | bytes 16384 | tf_op jit(solution)/shard_map/all_to_all | solution.py:177
  144.3 7.2 %all-to-all-start.5 = ((bf16[16,2,256]{2,1,0:T(2,128)(2,1)}), bf16[16,2,256]{2,1,0:T(2,128)(2,1)S(1)}, u32[]{:S(2)}, u32[]{:S(2)}) async-start(bf16[16,2,256]{2,1,0:T(2,128)(2,1)} %reshape.661), calls=%async_computation.5 | async-start | bytes 32768 | tf_op jit(solution)/shard_map/all_to_all | solution.py:170
  153.0 6.1 %all-to-all-done.5 = bf16[16,2,256]{2,1,0:T(2,128)(2,1)S(1)} async-done(((bf16[16,2,256]{2,1,0:T(2,128)(2,1)}), bf16[16,2,256]{2,1,0:T(2,128)(2,1)S(1)}, u32[]{:S(2)}, u32[]{:S(2)}) %all-to-all-start.5) | async-done | bytes 16416 | tf_op jit(solution)/shard_map/all_to_all | solution.py:170
  164.1 6.1 %all-to-all-done = bf16[16,2,448]{2,1,0:T(2,128)(2,1)S(1)} async-done(((bf16[16,2,448]{2,1,0:T(2,128)(2,1)}), bf16[16,2,448]{2,1,0:T(2,128)(2,1)S(1)}, u32[]{:S(2)}, u32[]{:S(2)}) %all-to-all-start) | async-done | bytes 28704 | tf_op jit(solution)/shard_map/all_to_all | solution.py:184
  173.7 13.3 %all-gather = f32[64,32]{1,0:T(8,128)S(1)} all-gather(f32[8,32]{1,0:T(8,128)S(1)} %pad_maximum_fusion.2), channel_id=2, replica_groups=mesh['group'=16,'lane'=8] {'lane'}, dimensions={0}, use_global_device_ids=true | all-gather | bytes 9216 | tf_op jit(solution)/shard_map/all_gather | solution.py:14
  187.9 12.8 %all-gather.1 = f32[64,32]{1,0:T(8,128)S(1)} all-gather(f32[8,32]{1,0:T(8,128)S(1)} %pad_maximum_fusion.3), channel_id=3, replica_groups=mesh['group'=16,'lane'=8] {'lane'}, dimensions={0}, use_global_device_ids=true | all-gather | bytes 9216 | tf_op jit(solution)/shard_map/all_gather | solution.py:14
  200.8 4.6 %slice.69 = f32[56,32,512]{2,1,0:T(8,128)} slice(f32[64,32,512]{2,1,0:T(8,128)} %all-gather.5.cloned.1.call-done), slice={[8:64], [0:32], [0:512]} | slice | bytes 7340032 | tf_op jit(solution)/shard_map/slice | solution.py:16
  205.4 8.8 %while.14 = (s32[]{:T(128)}, f32[8,32]{1,0:T(8,128)S(1)}, f32[8,32]{1,0:T(8,128)S(1)}, f32[8,32,512]{2,1,0:T(8,128)S(1)}, f32[7,8,32]{2,1,0:T(8,128)S(1)}, /*ind...) while((s32[]{:T(128)}, f32[8,32]{1,0:T(8,128)S(1)}, f32[8,32]{1,0:T(8,128)S(1)}, ...), condition=%wide.region_13.14_spmd, body=%wide.region_12.13_spmd.sunk | while | flops 394754 | bytes 1583205 | solution.py:17
  214.4 6.1 %fusion.17 = bf16[8,896]{1,0:T(8,128)(2,1)S(1)} fusion(bf16[4096,896]{1,0:T(8,128)(2,1)} %param.31, bf16[32,512,128]{2,1,0:T(8,128)(2,1)} %param.30, bf16[8,32,512]{2,1,0:T(8,128)(2,1)S(1)} %divide_convert_fusion, bf16[4,896]{1,0:T(4,128)(2,1)S(1)} %broadcast_select_fusion.7, bf16[4,896]{1,0:T(4,128)(2,1)S(1)} %copy-done.1, pred[]{:T(512)S(6)} %not.3), kind=kOutput, calls=%fused_computation.47 | convolution fusion | flops 92357632 | bytes 11825153 | tf_op jit(solution)/shard_map/dot_general | solution.py:226
  225.7 6.6 %all-to-all-done.7 = bf16[16,2,896]{2,1,0:T(2,128)(2,1)S(1)} async-done(((bf16[16,2,896]{2,1,0:T(2,128)(2,1)}), bf16[16,2,896]{2,1,0:T(2,128)(2,1)S(1)}, u32[]{:S(2)}, u32[]{:S(2)}) %all-to-all-start.7) | async-done | bytes 57376 | tf_op jit(solution)/shard_map/all_to_all | solution.py:254
  232.5 3.6 %fusion.5 = f32[32,2048]{1,0:T(8,128)} fusion(bf16[32,896]{1,0:T(8,128)(2,1)S(1)} %convert_element_type.113, bf16[1,896,2048]{2,1,0:T(8,128)(2,1)} %param.34), kind=kOutput, calls=%fused_computation.28 | convolution fusion | flops 117440512 | bytes 3989504 | tf_op jit(solution)/shard_map/dot_general | solution.py:261
  239.2 13.6 %psum.22 = f32[32]{0:T(128)S(1)} all-reduce(f32[32]{0:T(128)S(1)} %reduce_sum.118), channel_id=1, replica_groups=mesh['group'=16,'lane'=8] {'lane'}, use_global_device_ids=true, to_apply=%region_21.22 | all-reduce | flops 32 | bytes 256 | tf_op jit(solution)/shard_map/psum | solution.py:262
  252.9 42.9 %all-reduce.3.cloned.1.call-done = (f32[32,2048]{1,0:T(8,128)}, f32[32,2048]{1,0:T(8,128)}) async-done(((f32[32,2048]{1,0:T(8,128)}, f32[32,2048]{1,0:T(8,128)}), (f32[32,2048]{1,0:T(8,128)}, f32[32,2048]{1,0:T(8,128)})) %all-reduce.3.cloned.1.call-update) | async-done | bytes 524304 | tf_op jit(solution)/shard_map/psum | solution.py:262
  299.4 6.9 %all-to-all-start.8 = ((bf16[16,2,896]{2,1,0:T(2,128)(2,1)}), bf16[16,2,896]{2,1,0:T(2,128)(2,1)S(1)}, u32[]{:S(2)}, u32[]{:S(2)}) async-start(bf16[16,2,896]{2,1,0:T(2,128)(2,1)} %reshape.492), calls=%async_computation.8 | async-start | bytes 114688 | tf_op jit(solution)/shard_map/all_to_all | solution.py:269
  307.9 6.1 %all-to-all-done.8 = bf16[16,2,896]{2,1,0:T(2,128)(2,1)S(1)} async-done(((bf16[16,2,896]{2,1,0:T(2,128)(2,1)}), bf16[16,2,896]{2,1,0:T(2,128)(2,1)S(1)}, u32[]{:S(2)}, u32[]{:S(2)}) %all-to-all-start.8) | async-done | bytes 57376 | tf_op jit(solution)/shard_map/all_to_all | solution.py:269
  (232 shorter events, 87.3 us)
Async XLA Ops:
  12.5 15.7 %all-to-all-start.3 = ((bf16[16,2,1024]{2,1,0:T(2,128)(2,1)}), bf16[16,2,1024]{2,1,0:T(2,128)(2,1)S(1)}, u32[]{:S(2)}, u32[]{:S(2)}) async-start(bf16[16,2,1024]{2,1,0:T(2,128)(2,1)} %reshape.659), calls=%async_computation.3 | async-start | bytes 131072 | tf_op jit(solution)/shard_map/all_to_all | solution.py:163
  28.3 18.3 %all-to-all-start.4 = ((bf16[16,2,64,128]{3,2,1,0:T(8,128)(2,1)}), bf16[16,2,64,128]{3,2,1,0:T(8,128)(2,1)}, u32[]{:S(2)}, u32[]{:S(2)}) async-start(bf16[16,2,64,128]{3,2,1,0:T(8,128)(2,1)} %select_select_fusion.2), calls=%async_computation.4 | async-start | bytes 1048576 | tf_op jit(solution)/shard_map/all_to_all | solution.py:149
  46.5 14.4 %all-to-all-start.1 = ((bf16[16,32,512]{2,1,0:T(8,128)(2,1)}), bf16[16,32,512]{2,1,0:T(8,128)(2,1)}, u32[]{:S(2)}, u32[]{:S(2)}) async-start(bf16[16,32,512]{2,1,0:T(8,128)(2,1)} %select_select_fusion.3), calls=%async_computation.1 | async-start | bytes 1048576 | tf_op jit(solution)/shard_map/all_to_all | solution.py:156
  60.9 54.1 %all-to-all-start.2 = ((bf16[16,2,128,512]{3,2,1,0:T(8,128)(2,1)}), bf16[16,2,128,512]{3,2,1,0:T(8,128)(2,1)}, u32[]{:S(2)}, u32[]{:S(2)}) async-start(bf16[16,2,128,512]{3,2,1,0:T(8,128)(2,1)} %select_select_fusion), calls=%async_computation.2 | async-start | bytes 8388608 | tf_op jit(solution)/shard_map/all_to_all | solution.py:142
  65.5 135.3 %all-gather.5.cloned.1.call-start = ((), (), s32[]{:S(2)}) async-start(), calls=%async_computation.9 | async-start | bytes 4718592 | tf_op jit(solution)/shard_map/all_gather | solution.py:14
  78.1 45.3 %copy-start.17 = (pred[4]{0:T(512)(128)(4,1)}, pred[4]{0:T(512)(128)(4,1)S(1)}, u32[]{:S(2)}) copy-start(pred[4]{0:T(512)(128)(4,1)S(1)} %compare_and_fusion.2) | copy-start | bytes 16
  78.2 45.3 %copy-start.8 = (bf16[4,64]{1,0:T(4,128)(2,1)S(1)}, bf16[4,64]{1,0:T(4,128)(2,1)}, u32[]{:S(2)}) copy-start(bf16[4,64]{1,0:T(4,128)(2,1)} %param.28) | copy-start | bytes 1540
  79.2 45.0 %copy-start.14 = (pred[16]{0:T(512)(128)(4,1)S(1)}, pred[16]{0:T(512)(128)(4,1)}, u32[]{:S(2)}) copy-start(pred[16]{0:T(512)(128)(4,1)} %copy-done.13) | copy-start | bytes 52
  79.2 52.8 %copy-start.34 = (pred[4,2]{1,0:T(4,128)(4,1)S(1)}, pred[4,2]{1,0:T(4,128)(4,1)}, u32[]{:S(2)}) copy-start(pred[4,2]{1,0:T(4,128)(4,1)} %copy-done.33) | copy-start | bytes 28
  79.2 52.9 %copy-start.36 = (s32[2]{0:T(128)S(1)}, s32[2]{0:T(128)}, u32[]{:S(2)}) copy-start(s32[2]{0:T(128)} %copy-done.35) | copy-start | bytes 28
  79.2 53.0 %copy-start.20 = (s32[8,4]{0,1:T(4,128)S(1)}, s32[8,4]{0,1:T(4,128)}, u32[]{:S(2)}) copy-start(s32[8,4]{0,1:T(4,128)} %param.36) | copy-start | bytes 388
  79.2 53.8 %copy-start.29 = (s32[4]{0:T(128)S(1)}, s32[4]{0:T(128)}, u32[]{:S(2)}) copy-start(s32[4]{0:T(128)} %copy-done.28) | copy-start | bytes 52
  79.3 53.9 %copy-start.27 = (s32[4]{0:T(128)S(1)}, s32[4]{0:T(128)}, u32[]{:S(2)}) copy-start(s32[4]{0:T(128)} %get-tuple-element.87) | copy-start | bytes 52
  79.3 54.1 %copy-start.2 = (bf16[4,512]{1,0:T(4,128)(2,1)S(1)}, bf16[4,512]{1,0:T(4,128)(2,1)}, u32[]{:S(2)}) copy-start(bf16[4,512]{1,0:T(4,128)(2,1)} %param.27) | copy-start | bytes 12292
  80.1 54.1 %copy-start.1 = (bf16[4,896]{1,0:T(4,128)(2,1)S(1)}, bf16[4,896]{1,0:T(4,128)(2,1)}, u32[]{:S(2)}) copy-start(bf16[4,896]{1,0:T(4,128)(2,1)} %param.29) | copy-start | bytes 21508
  120.7 51.8 %copy-start.10 = (bf16[4,32,64]{2,1,0:T(8,128)(2,1)S(1)}, bf16[4,32,64]{2,1,0:T(8,128)(2,1)}, u32[]{:S(2)}) copy-start(bf16[4,32,64]{2,1,0:T(8,128)(2,1)} %param.26) | copy-start | bytes 49156
  124.9 19.4 %all-to-all-start.6 = ((bf16[16,1,64]{2,1,0:T(2,128)(2,1)}), bf16[16,1,64]{2,1,0:T(2,128)(2,1)S(1)}, u32[]{:S(2)}, u32[]{:S(2)}) async-start(bf16[16,1,64]{2,1,0:T(2,128)(2,1)} %copy.66), calls=%async_computation.6 | async-start | bytes 16384 | tf_op jit(solution)/shard_map/all_to_all | solution.py:177
  136.6 64.1 %copy-start.31 = (pred[8]{0:T(512)(128)(4,1)}, pred[8]{0:T(512)(128)(4,1)S(1)}, u32[]{:S(2)}) copy-start(pred[8]{0:T(512)(128)(4,1)S(1)} %get-tuple-element.79) | copy-start | bytes 28
  144.3 14.8 %all-to-all-start.5 = ((bf16[16,2,256]{2,1,0:T(2,128)(2,1)}), bf16[16,2,256]{2,1,0:T(2,128)(2,1)S(1)}, u32[]{:S(2)}, u32[]{:S(2)}) async-start(bf16[16,2,256]{2,1,0:T(2,128)(2,1)} %reshape.661), calls=%async_computation.5 | async-start | bytes 32768 | tf_op jit(solution)/shard_map/all_to_all | solution.py:170
  159.1 11.1 %all-to-all-start = ((bf16[16,2,448]{2,1,0:T(2,128)(2,1)}), bf16[16,2,448]{2,1,0:T(2,128)(2,1)S(1)}, u32[]{:S(2)}, u32[]{:S(2)}) async-start(bf16[16,2,448]{2,1,0:T(2,128)(2,1)} %reshape.663), calls=%async_computation | async-start | bytes 65536 | tf_op jit(solution)/shard_map/all_to_all | solution.py:184
  221.2 11.1 %all-to-all-start.7 = ((bf16[16,2,896]{2,1,0:T(2,128)(2,1)}), bf16[16,2,896]{2,1,0:T(2,128)(2,1)S(1)}, u32[]{:S(2)}, u32[]{:S(2)}) async-start(bf16[16,2,896]{2,1,0:T(2,128)(2,1)} %reshape.491), calls=%async_computation.7 | async-start | bytes 114688 | tf_op jit(solution)/shard_map/all_to_all | solution.py:254
  224.7 71.0 %all-reduce.3.cloned.1.call-start = ((), (), s32[]{:S(2)}) async-start(), calls=%async_computation.10 | async-start | bytes 1048576 | tf_op jit(solution)/shard_map/psum | solution.py:262
  237.6 68.7 %copy-start.3 = (bf16[8,128,512]{2,1,0:T(8,128)(2,1)S(1)}, bf16[8,128,512]{2,1,0:T(8,128)(2,1)}, u32[]{:S(2)}) copy-start(bf16[8,128,512]{2,1,0:T(8,128)(2,1)} %select_select_fusion.1) | copy-start | bytes 3145732
  299.4 14.6 %all-to-all-start.8 = ((bf16[16,2,896]{2,1,0:T(2,128)(2,1)}), bf16[16,2,896]{2,1,0:T(2,128)(2,1)S(1)}, u32[]{:S(2)}, u32[]{:S(2)}) async-start(bf16[16,2,896]{2,1,0:T(2,128)(2,1)} %reshape.492), calls=%async_computation.8 | async-start | bytes 114688 | tf_op jit(solution)/shard_map/all_to_all | solution.py:269
  (25 other events, 419.3 us)
Sparse Core Ops, SparseCore 0:
  123.6 33.7 all-gather.4
  237.8 57.9 all-reduce.2
where the time goes:
time: 324 us; the launch traced here: 322 us
  waiting for transfers between devices  111 us (34%)
  starting transfers between devices  52.6 us (16%)
  other arithmetic  41 us (13%)
  local copies, waits for them, and re-layouts  40.4 us (12%)
  blocking collectives  39.8 us (12%)
  matrix products  21.5 us (7%)
  between operations  15.5 us (5%)
    psum x1, waiting for transfers between devices, per_device(): lax.psum((gate_part, up_part, squares), 'lane')  42.9 us
    all_to_all x1, waiting for transfers between devices, per_device(): lax.all_to_all(outbound(own_latent, outbound_index, outbound_present), 'g...  31.5 us
    all_gather x2, blocking collectives, merged_2(): pieces = jax.tree.map(lambda part: lax.all_gather(part, axis), value)  26.2 us
    psum x1, blocking collectives, per_device(): lax.psum((gate_part, up_part, squares), 'lane')  13.6 us
    gather x7, local copies, waits for them, and re-layouts, per_device(): incoming = [jnp.take(values, source_of, axis=0) for values in arrived]  10.2 us
    select_n x9, other arithmetic, outbound(): return jnp.where(present.reshape(shape), picked, jnp.zeros_like(picked))  9.86 us
    gather x7, local copies, waits for them, and re-layouts, outbound(): picked = jnp.take(values, index, axis=0)  9.29 us
    add x7, other arithmetic, combine_parts(): first[2] * first_weight[..., None] + second[2] * second_weight[..., None]  8.5 us
  transfers between devices with their start and end apart: 11, of which 8 were waited for; matrix products, arithmetic and copies ran while one was open for 18% of the time, Pallas kernels for 0%

commit v1 on v0

v1 whole, which is shorter than its diff:
```python
import functools

import jax
import jax.numpy as jnp
from jax import lax
from jax.experimental import pallas as pl
from jax.experimental.pallas import tpu as pltpu
from jax.sharding import PartitionSpec as P

F32 = jnp.float32
BF16 = jnp.bfloat16
I32 = jnp.int32

D = 7168
EPSILON = 1e-06
MASKED = -1e30

GROUPS = 16
LANES = 8
SEQ_G = 4
SEQS = 64
NEW_G = 8
SLOTS = 128
HEADS = 32
HEAD_V = 128
LAT = 512
ROPE = 64
PAGE = 128
PSL = 2
TOP = 4
CAP = 2
FF = 2048
WIDTH = 896
ROWS = 16
CHUNKS = 8
PIECE_ROWS = SEQ_G * 16 + 16
HALF = FF // 2
SCALE = (HEAD_V + ROPE) ** -0.5

VM = pl.BlockSpec(memory_space=pltpu.VMEM)
SM = pl.BlockSpec(memory_space=pltpu.SMEM)
ANY = pl.BlockSpec(memory_space=pl.ANY)
MIB = 1024 * 1024


def shape(dims, dtype):
    return jax.ShapeDtypeStruct(dims, dtype)


def iota(dims, dim):
    return lax.broadcasted_iota(I32, dims, dim)


def call(kernel, outs, in_specs, out_specs, scratch, vmem, name, flops=0, moved=0):
    return pl.pallas_call(
        kernel,
        out_shape=outs,
        in_specs=in_specs,
        out_specs=out_specs,
        scratch_shapes=scratch,
        compiler_params=pltpu.CompilerParams(vmem_limit_bytes=vmem * MIB),
        cost_estimate=pl.CostEstimate(flops=flops, bytes_accessed=moved, transcendentals=0),
        name=name,
    )


def split_terms(value, count):
    terms = []
    for _ in range(count):
        term = value.astype(BF16).astype(F32)
        terms.append(term)
        value = value - term
    return terms


def pack_rows(summed, highest, normalizer):
    lane = iota(summed.shape, 1)
    meta = jnp.zeros_like(summed)
    for i, term in enumerate(split_terms(highest, 3) + split_terms(normalizer, 2)):
        meta = jnp.where(lane == i, term, meta)
    return jnp.concatenate([summed, meta], axis=1).astype(BF16)


def unpack_rows(packed):
    wide = packed.astype(F32)
    highest = wide[:, 128:129] + wide[:, 129:130] + wide[:, 130:131]
    normalizer = wide[:, 131:132] + wide[:, 132:133]
    return wide[:, :128], highest, normalizer


def join_rows(parts):
    highest = functools.reduce(jnp.maximum, [m for _, m, _ in parts])
    weights = [jnp.exp(m - highest) for _, m, _ in parts]
    summed = sum(u * w for (u, _, _), w in zip(parts, weights))
    normalizer = sum(z * w for (_, _, z), w in zip(parts, weights))
    return summed, highest, normalizer


def attend_kernel(
    table, lengths, q_latent, q_rope, fresh_latent, fresh_rope, latent, rope, w_uv, packed, wide, narrow
):
    group, lane = lax.axis_index("group"), lax.axis_index("lane")
    tops, norms = [], []
    for s in range(SEQ_G):
        length = lengths[group * SEQ_G + s]
        query, turned = q_latent[s], q_rope[s]
        pages, shown, scores = [], [], []
        for p in range(PSL):
            page = table[s, p]
            tokens = latent[page]
            score = lax.dot_general(query, tokens, (((1,), (1,)), ((), ())), preferred_element_type=F32)
            score = score + jnp.dot(turned, rope[page], preferred_element_type=F32)
            visible = (p * LANES + lane) < length
            pages.append(tokens)
            shown.append(visible)
            scores.append(jnp.where(visible, score * SCALE, MASKED))
        own_row = fresh_latent[s : s + 1, :].astype(F32)
        own = jnp.sum(query.astype(F32) * own_row, axis=1, keepdims=True)
        own = own + jnp.sum(turned.astype(F32) * fresh_rope[s : s + 1, :].astype(F32), axis=1, keepdims=True)
        own = jnp.where(lane == 0, own * SCALE, MASKED)
        top = jnp.maximum(jnp.max(jnp.maximum(scores[0], scores[1]), axis=1, keepdims=True), own)
        weights = [jnp.where(v, jnp.exp(x - top), 0.0) for v, x in zip(shown, scores)]
        own_weight = jnp.where(lane == 0, jnp.exp(own - top), 0.0)
        norms.append(jnp.sum(weights[0] + weights[1], axis=1, keepdims=True) + own_weight)
        tops.append(top)
        summed = own_weight * own_row
        for weight, tokens in zip(weights, pages):
            summed = summed + jnp.dot(weight.astype(BF16), tokens, preferred_element_type=F32)
        for c in range(LAT // 128):
            wide[c, s * HEADS : (s + 1) * HEADS, :] = summed[:, c * 128 : (c + 1) * 128]
    for h in range(HEADS):
        rows = pl.ds(h, SEQ_G, stride=HEADS)
        row = jnp.concatenate([wide[c, rows, :] for c in range(LAT // 128)], axis=1).astype(BF16)
        narrow[rows, :] = jnp.dot(row, w_uv[h], preferred_element_type=F32)
    packed[...] = pack_rows(narrow[...], jnp.concatenate(tops, axis=0), jnp.concatenate(norms, axis=0))


def attend(table, lengths, q_latent, q_rope, fresh_latent, fresh_rope, latent, rope, w_uv):
    return call(
        attend_kernel,
        shape((SEQ_G * HEADS, 256), BF16),
        [SM, SM] + [VM] * 7,
        VM,
        [pltpu.VMEM((LAT // 128, SEQ_G * HEADS, 128), F32), pltpu.VMEM((SEQ_G * HEADS, 128), F32)],
        12,
        "attend",
    )(table, lengths, q_latent, q_rope, fresh_latent, fresh_rope, latent, rope, w_uv)


def join_kernel(first, second, packed):
    packed[...] = pack_rows(*join_rows([unpack_rows(first[...]), unpack_rows(second[...])]))


def join_pair(first, second):
    return call(join_kernel, shape(first.shape, BF16), [VM, VM], VM, [], 4, "join_pair")(first, second)


def hidden_kernel(a, b, c, d, residual, w_out, copies, heads):
    summed, _, normalizer = join_rows([unpack_rows(x[...]) for x in (a, b, c, d)])
    heads[...] = summed / normalizer
    flat = jnp.concatenate(
        [heads[pl.ds(h, SEQ_G, stride=HEADS), :] for h in range(HEADS)], axis=1
    ).astype(BF16)
    hidden = residual[...].astype(F32) + jnp.dot(flat, w_out[...], preferred_element_type=F32)
    hidden = hidden.astype(BF16)
    for g in range(GROUPS):
        copies[g] = hidden


def hidden_rows(parts, residual, w_out):
    return call(
        hidden_kernel,
        shape((GROUPS, SEQ_G, WIDTH), BF16),
        [VM] * 6,
        VM,
        [pltpu.VMEM((SEQ_G * HEADS, HEAD_V), F32)],
        12,
        "hidden",
    )(*parts, residual, w_out)


def spread_kernel(table, routes, latent, rope, out, tail, sems):
    copies = []
    for s in range(SEQ_G):
        for p in range(PSL):
            copies.append(
                pltpu.make_async_copy(
                    latent.at[table[s, p]],
                    out.at[pl.ds(p * CHUNKS, CHUNKS), pl.ds(s * 16, 16), :],
                    sems.at[s * PSL + p],
                )
            )
            copies[-1].start()
    lane = iota((NEW_G, LAT), 1)
    named = jnp.zeros((NEW_G, LAT), F32)
    for j in range(TOP):
        named = jnp.where(lane == j, routes[:, j : j + 1].astype(F32), named)
    named = jnp.broadcast_to(named[None], (CHUNKS, NEW_G, LAT))
    for p in range(PSL):
        turned = [rope[table[s, p]].astype(F32).reshape(CHUNKS, 8, PAGE) for s in range(SEQ_G)]
        turned = jnp.concatenate(turned, axis=2)
        tail[p * CHUNKS : (p + 1) * CHUNKS] = jnp.concatenate([turned, named], axis=1).astype(BF16)
    copies.append(pltpu.make_async_copy(tail, out.at[:, pl.ds(SEQ_G * 16, 16), :], sems.at[SEQ_G * PSL]))
    copies[-1].start()
    for copy in copies:
        copy.wait()


def spread(table, routes, latent, rope):
    return call(
        spread_kernel,
        shape((GROUPS, PIECE_ROWS, LAT), BF16),
        [SM, VM, ANY, VM],
        ANY,
        [pltpu.VMEM((GROUPS, 16, LAT), BF16), pltpu.SemaphoreType.DMA((SEQ_G * PSL + 1,))],
        6,
        "spread",
    )(table, routes, latent, rope)


def to_column(row):
    size = row.shape[1]
    eye = iota((size, size), 0) == iota((size, size), 1)
    return jnp.sum(jnp.where(eye, row, 0.0), axis=1, keepdims=True)


def slots_of(destiny_row):
    seq = iota((1, SEQS), 1)
    home = (seq // SEQ_G).astype(F32)
    leaves = jnp.where(destiny_row == home, 0.0, 1.0)
    target_col, leaves_col = to_column(destiny_row), to_column(leaves)
    earlier = iota((SEQS, SEQS), 0) < iota((SEQS, SEQS), 1)
    rank = jnp.sum(
        jnp.where(earlier & (target_col == destiny_row) & (leaves_col > 0.5), 1.0, 0.0), axis=0, keepdims=True
    )
    own_slot = home * NEW_G + (seq % SEQ_G).astype(F32)
    slot = jnp.where(leaves > 0.5, destiny_row * NEW_G + SEQ_G + rank, own_slot)
    return slot, leaves


def route_kernel(destiny, destiny_row, pieces, out, choose, source, count):
    expert = lax.axis_index("group")
    for i in range(GROUPS):
        count[i] = 0
    for i in range(SEQS):
        source[i] = 0
    for q in range(SEQS):
        g, s = q // SEQ_G, q % SEQ_G
        keeper = destiny[q]

        @pl.when(keeper != g)
        def _():
            rank = count[keeper]
            count[keeper] = rank + 1
            source[keeper * SEQ_G + rank] = q
            rows = pl.ds(pl.multiple_of(rank * 16, 16), 16)
            out[keeper, rows, :] = pieces[g, s * 16 : (s + 1) * 16, :]
            cols = pl.ds(pl.multiple_of(rank * 128, 128), 128)
            out[keeper, SEQ_G * 16 :, cols] = pieces[g, SEQ_G * 16 :, s * 128 : (s + 1) * 128]

    slot, leaves = slots_of(destiny_row[...].astype(F32))
    new_group = jnp.floor(slot * (1.0 / NEW_G))
    named = pieces[:, SEQ_G * 16 :, 0:128].astype(F32)[:, 8:, :].reshape(SLOTS, 128)
    lane = iota((SLOTS, 128), 1)
    hit = jnp.where((lane < TOP) & (named == expert.astype(F32)), 1.0, 0.0)
    hit = jnp.sum(hit, axis=1, keepdims=True)
    slot_col = iota((SLOTS, SEQS), 0)
    slot_group = (slot_col // NEW_G).astype(F32)
    slot_col = slot_col.astype(F32)
    mine = jnp.sum(jnp.where(slot_col == slot, hit, 0.0), axis=0, keepdims=True)
    before = jnp.sum(jnp.where((slot_group == new_group) & (slot_col < slot), hit, 0.0), axis=0, keepdims=True)
    stays_col = 1.0 - to_column(leaves)
    other = iota((SEQS, SEQS), 0)
    first = (other % SEQ_G) == 0
    keeper_rank = jnp.sum(
        jnp.where(first & ((other // SEQ_G).astype(F32) < new_group), stays_col, 0.0), axis=0, keepdims=True
    )
    row = iota((ROWS, SEQS), 0).astype(F32)
    choose[...] = jnp.where((row == keeper_rank * CAP + before) & (mine > 0.5), 1.0, 0.0).astype(BF16)


def route(destiny, destiny_row, pieces):
    return call(
        route_kernel,
        (shape((GROUPS, PIECE_ROWS, LAT), BF16), shape((ROWS, SEQS), BF16), shape((SEQS,), I32)),
        [SM, VM, VM],
        (VM, VM, SM),
        [pltpu.SMEM((GROUPS,), I32)],
        8,
        "route",
    )(destiny, destiny_row, pieces)


def keep_kernel(destiny, lengths, table, source, latent, rope, pieces, tails, kept, kept_rope, zeros, sems):
    group, lane = lax.axis_index("group"), lax.axis_index("lane")
    stays = destiny[group * SEQ_G] == group
    zeros[...] = jnp.zeros_like(zeros)
    waits = []
    for i in range(NEW_G * PSL):
        s, p = i // PSL, i % PSL
        if s < SEQ_G:
            seq = group * SEQ_G + s
            taken = latent.at[table[s, p]]
        else:
            seq = source[group * SEQ_G + s - SEQ_G]
            taken = pieces.at[pl.ds(p * CHUNKS, CHUNKS), pl.ds((s - SEQ_G) * 16, 16), :]
        visible = stays & ((p * LANES + lane) < lengths[seq])
        copy = pltpu.make_async_copy(taken, kept.at[i], sems.at[i])
        blank = pltpu.make_async_copy(zeros, kept.at[i], sems.at[i])
        pl.when(visible)(copy.start)
        pl.when(jnp.logical_not(visible))(blank.start)
        waits.append(blank)
        if s < SEQ_G:
            page = rope[table[s, p]].astype(F32)
        else:
            c = s - SEQ_G
            page = tails[p * CHUNKS : (p + 1) * CHUNKS, SEQ_G * 16 :, c * 128 : (c + 1) * 128].astype(F32)
            page = page[:, :8, :].reshape(ROPE, PAGE)
        kept_rope[i] = jnp.where(visible, page, 0.0).astype(BF16)
    for wait in waits:
        wait.wait()


def keep(destiny, lengths, table, source, latent, rope, pieces):
    return call(
        keep_kernel,
        (shape((NEW_G * PSL, CHUNKS, 16, LAT), BF16), shape((NEW_G * PSL, ROPE, PAGE), BF16)),
        [SM, SM, SM, SM, ANY, VM, ANY, VM],
        (ANY, VM),
        [pltpu.VMEM((CHUNKS, 16, LAT), BF16), pltpu.SemaphoreType.DMA((NEW_G * PSL,))],
        6,
        "keep",
    )(destiny, lengths, table, source, latent, rope, pieces, pieces)


def gather_hidden(hidden, rows):
    for g in range(GROUPS):
        rows[g * SEQ_G : (g + 1) * SEQ_G, :] = hidden[g].astype(F32)
    return rows[...].astype(BF16)


def expand_kernel(hidden, choose, gain, w_gate, w_up, keep_half, send_half, rows):
    core = lax.rem(lax.axis_index("lane"), 2)
    mine = pl.ds(pl.multiple_of(core * HALF, HALF), HALF)
    other = pl.ds(pl.multiple_of((1 - core) * HALF, HALF), HALF)
    taken = jnp.dot(choose[...], gather_hidden(hidden, rows), preferred_element_type=F32)
    squares = jnp.sum(taken * taken, axis=1, keepdims=True)
    scaled = (taken * gain[...].astype(F32)).astype(BF16)
    for i, weights in enumerate((w_gate, w_up)):
        cols = slice(i * HALF, (i + 1) * HALF)
        send_half[:, cols] = jnp.dot(scaled, weights[0, :, other], preferred_element_type=F32).astype(BF16)
        keep_half[:, cols] = jnp.dot(scaled, weights[0, :, mine], preferred_element_type=F32)
    lane = iota((ROWS, 128), 1)
    keep_half[:, FF:] = jnp.where(lane == 0, squares, 0.0)
    high, low = split_terms(squares, 2)
    send_half[:, FF:] = jnp.where(lane == 0, high, jnp.where(lane == 1, low, 0.0)).astype(BF16)


def expand(hidden, choose, gain, w_gate, w_up):
    return call(
        expand_kernel,
        (shape((ROWS, FF + 128), F32), shape((ROWS, FF + 128), BF16)),
        [VM] * 5,
        (VM, VM),
        [pltpu.VMEM((SEQS, WIDTH), F32)],
        12,
        "expand",
    )(hidden, choose, gain, w_gate, w_up)


def pair_kernel(kept, arrived, out):
    out[:, :FF] = (kept[:, :FF] + arrived[:, :FF].astype(F32)).astype(BF16)
    squares = kept[:, FF : FF + 1] + arrived[:, FF : FF + 1].astype(F32) + arrived[:, FF + 1 : FF + 2].astype(F32)
    high, low = split_terms(squares, 2)
    lane = iota((ROWS, 128), 1)
    out[:, FF:] = jnp.where(lane == 0, high, jnp.where(lane == 1, low, 0.0)).astype(BF16)


def pair_sum(kept, arrived):
    return call(pair_kernel, shape((ROWS, FF + 128), BF16), [VM, VM], VM, [], 4, "pair_sum")(kept, arrived)


def activate_kernel(a, b, c, d, out):
    total = sum(x[...].astype(F32) for x in (a, b, c, d))
    squares = total[:, FF : FF + 1] + total[:, FF + 1 : FF + 2]
    factor = lax.rsqrt(squares / D + EPSILON)
    gate = total[:, :HALF] * factor
    up = total[:, HALF:FF] * factor
    out[...] = (jax.nn.silu(gate) * up).astype(BF16)


def activate(parts):
    return call(activate_kernel, shape((ROWS, HALF), BF16), [VM] * 4, VM, [], 4, "activate")(*parts)


def down_kernel(mine, other, destiny_row, w_down, out, rows):
    core = lax.rem(lax.axis_index("lane"), 2)
    here = pl.ds(pl.multiple_of(core * HALF, HALF), HALF)
    there = pl.ds(pl.multiple_of((1 - core) * HALF, HALF), HALF)
    made = jnp.dot(mine[...], w_down[0, here, :], preferred_element_type=F32)
    made = made + jnp.dot(other[...], w_down[0, there, :], preferred_element_type=F32)
    made = made.astype(BF16)
    seq = iota((1, SEQS), 1)
    keeper = jnp.where(
        (destiny_row[...] == seq // SEQ_G) & (seq % SEQ_G == 0), 1.0, 0.0
    )
    at, home = iota((GROUPS * CAP, SEQS), 0) // CAP, iota((GROUPS * CAP, SEQS), 1) // SEQ_G
    rank = jnp.sum(jnp.where(home < at, keeper, 0.0), axis=1, keepdims=True)
    present = jnp.sum(jnp.where(home == at, keeper, 0.0), axis=1, keepdims=True)
    place = iota((GROUPS * CAP, ROWS), 0)
    wanted = rank * CAP + (place % CAP).astype(F32)
    matrix = jnp.where(iota((GROUPS * CAP, ROWS), 1).astype(F32) == wanted, present, 0.0).astype(BF16)
    rows[...] = jnp.dot(matrix, made, preferred_element_type=F32)
    for g in range(GROUPS):
        out[g] = rows[g * CAP : (g + 1) * CAP, :].astype(BF16)


def down(mine, other, destiny_row, w_down):
    return call(
        down_kernel,
        shape((GROUPS, CAP, WIDTH), BF16),
        [VM] * 4,
        VM,
        [pltpu.VMEM((GROUPS * CAP, WIDTH), F32)],
        8,
        "down",
    )(mine, other, destiny_row, w_down)


def own_kernel(hidden, destiny_row, routes, gates, own, combine, rows):
    group = lax.axis_index("group")
    slot, _ = slots_of(destiny_row[...].astype(F32))
    place = (iota((NEW_G, SEQS), 0) + group * NEW_G).astype(F32)
    matrix = jnp.where(place == slot, 1.0, 0.0).astype(BF16)
    own[...] = jnp.dot(matrix, gather_hidden(hidden, rows), preferred_element_type=F32)
    expert = iota((NEW_G, GROUPS * CAP), 1) // CAP
    hits = jnp.zeros((NEW_G, GROUPS * CAP), F32)
    weight = jnp.zeros((NEW_G, GROUPS * CAP), F32)
    for j in range(TOP):
        same = routes[:, j : j + 1] == expert
        hits = jnp.where(same, 1.0, hits)
        weight = jnp.where(same, gates[:, j : j + 1], weight)
    later = (iota((NEW_G, NEW_G), 1) < iota((NEW_G, NEW_G), 0)).astype(F32)
    before = jnp.dot(later, hits, preferred_element_type=F32)
    want = (iota((NEW_G, GROUPS * CAP), 1) % CAP).astype(F32)
    combine[...] = jnp.where(before == want, weight, 0.0)


def own_rows(hidden, destiny_row, routes, gates):
    return call(
        own_kernel,
        (shape((NEW_G, WIDTH), F32), shape((NEW_G, GROUPS * CAP), F32)),
        [VM] * 4,
        (VM, VM),
        [pltpu.VMEM((SEQS, WIDTH), F32)],
        4,
        "own_rows",
    )(hidden, destiny_row, routes, gates)


def finish_kernel(returned, own, combine, out, rows):
    for g in range(GROUPS):
        rows[g * CAP : (g + 1) * CAP, :] = returned[g].astype(F32)
    back = rows[...].astype(BF16)
    mixed = own[...]
    for term in split_terms(combine[...], 3):
        mixed = mixed + jnp.dot(term.astype(BF16), back, preferred_element_type=F32)
    out[...] = mixed.astype(BF16)


def finish(returned, own, combine):
    return call(
        finish_kernel,
        shape((NEW_G, WIDTH), BF16),
        [VM] * 3,
        VM,
        [pltpu.VMEM((GROUPS * CAP, WIDTH), F32)],
        4,
        "finish",
    )(returned, own, combine)


def swap_core(value):
    return lax.ppermute(value, "lane", [(i, i ^ 1) for i in range(LANES)])


def around(value):
    return [value] + [
        lax.ppermute(value, "lane", [(i, (i + 2 * step) % LANES) for i in range(LANES)]) for step in (1, 3, 2)
    ]


def exchange(value):
    return lax.all_to_all(value, "group", split_axis=0, concat_axis=0, tiled=True)


def in_vmem(value):
    return pltpu.with_memory_space_constraint(value, pltpu.VMEM)


def per_device(
    kv_latent,
    kv_rope,
    page_table,
    seq_pages,
    destiny,
    q_latent,
    q_rope,
    new_latent,
    new_rope,
    residual_in,
    w_uv,
    w_out,
    norm_gain,
    w_gate,
    w_up,
    w_down,
    routes,
    route_gates,
):
    cut_latent = kv_latent.reshape(-1, CHUNKS, 16, LAT)
    destiny_row = destiny.reshape(1, SEQS)
    gain = norm_gain.reshape(1, WIDTH)

    scattered = exchange(spread(page_table, routes, cut_latent, kv_rope))

    packed = attend(page_table, seq_pages, q_latent, q_rope, new_latent, new_rope, kv_latent, kv_rope, in_vmem(w_uv))
    packed = join_pair(packed, swap_core(packed))
    copies = hidden_rows(around(packed), residual_in, in_vmem(w_out))
    hidden = exchange(copies)

    forwarded, choose, source = route(destiny, destiny_row, scattered)
    gathered = exchange(forwarded)

    keep_half, send_half = expand(hidden, choose, gain, in_vmem(w_gate), in_vmem(w_up))
    total = pair_sum(keep_half, swap_core(send_half))
    active = activate(around(total))
    made = down(active, swap_core(active), destiny_row, in_vmem(w_down))
    returned = exchange(made)

    own, combine = own_rows(hidden, destiny_row, routes, route_gates)
    layer_out = finish(returned, own, combine)
    kept_latent, kept_rope = keep(destiny, seq_pages, page_table, source, cut_latent, kv_rope, gathered)
    return layer_out, kept_latent.reshape(-1, PAGE, LAT), kept_rope


def solution(mesh):
    in_specs = (
        P(("group", "lane"), None, None),
        P(("group", "lane"), None, None),
        P(("group", "lane"), None),
        P(),
        P(),
        P("group", None, None),
        P("group", None, None),
        P("group", None),
        P("group", None),
        P("group", "lane"),
        P(),
        P(None, "lane"),
        P("lane"),
        P("group", "lane", None),
        P("group", "lane", None),
        P("group", None, "lane"),
        P("group", None),
        P("group", None),
    )
    out_specs = (
        P("group", "lane"),
        P(("group", "lane"), None, None),
        P(("group", "lane"), None, None),
    )
    return jax.shard_map(per_device, mesh=mesh, in_specs=in_specs, out_specs=out_specs, check_vma=False)
```

time: 324 us -> 106 us (0.33)
  waiting for transfers between devices: 111 us -> 37 us
  other arithmetic: 41 us -> 0 us
  blocking collectives: 39.8 us -> 11 us
  starting transfers between devices: 52.6 us -> 27 us
  local copies, waits for them, and re-layouts: 40.4 us -> 15.2 us
  matrix products: 21.5 us -> 0 us
  between operations: 15.5 us -> 0.88 us
  Pallas kernels: 0 us -> 13.9 us
    all_to_all x9 -> x3, waiting for transfers between devices: 67.8 us -> 23.4 us  [exchange(): lax.all_to_all(value, 'group', split_axis=0, concat_axis=0, tiled=True)]
    psum x1 -> x0, waiting for transfers between devices: 42.9 us -> none  [per_device(): lax.psum((gate_part, up_part, squares), 'lane')]
    all_to_all x9 -> x3, starting transfers between devices: 52.3 us -> 19 us  [exchange(): lax.all_to_all(value, 'group', split_axis=0, concat_axis=0, tiled=True)]
    all_gather x2 -> x0, blocking collectives: 26.2 us -> none  [merged_2(): pieces = jax.tree.map(lambda part: lax.all_gather(part, axis), value)]
    gather x17 -> x0, local copies, waits for them, and re-layouts: 22.3 us -> none  [the longest x7 10.2 us: per_device(): incoming = [jnp.take(values, source_of, axis=0) for values in arrived]]
    dot_general x14 -> x0, matrix products: 21.5 us -> none  [the longest x1 6.06 us: per_device(): jnp.dot(heads_flat, w_out, preferred_element_type=jnp.float32)]
    select_n x26 -> x0, other arithmetic: 19.8 us -> none  [the longest x9 9.86 us: outbound(): return jnp.where(present.reshape(shape), picked, jnp.zeros_like(picked))]
    pallas_call x0 -> x12, Pallas kernels: none -> 13.9 us  [the longest x1 2.74 us: keep(): call(keep_kernel, (shape((NEW_G * PSL, CHUNKS, 16, LAT), BF16), shape((NE...]
  transfers between devices with their start and end apart: 11 -> 12, of which waited for: 8 -> 10; matrix products, arithmetic and copies ran while one was open for 18% -> 0% of each run, Pallas kernels for 0% -> 8%
where the time goes in v1:
time: 106 us; the launch traced here: 105 us
  waiting for transfers between devices  37 us (35%)
  starting transfers between devices  27 us (25%)
  local copies, waits for them, and re-layouts  15.2 us (14%)
  Pallas kernels  13.9 us (13%)
  blocking collectives  11 us (10%)
    all_to_all x3, waiting for transfers between devices, exchange(): lax.all_to_all(value, 'group', split_axis=0, concat_axis=0, tiled=True)  23.4 us
    all_to_all x3, starting transfers between devices, exchange(): lax.all_to_all(value, 'group', split_axis=0, concat_axis=0, tiled=True)  19 us
    unnamed x43, local copies, waits for them, and re-layouts  15.2 us
    all_to_all x1, blocking collectives, exchange(): lax.all_to_all(value, 'group', split_axis=0, concat_axis=0, tiled=True)  11 us
    ppermute x6, waiting for transfers between devices, around(): lax.ppermute(value, 'lane', [(i, (i + 2 * step) % LANES) for i in range(L...  9.9 us
    ppermute x6, starting transfers between devices, around(): lax.ppermute(value, 'lane', [(i, (i + 2 * step) % LANES) for i in range(L...  7.86 us
    ppermute x3, waiting for transfers between devices, swap_core(): return lax.ppermute(value, 'lane', [(i, i ^ 1) for i in range(LANES)])  3.7 us
    pallas_call x1, Pallas kernels, keep(): call(keep_kernel, (shape((NEW_G * PSL, CHUNKS, 16, LAT), BF16), shape((NE...  2.74 us
  transfers between devices with their start and end apart: 12, of which 10 were waited for; matrix products, arithmetic and copies ran while one was open for 0% of the time, Pallas kernels for 8%

profile of v1, /device:TPU:0, one launch (start us, length us, event | category | flops | bytes accessed | tf_op | source)
XLA Modules:
  0.0 105.1 jit_solution(8019948616890666985)
XLA Ops:
  2.2 1.2 %copy-done = bf16[8,128,512]{2,1,0:T(8,128)(2,1)S(1)} copy-done((bf16[8,128,512]{2,1,0:T(8,128)(2,1)S(1)}, bf16[8,128,512]{2,1,0:T(8,128)(2,1)}, u32[]{:S(2)}) %copy-start) | copy-done | bytes 1048600
  6.4 8.1 %all-to-all-start.1 = ((bf16[16,80,512]{2,1,0:T(8,128)(2,1)}), bf16[16,80,512]{2,1,0:T(8,128)(2,1)S(1)}, u32[]{:S(2)}, u32[]{:S(2)}) async-start(bf16[16,80,512]{2,1,0:T(8,128)(2,1)} %copy-done.3), calls=%async_computation.1 | async-start | bytes 2621440 | tf_op jit(solution)/shard_map/all_to_all | solution.py:494
  14.6 2.2 %copy-done.4 = bf16[32,512,128]{2,1,0:T(8,128)(2,1)S(1)} copy-done((bf16[32,512,128]{2,1,0:T(8,128)(2,1)S(1)}, bf16[32,512,128]{2,1,0:T(8,128)(2,1)}, u32[]{:S(2)}) %copy-start.4) | copy-done | bytes 4194328
  16.7 2.6 %attend.1.first = bf16[128,256]{1,0:T(8,128)(2,1)S(1)} custom-call(s32[4,2]{1,0:T(4,128)S(1)} %copy.21.table, s32[64]{0:T(128)S(1)} %copy-done.16, bf16[4,32,512]{2,1,0:T(8,128)(2,1)S(1)} %copy-done.11, bf16[4,32,64]{2,1,0:T(8,128)(2,1)S(1)} %copy-done.12, bf16[4,512]{1,0:T(4,128)(2,1)S(1)} %copy-done.15, bf16[4,64]{1,0:T(4,128)(2,1)S(1)} %copy-done.17, ...), custom_call_target="tpu_custom_call" | custom-call | tf_op jit(solution)/shard_map/attend/pallas_call | solution.py:139
  19.5 1.2 %collective-permute-done.second = bf16[128,256]{1,0:T(8,128)(2,1)S(1)} collective-permute-done((bf16[128,256]{1,0:T(8,128)(2,1)S(1)}, bf16[128,256]{1,0:T(8,128)(2,1)S(1)}, u32[]{:S(2)}, u32[]{:S(2)}) %collective-permute-start) | collective-permute-done | bytes 65568 | tf_op jit(solution)/shard_map/ppermute | solution.py:484
  21.0 3.3 %collective-permute-start.3 = (bf16[128,256]{1,0:T(8,128)(2,1)S(1)}, bf16[128,256]{1,0:T(8,128)(2,1)S(1)}, u32[]{:S(2)}, u32[]{:S(2)}) collective-permute-start(bf16[128,256]{1,0:T(8,128)(2,1)S(1)} %join_pair.1.a), channel_id=1, source_target_pairs={{0,4},{1,5},{2,6},{3,7},{4,0},{5,1},{6,2},{7,3},{8,12},{9,13},{10,... | collective-permute-start | bytes 196616 | tf_op jit(solution)/shard_map/ppermute | solution.py:489
  26.9 1.7 %collective-permute-done.2.c = bf16[128,256]{1,0:T(8,128)(2,1)S(1)} collective-permute-done((bf16[128,256]{1,0:T(8,128)(2,1)S(1)}, bf16[128,256]{1,0:T(8,128)(2,1)S(1)}, u32[]{:S(2)}, u32[]{:S(2)}) %collective-permute-start.2) | collective-permute-done | bytes 65568 | tf_op jit(solution)/shard_map/ppermute | solution.py:489
  28.6 2.2 %collective-permute-done.1.b = bf16[128,256]{1,0:T(8,128)(2,1)S(1)} collective-permute-done((bf16[128,256]{1,0:T(8,128)(2,1)S(1)}, bf16[128,256]{1,0:T(8,128)(2,1)S(1)}, u32[]{:S(2)}, u32[]{:S(2)}) %collective-permute-start.1) | collective-permute-done | bytes 65568 | tf_op jit(solution)/shard_map/ppermute | solution.py:489
  30.8 3.1 %copy-done.2 = bf16[4096,896]{1,0:T(8,128)(2,1)S(1)} copy-done((bf16[4096,896]{1,0:T(8,128)(2,1)S(1)}, bf16[4096,896]{1,0:T(8,128)(2,1)}, u32[]{:S(2)}) %copy-start.2) | copy-done | bytes 7340056
  33.9 2.1 %hidden.1 = bf16[16,4,896]{2,1,0:T(4,128)(2,1)} custom-call(bf16[128,256]{1,0:T(8,128)(2,1)S(1)} %join_pair.1.a, bf16[128,256]{1,0:T(8,128)(2,1)S(1)} %collective-permute-done.1.b, bf16[128,256]{1,0:T(8,128)(2,1)S(1)} %collective-permute-done.2.c, bf16[128,256]{1,0:T(8,128)(2,1)S(1)} %collective-permute-done.3.d, bf16[4,896]{1,0:T(4,128)(2,1)S(1)} %copy-done.14, ...), custom_call_target="tpu_custom_call" | custom-call | tf_op jit(solution)/shard_map/hidden/pallas_call | solution.py:171
  36.0 7.2 %all-to-all-start = ((bf16[16,4,896]{2,1,0:T(4,128)(2,1)}), bf16[16,4,896]{2,1,0:T(4,128)(2,1)S(1)}, u32[]{:S(2)}, u32[]{:S(2)}) async-start(bf16[16,4,896]{2,1,0:T(4,128)(2,1)} %hidden.1), calls=%async_computation | async-start | bytes 229376 | tf_op jit(solution)/shard_map/all_to_all | solution.py:494
  43.3 1.9 %route.1 = (bf16[16,80,512]{2,1,0:T(8,128)(2,1)S(1)}, bf16[16,64]{1,0:T(8,128)(2,1)S(1)}, s32[64]{0:T(128)S(1)}) custom-call(s32[64]{0:T(128)S(1)} %copy-done.13, s32[1,64]{1,0:T(1,128)S(1)} %bitcast.5, bf16[16,80,512]{2,1,0:T(8,128)(2,1)S(1)} %all-to-all-done.1.pieces), custom_call_target="tpu_custom_call" | custom-call | tf_op jit(solution)/shard_map/route/pallas_call | solution.py:283
  46.2 4.8 %all-to-all-done.hidden = bf16[16,4,896]{2,1,0:T(4,128)(2,1)S(1)} async-done(((bf16[16,4,896]{2,1,0:T(4,128)(2,1)}), bf16[16,4,896]{2,1,0:T(4,128)(2,1)S(1)}, u32[]{:S(2)}, u32[]{:S(2)}) %all-to-all-start) | async-done | bytes 114720 | tf_op jit(solution)/shard_map/all_to_all | solution.py:494
  51.1 2.0 %copy-done.5 = bf16[1,896,2048]{2,1,0:T(8,128)(2,1)S(1)} copy-done((bf16[1,896,2048]{2,1,0:T(8,128)(2,1)S(1)}, bf16[1,896,2048]{2,1,0:T(8,128)(2,1)}, u32[]{:S(2)}) %copy-start.5) | copy-done | bytes 3670040
  53.1 2.0 %copy-done.6 = bf16[1,896,2048]{2,1,0:T(8,128)(2,1)S(1)} copy-done((bf16[1,896,2048]{2,1,0:T(8,128)(2,1)S(1)}, bf16[1,896,2048]{2,1,0:T(8,128)(2,1)}, u32[]{:S(2)}) %copy-start.6) | copy-done | bytes 3670040
  56.3 1.3 %collective-permute-done.4.arrived = bf16[16,2176]{1,0:T(8,128)(2,1)S(1)} collective-permute-done((bf16[16,2176]{1,0:T(8,128)(2,1)S(1)}, bf16[16,2176]{1,0:T(8,128)(2,1)S(1)}, u32[]{:S(2)}, u32[]{:S(2)}) %collective-permute-start.4) | collective-permute-done | bytes 69664 | tf_op jit(solution)/shard_map/ppermute | solution.py:484
  58.3 1.9 %collective-permute-start.6 = (bf16[16,2176]{1,0:T(8,128)(2,1)S(1)}, bf16[16,2176]{1,0:T(8,128)(2,1)S(1)}, u32[]{:S(2)}, u32[]{:S(2)}) collective-permute-start(bf16[16,2176]{1,0:T(8,128)(2,1)S(1)} %pair_sum.1.a), channel_id=1, source_target_pairs={{0,6},{1,7},{2,0},{3,1},{4,2},{5,3},{6,4},{7,5},{8,14},{9,15},{10,... | collective-permute-start | bytes 208904 | tf_op jit(solution)/shard_map/ppermute | solution.py:489
  60.3 3.4 %collective-permute-done.7.d = bf16[16,2176]{1,0:T(8,128)(2,1)S(1)} collective-permute-done((bf16[16,2176]{1,0:T(8,128)(2,1)S(1)}, bf16[16,2176]{1,0:T(8,128)(2,1)S(1)}, u32[]{:S(2)}, u32[]{:S(2)}) %collective-permute-start.7) | collective-permute-done | bytes 69664 | tf_op jit(solution)/shard_map/ppermute | solution.py:489
  63.7 2.0 %collective-permute-done.5.b = bf16[16,2176]{1,0:T(8,128)(2,1)S(1)} collective-permute-done((bf16[16,2176]{1,0:T(8,128)(2,1)S(1)}, bf16[16,2176]{1,0:T(8,128)(2,1)S(1)}, u32[]{:S(2)}, u32[]{:S(2)}) %collective-permute-start.5) | collective-permute-done | bytes 69664 | tf_op jit(solution)/shard_map/ppermute | solution.py:489
  66.0 1.2 %collective-permute-done.8.other = bf16[16,1024]{1,0:T(8,128)(2,1)S(1)} collective-permute-done((bf16[16,1024]{1,0:T(8,128)(2,1)S(1)}, bf16[16,1024]{1,0:T(8,128)(2,1)S(1)}, u32[]{:S(2)}, u32[]{:S(2)}) %collective-permute-start.8) | collective-permute-done | bytes 32800 | tf_op jit(solution)/shard_map/ppermute | solution.py:484
  67.9 11.0 %all_to_all.20.returned = bf16[16,2,896]{2,1,0:T(2,128)(2,1)S(1)} all-to-all(bf16[16,2,896]{2,1,0:T(2,128)(2,1)S(1)} %down.1), channel_id=1, replica_groups=mesh['group'=16,'lane'=8] {'group'}, dimensions={0} | all-to-all | bytes 114688 | tf_op jit(solution)/shard_map/all_to_all | solution.py:494
  78.9 3.7 %all-to-all-start.3 = ((bf16[16,80,512]{2,1,0:T(8,128)(2,1)}), bf16[16,80,512]{2,1,0:T(8,128)(2,1)S(1)}, u32[]{:S(2)}, u32[]{:S(2)}) async-start(bf16[16,80,512]{2,1,0:T(8,128)(2,1)} %copy-done.8), calls=%async_computation.3 | async-start | bytes 2621440 | tf_op jit(solution)/shard_map/all_to_all | solution.py:494
  83.8 18.5 %all-to-all-done.3.pieces.tails = bf16[16,80,512]{2,1,0:T(8,128)(2,1)S(1)} async-done(((bf16[16,80,512]{2,1,0:T(8,128)(2,1)}), bf16[16,80,512]{2,1,0:T(8,128)(2,1)S(1)}, u32[]{:S(2)}, u32[]{:S(2)}) %all-to-all-start.3) | async-done | bytes 1310752 | tf_op jit(solution)/shard_map/all_to_all | solution.py:494
  102.3 2.7 %keep.1 = (bf16[16,8,16,512]{3,2,1,0:T(8,128)(2,1)}, bf16[16,64,128]{2,1,0:T(8,128)(2,1)}) custom-call(s32[64]{0:T(128)S(1)} %copy-done.13, s32[64]{0:T(128)S(1)} %copy-done.16, s32[4,2]{1,0:T(4,128)S(1)} %copy.21.table, s32[64]{0:T(128)S(1)} %get-tuple-element.17.source, bf16[8,8,16,512]{3,2,1,0:T(8,128)(2,1)S(1)} %bitcast.4, ...), custom_call_target="tpu_custom_call" | custom-call | tf_op jit(solution)/shard_map/keep/pallas_call | solution.py:325
  (57 shorter events, 12.7 us)
Async XLA Ops:
  0.6 13.8 %copy-start.16 = (s32[64]{0:T(128)S(1)}, s32[64]{0:T(128)}, u32[]{:S(2)}) copy-start(s32[64]{0:T(128)} %lengths.3) | copy-start | bytes 772
  0.6 13.8 %copy-start.17 = (bf16[4,64]{1,0:T(4,128)(2,1)S(1)}, bf16[4,64]{1,0:T(4,128)(2,1)}, u32[]{:S(2)}) copy-start(bf16[4,64]{1,0:T(4,128)(2,1)} %fresh_rope.1) | copy-start | bytes 1540
  0.7 13.8 %copy-start.15 = (bf16[4,512]{1,0:T(4,128)(2,1)S(1)}, bf16[4,512]{1,0:T(4,128)(2,1)}, u32[]{:S(2)}) copy-start(bf16[4,512]{1,0:T(4,128)(2,1)} %fresh_latent.1) | copy-start | bytes 12292
  4.3 10.2 %copy-start.1 = (bf16[8,128,512]{2,1,0:T(8,128)(2,1)S(1)}, bf16[8,128,512]{2,1,0:T(8,128)(2,1)}, u32[]{:S(2)}) copy-start(bf16[8,128,512]{2,1,0:T(8,128)(2,1)} %latent.1) | copy-start | bytes 3145732
  4.3 10.2 %copy-start.10 = (bf16[8,64,128]{2,1,0:T(8,128)(2,1)S(1)}, bf16[8,64,128]{2,1,0:T(8,128)(2,1)}, u32[]{:S(2)}) copy-start(bf16[8,64,128]{2,1,0:T(8,128)(2,1)} %rope.5) | copy-start | bytes 393220
  4.3 10.2 %copy-start.11 = (bf16[4,32,512]{2,1,0:T(8,128)(2,1)S(1)}, bf16[4,32,512]{2,1,0:T(8,128)(2,1)}, u32[]{:S(2)}) copy-start(bf16[4,32,512]{2,1,0:T(8,128)(2,1)} %q_latent.1) | copy-start | bytes 393220
  4.3 10.2 %copy-start.12 = (bf16[4,32,64]{2,1,0:T(8,128)(2,1)S(1)}, bf16[4,32,64]{2,1,0:T(8,128)(2,1)}, u32[]{:S(2)}) copy-start(bf16[4,32,64]{2,1,0:T(8,128)(2,1)} %q_rope.1) | copy-start | bytes 49156
  6.4 24.5 %copy-start.14 = (bf16[4,896]{1,0:T(4,128)(2,1)S(1)}, bf16[4,896]{1,0:T(4,128)(2,1)}, u32[]{:S(2)}) copy-start(bf16[4,896]{1,0:T(4,128)(2,1)} %residual.1) | copy-start | bytes 21508
  6.4 29.7 %all-to-all-start.1 = ((bf16[16,80,512]{2,1,0:T(8,128)(2,1)}), bf16[16,80,512]{2,1,0:T(8,128)(2,1)S(1)}, u32[]{:S(2)}, u32[]{:S(2)}) async-start(bf16[16,80,512]{2,1,0:T(8,128)(2,1)} %copy-done.3), calls=%async_computation.1 | async-start | bytes 2621440 | tf_op jit(solution)/shard_map/all_to_all | solution.py:494
  19.4 1.3 %collective-permute-start = (bf16[128,256]{1,0:T(8,128)(2,1)S(1)}, bf16[128,256]{1,0:T(8,128)(2,1)S(1)}, u32[]{:S(2)}, u32[]{:S(2)}) collective-permute-start(bf16[128,256]{1,0:T(8,128)(2,1)S(1)} %attend.1.first), channel_id=1, source_target_pairs={{0,1},{1,0},{2,3},{3,2},{4,5},{5,4},{6,7},{7,6},{8,9},{9,8},{10,11... | collective-permute-start | bytes 196616 | tf_op jit(solution)/shard_map/ppermute | solution.py:484
  20.7 22.6 %copy-start.19 = (bf16[896]{0:T(1024)(128)(2,1)S(1)}, bf16[896]{0:T(1024)(128)(2,1)}, u32[]{:S(2)}) copy-start(bf16[896]{0:T(1024)(128)(2,1)} %param.30) | copy-start | bytes 5380
  20.7 22.6 %copy-start.13 = (s32[64]{0:T(128)S(1)}, s32[64]{0:T(128)}, u32[]{:S(2)}) copy-start(s32[64]{0:T(128)} %destiny.3) | copy-start | bytes 772
  21.0 5.8 %collective-permute-start.3 = (bf16[128,256]{1,0:T(8,128)(2,1)S(1)}, bf16[128,256]{1,0:T(8,128)(2,1)S(1)}, u32[]{:S(2)}, u32[]{:S(2)}) collective-permute-start(bf16[128,256]{1,0:T(8,128)(2,1)S(1)} %join_pair.1.a), channel_id=1, source_target_pairs={{0,4},{1,5},{2,6},{3,7},{4,0},{5,1},{6,2},{7,3},{8,12},{9,13},{10,... | collective-permute-start | bytes 196616 | tf_op jit(solution)/shard_map/ppermute | solution.py:489
  24.3 4.3 %collective-permute-start.2 = (bf16[128,256]{1,0:T(8,128)(2,1)S(1)}, bf16[128,256]{1,0:T(8,128)(2,1)S(1)}, u32[]{:S(2)}, u32[]{:S(2)}) collective-permute-start(bf16[128,256]{1,0:T(8,128)(2,1)S(1)} %join_pair.1.a), channel_id=1, source_target_pairs={{0,6},{1,7},{2,0},{3,1},{4,2},{5,3},{6,4},{7,5},{8,14},{9,15},{10,... | collective-permute-start | bytes 196616 | tf_op jit(solution)/shard_map/ppermute | solution.py:489
  25.4 5.5 %collective-permute-start.1 = (bf16[128,256]{1,0:T(8,128)(2,1)S(1)}, bf16[128,256]{1,0:T(8,128)(2,1)S(1)}, u32[]{:S(2)}, u32[]{:S(2)}) collective-permute-start(bf16[128,256]{1,0:T(8,128)(2,1)S(1)} %join_pair.1.a), channel_id=1, source_target_pairs={{0,2},{1,3},{2,4},{3,5},{4,6},{5,7},{6,0},{7,1},{8,10},{9,11},{10,... | collective-permute-start | bytes 196616 | tf_op jit(solution)/shard_map/ppermute | solution.py:489
  36.0 15.0 %all-to-all-start = ((bf16[16,4,896]{2,1,0:T(4,128)(2,1)}), bf16[16,4,896]{2,1,0:T(4,128)(2,1)S(1)}, u32[]{:S(2)}, u32[]{:S(2)}) async-start(bf16[16,4,896]{2,1,0:T(4,128)(2,1)} %hidden.1), calls=%async_computation | async-start | bytes 229376 | tf_op jit(solution)/shard_map/all_to_all | solution.py:494
  55.2 12.0 %copy-start.7 = (bf16[1,2048,896]{2,1,0:T(8,128)(2,1)S(1)}, bf16[1,2048,896]{2,1,0:T(8,128)(2,1)}, u32[]{:S(2)}) copy-start(bf16[1,2048,896]{2,1,0:T(8,128)(2,1)} %w_down.1) | copy-start | bytes 11010052
  56.3 26.3 %copy-start.18 = (f32[8,4]{0,1:T(4,128)S(1)}, f32[8,4]{0,1:T(4,128)}, u32[]{:S(2)}) copy-start(f32[8,4]{0,1:T(4,128)} %param.35) | copy-start | bytes 388
  56.3 1.3 %collective-permute-start.4 = (bf16[16,2176]{1,0:T(8,128)(2,1)S(1)}, bf16[16,2176]{1,0:T(8,128)(2,1)S(1)}, u32[]{:S(2)}, u32[]{:S(2)}) collective-permute-start(bf16[16,2176]{1,0:T(8,128)(2,1)S(1)} %get-tuple-element.14), channel_id=1, source_target_pairs={{0,1},{1,0},{2,3},{3,2},{4,5},{5,4},{6,7},{7,6},{8,9},{9,8},{10,11... | collective-permute-start | bytes 208904 | tf_op jit(solution)/shard_map/ppermute | solution.py:484
  57.8 6.0 %collective-permute-start.7 = (bf16[16,2176]{1,0:T(8,128)(2,1)S(1)}, bf16[16,2176]{1,0:T(8,128)(2,1)S(1)}, u32[]{:S(2)}, u32[]{:S(2)}) collective-permute-start(bf16[16,2176]{1,0:T(8,128)(2,1)S(1)} %pair_sum.1.a), channel_id=1, source_target_pairs={{0,4},{1,5},{2,6},{3,7},{4,0},{5,1},{6,2},{7,3},{8,12},{9,13},{10,... | collective-permute-start | bytes 208904 | tf_op jit(solution)/shard_map/ppermute | solution.py:489
  58.3 5.4 %collective-permute-start.6 = (bf16[16,2176]{1,0:T(8,128)(2,1)S(1)}, bf16[16,2176]{1,0:T(8,128)(2,1)S(1)}, u32[]{:S(2)}, u32[]{:S(2)}) collective-permute-start(bf16[16,2176]{1,0:T(8,128)(2,1)S(1)} %pair_sum.1.a), channel_id=1, source_target_pairs={{0,6},{1,7},{2,0},{3,1},{4,2},{5,3},{6,4},{7,5},{8,14},{9,15},{10,... | collective-permute-start | bytes 208904 | tf_op jit(solution)/shard_map/ppermute | solution.py:489
  60.2 5.5 %collective-permute-start.5 = (bf16[16,2176]{1,0:T(8,128)(2,1)S(1)}, bf16[16,2176]{1,0:T(8,128)(2,1)S(1)}, u32[]{:S(2)}, u32[]{:S(2)}) collective-permute-start(bf16[16,2176]{1,0:T(8,128)(2,1)S(1)} %pair_sum.1.a), channel_id=1, source_target_pairs={{0,2},{1,3},{2,4},{3,5},{4,6},{5,7},{6,0},{7,1},{8,10},{9,11},{10,... | collective-permute-start | bytes 208904 | tf_op jit(solution)/shard_map/ppermute | solution.py:489
  65.9 1.3 %collective-permute-start.8 = (bf16[16,1024]{1,0:T(8,128)(2,1)S(1)}, bf16[16,1024]{1,0:T(8,128)(2,1)S(1)}, u32[]{:S(2)}, u32[]{:S(2)}) collective-permute-start(bf16[16,1024]{1,0:T(8,128)(2,1)S(1)} %activate.1.mine), channel_id=1, source_target_pairs={{0,1},{1,0},{2,3},{3,2},{4,5},{5,4},{6,7},{7,6},{8,9},{9,8},{10,11... | collective-permute-start | bytes 98312 | tf_op jit(solution)/shard_map/ppermute | solution.py:484
  78.9 23.4 %all-to-all-start.3 = ((bf16[16,80,512]{2,1,0:T(8,128)(2,1)}), bf16[16,80,512]{2,1,0:T(8,128)(2,1)S(1)}, u32[]{:S(2)}, u32[]{:S(2)}) async-start(bf16[16,80,512]{2,1,0:T(8,128)(2,1)} %copy-done.8), calls=%async_computation.3 | async-start | bytes 2621440 | tf_op jit(solution)/shard_map/all_to_all | solution.py:494
  (8 other events, 13.6 us)

commit v2 on v1

--- a/solution.py
+++ b/solution.py
@@ -35,6 +35,9 @@
 CHUNKS = 8
 PIECE_ROWS = SEQ_G * 16 + 16
 HALF = FF // 2
+WEIGHT_CUTS = 4
+HIDDEN_CUTS = 8
+EXPAND_COLS = 512
 SCALE = (HEAD_V + ROPE) ** -0.5
 
 VM = pl.BlockSpec(memory_space=pltpu.VMEM)
@@ -64,6 +67,14 @@
     )
 
 
+def in_hbm(value):
+    return pltpu.with_memory_space_constraint(value, pltpu.HBM)
+
+
+def in_vmem(value):
+    return pltpu.with_memory_space_constraint(value, pltpu.VMEM)
+
+
 def split_terms(value, count):
     terms = []
     for _ in range(count):
@@ -97,19 +108,72 @@
 
 
 def attend_kernel(
-    table, lengths, q_latent, q_rope, fresh_latent, fresh_rope, latent, rope, w_uv, packed, wide, narrow
+    table,
+    lengths,
+    routes,
+    q_latent,
+    q_rope,
+    fresh_latent,
+    fresh_rope,
+    rope,
+    latent_hbm,
+    w_uv_hbm,
+    packed,
+    pieces,
+    latent,
+    w_uv,
+    tail,
+    wide,
+    narrow,
+    sems,
+    head_sems,
+    out_sems,
 ):
     group, lane = lax.axis_index("group"), lax.axis_index("lane")
+    loads, pages = [], []
+    for s in range(SEQ_G):
+        for p in range(PSL):
+            at = s * PSL + p
+            loads.append(pltpu.make_async_copy(latent_hbm.at[table[p, s]], latent.at[at], sems.at[at]))
+            loads[-1].start()
+    heads_per = HEADS // WEIGHT_CUTS
+    weights_in = []
+    for i in range(WEIGHT_CUTS):
+        part = pl.ds(i * heads_per, heads_per)
+        weights_in.append(pltpu.make_async_copy(w_uv_hbm.at[part], w_uv.at[part], head_sems.at[i]))
+        weights_in[-1].start()
+    column = iota((NEW_G, LAT), 1)
+    named = jnp.zeros((NEW_G, LAT), F32)
+    for j in range(TOP):
+        named = jnp.where(column == j, to_column(routes[j : j + 1, :].astype(F32)), named)
+    named = jnp.broadcast_to(named[None], (CHUNKS, NEW_G, LAT))
+    for p in range(PSL):
+        turned = [rope[table[p, s]].astype(F32).reshape(CHUNKS, 8, PAGE) for s in range(SEQ_G)]
+        turned = jnp.concatenate(turned, axis=2)
+        tail[p * CHUNKS : (p + 1) * CHUNKS] = jnp.concatenate([turned, named], axis=1).astype(BF16)
+    stores = [pltpu.make_async_copy(tail, pieces.at[:, pl.ds(SEQ_G * 16, 16), :], out_sems.at[SEQ_G * PSL])]
+    stores[0].start()
+    for s in range(SEQ_G):
+        for p in range(PSL):
+            at = s * PSL + p
+            loads[at].wait()
+            stores.append(
+                pltpu.make_async_copy(
+                    latent.at[at],
+                    pieces.at[pl.ds(p * CHUNKS, CHUNKS), pl.ds(s * 16, 16), :],
+                    out_sems.at[at],
+                )
+            )
+            stores[-1].start()
     tops, norms = [], []
     for s in range(SEQ_G):
         length = lengths[group * SEQ_G + s]
         query, turned = q_latent[s], q_rope[s]
         pages, shown, scores = [], [], []
         for p in range(PSL):
-            page = table[s, p]
-            tokens = latent[page]
+            tokens = latent[s * PSL + p].reshape(PAGE, LAT)
             score = lax.dot_general(query, tokens, (((1,), (1,)), ((), ())), preferred_element_type=F32)
-            score = score + jnp.dot(turned, rope[page], preferred_element_type=F32)
+            score = score + jnp.dot(turned, rope[table[p, s]], preferred_element_type=F32)
             visible = (p * LANES + lane) < length
             pages.append(tokens)
             shown.append(visible)
@@ -129,22 +193,36 @@
         for c in range(LAT // 128):
             wide[c, s * HEADS : (s + 1) * HEADS, :] = summed[:, c * 128 : (c + 1) * 128]
     for h in range(HEADS):
+        if h % heads_per == 0:
+            weights_in[h // heads_per].wait()
         rows = pl.ds(h, SEQ_G, stride=HEADS)
         row = jnp.concatenate([wide[c, rows, :] for c in range(LAT // 128)], axis=1).astype(BF16)
         narrow[rows, :] = jnp.dot(row, w_uv[h], preferred_element_type=F32)
     packed[...] = pack_rows(narrow[...], jnp.concatenate(tops, axis=0), jnp.concatenate(norms, axis=0))
-
-
-def attend(table, lengths, q_latent, q_rope, fresh_latent, fresh_rope, latent, rope, w_uv):
+    for store in stores:
+        store.wait()
+
+
+def attend(table, lengths, routes, q_latent, q_rope, fresh_latent, fresh_rope, rope, latent, w_uv):
     return call(
         attend_kernel,
-        shape((SEQ_G * HEADS, 256), BF16),
-        [SM, SM] + [VM] * 7,
-        VM,
-        [pltpu.VMEM((LAT // 128, SEQ_G * HEADS, 128), F32), pltpu.VMEM((SEQ_G * HEADS, 128), F32)],
-        12,
+        (shape((SEQ_G * HEADS, 256), BF16), pltpu.HBM((GROUPS, PIECE_ROWS, LAT), BF16)),
+        [SM, SM] + [VM] * 6 + [ANY, ANY],
+        (VM, ANY),
+        [
+            pltpu.VMEM((SEQ_G * PSL, CHUNKS, 16, LAT), BF16),
+            pltpu.VMEM((HEADS, LAT, HEAD_V), BF16),
+            pltpu.VMEM((GROUPS, 16, LAT), BF16),
+            pltpu.VMEM((LAT // 128, SEQ_G * HEADS, 128), F32),
+            pltpu.VMEM((SEQ_G * HEADS, 128), F32),
+            pltpu.SemaphoreType.DMA((SEQ_G * PSL,)),
+            pltpu.SemaphoreType.DMA((WEIGHT_CUTS,)),
+            pltpu.SemaphoreType.DMA((SEQ_G * PSL + 1,)),
+        ],
+        16,
         "attend",
-    )(table, lengths, q_latent, q_rope, fresh_latent, fresh_rope, latent, rope, w_uv)
+        moved=8 * MIB,
+    )(*[in_hbm(x) for x in (table, lengths, routes, q_latent, q_rope, fresh_latent, fresh_rope, rope, latent, w_uv)])
 
 
 def join_kernel(first, second, packed):
@@ -152,16 +230,25 @@
 
 
 def join_pair(first, second):
-    return call(join_kernel, shape(first.shape, BF16), [VM, VM], VM, [], 4, "join_pair")(first, second)
-
-
-def hidden_kernel(a, b, c, d, residual, w_out, copies, heads):
+    return call(join_kernel, shape(first.shape, BF16), [VM, VM], VM, [], 4, "join_pair", moved=4 * MIB)(first, second)
+
+
+def hidden_kernel(a, b, c, d, residual, w_out_hbm, copies, w_out, heads, sems):
+    depth = HEADS * HEAD_V // HIDDEN_CUTS
+    loads = []
+    for i in range(HIDDEN_CUTS):
+        part = pl.ds(i * depth, depth)
+        loads.append(pltpu.make_async_copy(w_out_hbm.at[part, :], w_out.at[part, :], sems.at[i]))
+        loads[-1].start()
     summed, _, normalizer = join_rows([unpack_rows(x[...]) for x in (a, b, c, d)])
     heads[...] = summed / normalizer
-    flat = jnp.concatenate(
-        [heads[pl.ds(h, SEQ_G, stride=HEADS), :] for h in range(HEADS)], axis=1
-    ).astype(BF16)
-    hidden = residual[...].astype(F32) + jnp.dot(flat, w_out[...], preferred_element_type=F32)
+    hidden = residual[...].astype(F32)
+    per = HEADS // HIDDEN_CUTS
+    for i in range(HIDDEN_CUTS):
+        rows = [heads[pl.ds(h, SEQ_G, stride=HEADS), :] for h in range(i * per, (i + 1) * per)]
+        flat = jnp.concatenate(rows, axis=1).astype(BF16)
+        loads[i].wait()
+        hidden = hidden + jnp.dot(flat, w_out[i * depth : (i + 1) * depth, :], preferred_element_type=F32)
     hidden = hidden.astype(BF16)
     for g in range(GROUPS):
         copies[g] = hidden
@@ -170,52 +257,18 @@
 def hidden_rows(parts, residual, w_out):
     return call(
         hidden_kernel,
-        shape((GROUPS, SEQ_G, WIDTH), BF16),
-        [VM] * 6,
+        pltpu.HBM((GROUPS, SEQ_G, WIDTH), BF16),
+        [VM] * 5 + [ANY],
         VM,
-        [pltpu.VMEM((SEQ_G * HEADS, HEAD_V), F32)],
-        12,
+        [
+            pltpu.VMEM((HEADS * HEAD_V, WIDTH), BF16),
+            pltpu.VMEM((SEQ_G * HEADS, HEAD_V), F32),
+            pltpu.SemaphoreType.DMA((HIDDEN_CUTS,)),
+        ],
+        16,
         "hidden",
-    )(*parts, residual, w_out)
-
-
-def spread_kernel(table, routes, latent, rope, out, tail, sems):
-    copies = []
-    for s in range(SEQ_G):
-        for p in range(PSL):
-            copies.append(
-                pltpu.make_async_copy(
-                    latent.at[table[s, p]],
-                    out.at[pl.ds(p * CHUNKS, CHUNKS), pl.ds(s * 16, 16), :],
-                    sems.at[s * PSL + p],
-                )
-            )
-            copies[-1].start()
-    lane = iota((NEW_G, LAT), 1)
-    named = jnp.zeros((NEW_G, LAT), F32)
-    for j in range(TOP):
-        named = jnp.where(lane == j, routes[:, j : j + 1].astype(F32), named)
-    named = jnp.broadcast_to(named[None], (CHUNKS, NEW_G, LAT))
-    for p in range(PSL):
-        turned = [rope[table[s, p]].astype(F32).reshape(CHUNKS, 8, PAGE) for s in range(SEQ_G)]
-        turned = jnp.concatenate(turned, axis=2)
-        tail[p * CHUNKS : (p + 1) * CHUNKS] = jnp.concatenate([turned, named], axis=1).astype(BF16)
-    copies.append(pltpu.make_async_copy(tail, out.at[:, pl.ds(SEQ_G * 16, 16), :], sems.at[SEQ_G * PSL]))
-    copies[-1].start()
-    for copy in copies:
-        copy.wait()
-
-
-def spread(table, routes, latent, rope):
-    return call(
-        spread_kernel,
-        shape((GROUPS, PIECE_ROWS, LAT), BF16),
-        [SM, VM, ANY, VM],
-        ANY,
-        [pltpu.VMEM((GROUPS, 16, LAT), BF16), pltpu.SemaphoreType.DMA((SEQ_G * PSL + 1,))],
-        6,
-        "spread",
-    )(table, routes, latent, rope)
+        moved=8 * MIB,
+    )(*parts, residual, in_hbm(w_out))
 
 
 def to_column(row):
@@ -238,7 +291,7 @@
     return slot, leaves
 
 
-def route_kernel(destiny, destiny_row, pieces, out, choose, source, count):
+def route_kernel(destiny, destiny_row, pieces, sent, choose, source, count, out, sem):
     expert = lax.axis_index("group")
     for i in range(GROUPS):
         count[i] = 0
@@ -258,6 +311,11 @@
             cols = pl.ds(pl.multiple_of(rank * 128, 128), 128)
             out[keeper, SEQ_G * 16 :, cols] = pieces[g, SEQ_G * 16 :, s * 128 : (s + 1) * 128]
 
+    copies = []
+    for i in range(4):
+        part = pl.ds(i * (GROUPS // 4), GROUPS // 4)
+        copies.append(pltpu.make_async_copy(out.at[part], sent.at[part], sem.at[i]))
+        copies[-1].start()
     slot, leaves = slots_of(destiny_row[...].astype(F32))
     new_group = jnp.floor(slot * (1.0 / NEW_G))
     named = pieces[:, SEQ_G * 16 :, 0:128].astype(F32)[:, 8:, :].reshape(SLOTS, 128)
@@ -277,17 +335,20 @@
     )
     row = iota((ROWS, SEQS), 0).astype(F32)
     choose[...] = jnp.where((row == keeper_rank * CAP + before) & (mine > 0.5), 1.0, 0.0).astype(BF16)
+    for copy in copies:
+        copy.wait()
 
 
 def route(destiny, destiny_row, pieces):
     return call(
         route_kernel,
-        (shape((GROUPS, PIECE_ROWS, LAT), BF16), shape((ROWS, SEQS), BF16), shape((SEQS,), I32)),
+        (pltpu.HBM((GROUPS, PIECE_ROWS, LAT), BF16), shape((ROWS, SEQS), BF16), shape((SEQS,), I32)),
         [SM, VM, VM],
-        (VM, VM, SM),
-        [pltpu.SMEM((GROUPS,), I32)],
+        (ANY, VM, SM),
+        [pltpu.SMEM((GROUPS,), I32), pltpu.VMEM((GROUPS, PIECE_ROWS, LAT), BF16), pltpu.SemaphoreType.DMA((4,))],
         8,
         "route",
+        moved=8 * MIB,
     )(destiny, destiny_row, pieces)
 
 
@@ -300,7 +361,7 @@
         s, p = i // PSL, i % PSL
         if s < SEQ_G:
             seq = group * SEQ_G + s
-            taken = latent.at[table[s, p]]
+            taken = latent.at[table[p, s]]
         else:
             seq = source[group * SEQ_G + s - SEQ_G]
             taken = pieces.at[pl.ds(p * CHUNKS, CHUNKS), pl.ds((s - SEQ_G) * 16, 16), :]
@@ -311,7 +372,7 @@
         pl.when(jnp.logical_not(visible))(blank.start)
         waits.append(blank)
         if s < SEQ_G:
-            page = rope[table[s, p]].astype(F32)
+            page = rope[table[p, s]].astype(F32)
         else:
             c = s - SEQ_G
             page = tails[p * CHUNKS : (p + 1) * CHUNKS, SEQ_G * 16 :, c * 128 : (c + 1) * 128].astype(F32)
@@ -330,6 +391,7 @@
         [pltpu.VMEM((CHUNKS, 16, LAT), BF16), pltpu.SemaphoreType.DMA((NEW_G * PSL,))],
         6,
         "keep",
+        moved=8 * MIB,
     )(destiny, lengths, table, source, latent, rope, pieces, pieces)
 
 
@@ -339,33 +401,51 @@
     return rows[...].astype(BF16)
 
 
-def expand_kernel(hidden, choose, gain, w_gate, w_up, keep_half, send_half, rows):
+def expand_kernel(hidden, choose, gain, w_gate, w_up, keep_half, send_half, rows, held, sems):
     core = lax.rem(lax.axis_index("lane"), 2)
-    mine = pl.ds(pl.multiple_of(core * HALF, HALF), HALF)
-    other = pl.ds(pl.multiple_of((1 - core) * HALF, HALF), HALF)
+    loads = []
+    for half in range(2):
+        first = (1 - core if half == 0 else core) * HALF
+        for weights in (w_gate, w_up):
+            for part in range(HALF // EXPAND_COLS):
+                cols = pl.ds(pl.multiple_of(first + part * EXPAND_COLS, EXPAND_COLS), EXPAND_COLS)
+                at = len(loads)
+                loads.append(pltpu.make_async_copy(weights.at[0, :, cols], held.at[at], sems.at[at]))
+                loads[-1].start()
     taken = jnp.dot(choose[...], gather_hidden(hidden, rows), preferred_element_type=F32)
     squares = jnp.sum(taken * taken, axis=1, keepdims=True)
     scaled = (taken * gain[...].astype(F32)).astype(BF16)
-    for i, weights in enumerate((w_gate, w_up)):
-        cols = slice(i * HALF, (i + 1) * HALF)
-        send_half[:, cols] = jnp.dot(scaled, weights[0, :, other], preferred_element_type=F32).astype(BF16)
-        keep_half[:, cols] = jnp.dot(scaled, weights[0, :, mine], preferred_element_type=F32)
     lane = iota((ROWS, 128), 1)
     keep_half[:, FF:] = jnp.where(lane == 0, squares, 0.0)
     high, low = split_terms(squares, 2)
     send_half[:, FF:] = jnp.where(lane == 0, high, jnp.where(lane == 1, low, 0.0)).astype(BF16)
+    for at, load in enumerate(loads):
+        load.wait()
+        made = jnp.dot(scaled, held[at], preferred_element_type=F32)
+        per_half = len(loads) // 2
+        cols = slice((at % per_half) * EXPAND_COLS, (at % per_half + 1) * EXPAND_COLS)
+        if at < per_half:
+            send_half[:, cols] = made.astype(BF16)
+        else:
+            keep_half[:, cols] = made
 
 
 def expand(hidden, choose, gain, w_gate, w_up):
+    cuts = 2 * FF // EXPAND_COLS
     return call(
         expand_kernel,
         (shape((ROWS, FF + 128), F32), shape((ROWS, FF + 128), BF16)),
-        [VM] * 5,
+        [VM] * 3 + [ANY] * 2,
         (VM, VM),
-        [pltpu.VMEM((SEQS, WIDTH), F32)],
-        12,
+        [
+            pltpu.VMEM((SEQS, WIDTH), F32),
+            pltpu.VMEM((cuts, WIDTH, EXPAND_COLS), BF16),
+            pltpu.SemaphoreType.DMA((cuts,)),
+        ],
+        16,
         "expand",
-    )(hidden, choose, gain, w_gate, w_up)
+        moved=8 * MIB,
+    )(hidden, choose, gain, in_hbm(w_gate), in_hbm(w_up))
 
 
 def pair_kernel(kept, arrived, out):
@@ -377,7 +457,7 @@
 
 
 def pair_sum(kept, arrived):
-    return call(pair_kernel, shape((ROWS, FF + 128), BF16), [VM, VM], VM, [], 4, "pair_sum")(kept, arrived)
+    return call(pair_kernel, shape((ROWS, FF + 128), BF16), [VM, VM], VM, [], 4, "pair_sum", moved=4 * MIB)(kept, arrived)
 
 
 def activate_kernel(a, b, c, d, out):
@@ -390,7 +470,7 @@
 
 
 def activate(parts):
-    return call(activate_kernel, shape((ROWS, HALF), BF16), [VM] * 4, VM, [], 4, "activate")(*parts)
+    return call(activate_kernel, shape((ROWS, HALF), BF16), [VM] * 4, VM, [], 4, "activate", moved=4 * MIB)(*parts)
 
 
 def down_kernel(mine, other, destiny_row, w_down, out, rows):
@@ -424,6 +504,7 @@
         [pltpu.VMEM((GROUPS * CAP, WIDTH), F32)],
         8,
         "down",
+        moved=4 * MIB,
     )(mine, other, destiny_row, w_down)
 
 
@@ -433,13 +514,13 @@
     place = (iota((NEW_G, SEQS), 0) + group * NEW_G).astype(F32)
     matrix = jnp.where(place == slot, 1.0, 0.0).astype(BF16)
     own[...] = jnp.dot(matrix, gather_hidden(hidden, rows), preferred_element_type=F32)
-    expert = iota((NEW_G, GROUPS * CAP), 1) // CAP
+    expert = (iota((NEW_G, GROUPS * CAP), 1) // CAP).astype(F32)
     hits = jnp.zeros((NEW_G, GROUPS * CAP), F32)
     weight = jnp.zeros((NEW_G, GROUPS * CAP), F32)
     for j in range(TOP):
-        same = routes[:, j : j + 1] == expert
+        same = to_column(routes[j : j + 1, :].astype(F32)) == expert
         hits = jnp.where(same, 1.0, hits)
-        weight = jnp.where(same, gates[:, j : j + 1], weight)
+        weight = jnp.where(same, to_column(gates[j : j + 1, :]), weight)
     later = (iota((NEW_G, NEW_G), 1) < iota((NEW_G, NEW_G), 0)).astype(F32)
     before = jnp.dot(later, hits, preferred_element_type=F32)
     want = (iota((NEW_G, GROUPS * CAP), 1) % CAP).astype(F32)
@@ -455,6 +536,7 @@
         [pltpu.VMEM((SEQS, WIDTH), F32)],
         4,
         "own_rows",
+        moved=4 * MIB,
     )(hidden, destiny_row, routes, gates)
 
 
@@ -477,6 +559,7 @@
         [pltpu.VMEM((GROUPS * CAP, WIDTH), F32)],
         4,
         "finish",
+        moved=4 * MIB,
     )(returned, own, combine)
 
 
@@ -492,10 +575,6 @@
 
 def exchange(value):
     return lax.all_to_all(value, "group", split_axis=0, concat_axis=0, tiled=True)
-
-
-def in_vmem(value):
-    return pltpu.with_memory_space_constraint(value, pltpu.VMEM)
 
 
 def per_device(
@@ -521,21 +600,24 @@
     cut_latent = kv_latent.reshape(-1, CHUNKS, 16, LAT)
     destiny_row = destiny.reshape(1, SEQS)
     gain = norm_gain.reshape(1, WIDTH)
-
-    scattered = exchange(spread(page_table, routes, cut_latent, kv_rope))
-
-    packed = attend(page_table, seq_pages, q_latent, q_rope, new_latent, new_rope, kv_latent, kv_rope, in_vmem(w_uv))
+    page_table, routes, route_gates = page_table.T, routes.T, route_gates.T
+
+    packed, cut = attend(
+        page_table, seq_pages, routes, q_latent, q_rope, new_latent, new_rope, kv_rope, cut_latent, w_uv
+    )
+    scattered = exchange(cut)
     packed = join_pair(packed, swap_core(packed))
-    copies = hidden_rows(around(packed), residual_in, in_vmem(w_out))
+    copies = hidden_rows(around(packed), residual_in, w_out)
     hidden = exchange(copies)
 
     forwarded, choose, source = route(destiny, destiny_row, scattered)
     gathered = exchange(forwarded)
 
-    keep_half, send_half = expand(hidden, choose, gain, in_vmem(w_gate), in_vmem(w_up))
+    keep_half, send_half = expand(hidden, choose, gain, w_gate, w_up)
     total = pair_sum(keep_half, swap_core(send_half))
     active = activate(around(total))
     made = down(active, swap_core(active), destiny_row, in_vmem(w_down))
+    made, gathered = lax.optimization_barrier((made, gathered))
     returned = exchange(made)
 
     own, combine = own_rows(hidden, destiny_row, routes, route_gates)

time: 106 us -> 84.6 us (0.80)
  local copies, waits for them, and re-layouts: 15.2 us -> 0.07 us
  blocking collectives: 11 us -> 0 us
  waiting for transfers between devices: 37 us -> 27.1 us
  Pallas kernels: 13.9 us -> 23 us
  starting transfers between devices: 27 us -> 33.1 us
    unnamed x43 -> x20, local copies, waits for them, and re-layouts: 15.2 us -> 0.06 us
    all_to_all x1 -> x0, blocking collectives: 11 us -> none  [exchange(): lax.all_to_all(value, 'group', split_axis=0, concat_axis=0, tiled=True)]
    all_to_all x3 -> x4, waiting for transfers between devices: 23.4 us -> 14.4 us  [exchange(): lax.all_to_all(value, 'group', split_axis=0, concat_axis=0, tiled=True)]
    pallas_call x4 -> x3, Pallas kernels: 7.56 us -> 13.6 us  [the longest x1 6.3 us: attend(): call(attend_kernel, (shape((SEQ_G * HEADS, 256), BF16), pltpu.HBM((GROUPS...]
    all_to_all x3 -> x4, starting transfers between devices: 19 us -> 22.3 us  [exchange(): lax.all_to_all(value, 'group', split_axis=0, concat_axis=0, tiled=True)]
    ppermute x6, starting transfers between devices: 7.86 us -> 10.5 us  [around(): lax.ppermute(value, 'lane', [(i, (i + 2 * step) % LANES) for i in range(L...]
    pallas_call x1, Pallas kernels: 1.18 us -> 3.65 us  [expand(): call(expand_kernel, (shape((ROWS, FF + 128), F32), shape((ROWS, FF + 128)...]
  transfers between devices with their start and end apart: 12 -> 13, of which waited for: 10 -> 12; matrix products, arithmetic and copies ran while one was open for 0% -> 0% of each run, Pallas kernels for 8% -> 19%
where the time goes in v2:
time: 84.6 us; the launch traced here: 84.2 us
  starting transfers between devices  33.1 us (39%)
  waiting for transfers between devices  27.1 us (32%)
  Pallas kernels  23 us (27%)
  between operations  0.89 us (1%)
    all_to_all x4, starting transfers between devices, exchange(): lax.all_to_all(value, 'group', split_axis=0, concat_axis=0, tiled=True)  22.3 us
    all_to_all x4, waiting for transfers between devices, exchange(): lax.all_to_all(value, 'group', split_axis=0, concat_axis=0, tiled=True)  14.4 us
    ppermute x6, starting transfers between devices, around(): lax.ppermute(value, 'lane', [(i, (i + 2 * step) % LANES) for i in range(L...  10.5 us
    ppermute x6, waiting for transfers between devices, around(): lax.ppermute(value, 'lane', [(i, (i + 2 * step) % LANES) for i in range(L...  9.05 us
    pallas_call x1, Pallas kernels, attend(): call(attend_kernel, (shape((SEQ_G * HEADS, 256), BF16), pltpu.HBM((GROUPS...  6.3 us
    pallas_call x1, Pallas kernels, hidden_rows(): call(hidden_kernel, pltpu.HBM((GROUPS, SEQ_G, WIDTH), BF16), [VM] * 5 + [...  4.37 us
    ppermute x3, waiting for transfers between devices, swap_core(): return lax.ppermute(value, 'lane', [(i, i ^ 1) for i in range(LANES)])  3.68 us
    pallas_call x1, Pallas kernels, expand(): call(expand_kernel, (shape((ROWS, FF + 128), F32), shape((ROWS, FF + 128)...  3.65 us
  transfers between devices with their start and end apart: 13, of which 12 were waited for; matrix products, arithmetic and copies ran while one was open for 0% of the time, Pallas kernels for 19%

profile of v2, /device:TPU:0, one launch (start us, length us, event | category | flops | bytes accessed | tf_op | source)
XLA Modules:
  0.0 84.2 jit_solution(13827572693458936431)
XLA Ops:
  0.6 6.3 %attend.1 = (bf16[128,256]{1,0:T(8,128)(2,1)S(1)}, bf16[16,80,512]{2,1,0:T(8,128)(2,1)}) custom-call(s32[2,4]{1,0:T(2,128)} %bitcast.13, s32[64]{0:T(128)} %lengths.3, s32[4,8]{1,0:T(4,128)} %bitcast.11, bf16[4,32,512]{2,1,0:T(8,128)(2,1)} %q_latent.1, bf16[4,32,64]{2,1,0:T(8,128)(2,1)} %q_rope.1, bf16[4,512]{1,0:T(4,128)(2,1)} %fresh_latent.1, ...), custom_call_target="tpu_custom_call" | custom-call | bytes 8388608 | tf_op jit(solution)/shard_map/attend/pallas_call | solution.py:207
  7.0 8.0 %all-to-all-start.1 = ((bf16[16,80,512]{2,1,0:T(8,128)(2,1)}), bf16[16,80,512]{2,1,0:T(8,128)(2,1)S(1)}, u32[]{:S(2)}, u32[]{:S(2)}) async-start(bf16[16,80,512]{2,1,0:T(8,128)(2,1)} %get-tuple-element.17), calls=%async_computation.1 | async-start | bytes 2621440 | tf_op jit(solution)/shard_map/all_to_all | solution.py:577
  15.0 1.2 %collective-permute-done.second = bf16[128,256]{1,0:T(8,128)(2,1)S(1)} collective-permute-done((bf16[128,256]{1,0:T(8,128)(2,1)S(1)}, bf16[128,256]{1,0:T(8,128)(2,1)S(1)}, u32[]{:S(2)}, u32[]{:S(2)}) %collective-permute-start) | collective-permute-done | bytes 65568 | tf_op jit(solution)/shard_map/ppermute | solution.py:567
  16.6 3.3 %collective-permute-start.3 = (bf16[128,256]{1,0:T(8,128)(2,1)S(1)}, bf16[128,256]{1,0:T(8,128)(2,1)S(1)}, u32[]{:S(2)}, u32[]{:S(2)}) collective-permute-start(bf16[128,256]{1,0:T(8,128)(2,1)S(1)} %join_pair.1.a), channel_id=1, source_target_pairs={{0,4},{1,5},{2,6},{3,7},{4,0},{5,1},{6,2},{7,3},{8,12},{9,13},{10,... | collective-permute-start | bytes 196616 | tf_op jit(solution)/shard_map/ppermute | solution.py:572
  19.9 1.1 %collective-permute-start.2 = (bf16[128,256]{1,0:T(8,128)(2,1)S(1)}, bf16[128,256]{1,0:T(8,128)(2,1)S(1)}, u32[]{:S(2)}, u32[]{:S(2)}) collective-permute-start(bf16[128,256]{1,0:T(8,128)(2,1)S(1)} %join_pair.1.a), channel_id=1, source_target_pairs={{0,6},{1,7},{2,0},{3,1},{4,2},{5,3},{6,4},{7,5},{8,14},{9,15},{10,... | collective-permute-start | bytes 196616 | tf_op jit(solution)/shard_map/ppermute | solution.py:572
  22.5 1.7 %collective-permute-done.2.c = bf16[128,256]{1,0:T(8,128)(2,1)S(1)} collective-permute-done((bf16[128,256]{1,0:T(8,128)(2,1)S(1)}, bf16[128,256]{1,0:T(8,128)(2,1)S(1)}, u32[]{:S(2)}, u32[]{:S(2)}) %collective-permute-start.2) | collective-permute-done | bytes 65568 | tf_op jit(solution)/shard_map/ppermute | solution.py:572
  24.2 2.2 %collective-permute-done.1.b = bf16[128,256]{1,0:T(8,128)(2,1)S(1)} collective-permute-done((bf16[128,256]{1,0:T(8,128)(2,1)S(1)}, bf16[128,256]{1,0:T(8,128)(2,1)S(1)}, u32[]{:S(2)}, u32[]{:S(2)}) %collective-permute-start.1) | collective-permute-done | bytes 65568 | tf_op jit(solution)/shard_map/ppermute | solution.py:572
  26.4 4.4 %hidden.1 = bf16[16,4,896]{2,1,0:T(4,128)(2,1)} custom-call(bf16[128,256]{1,0:T(8,128)(2,1)S(1)} %join_pair.1.a, bf16[128,256]{1,0:T(8,128)(2,1)S(1)} %collective-permute-done.1.b, bf16[128,256]{1,0:T(8,128)(2,1)S(1)} %collective-permute-done.2.c, bf16[128,256]{1,0:T(8,128)(2,1)S(1)} %collective-permute-done.3.d, bf16[4,896]{1,0:T(4,128)(2,1)S(1)} %copy-done.5, ...), custom_call_target="tpu_custom_call" | custom-call | bytes 8388608 | tf_op jit(solution)/shard_map/hidden/pallas_call | solution.py:258
  30.8 4.9 %all-to-all-done.1.pieces = bf16[16,80,512]{2,1,0:T(8,128)(2,1)S(1)} async-done(((bf16[16,80,512]{2,1,0:T(8,128)(2,1)}), bf16[16,80,512]{2,1,0:T(8,128)(2,1)S(1)}, u32[]{:S(2)}, u32[]{:S(2)}) %all-to-all-start.1) | async-done | bytes 1310752 | tf_op jit(solution)/shard_map/all_to_all | solution.py:577
  35.7 3.5 %all-to-all-start = ((bf16[16,4,896]{2,1,0:T(4,128)(2,1)}), bf16[16,4,896]{2,1,0:T(4,128)(2,1)S(1)}, u32[]{:S(2)}, u32[]{:S(2)}) async-start(bf16[16,4,896]{2,1,0:T(4,128)(2,1)} %hidden.1), calls=%async_computation | async-start | bytes 229376 | tf_op jit(solution)/shard_map/all_to_all | solution.py:577
  39.3 2.9 %route.1 = (bf16[16,80,512]{2,1,0:T(8,128)(2,1)}, bf16[16,64]{1,0:T(8,128)(2,1)S(1)}, s32[64]{0:T(128)S(1)}) custom-call(s32[64]{0:T(128)S(1)} %copy-done.3, s32[1,64]{1,0:T(1,128)S(1)} %bitcast.8, bf16[16,80,512]{2,1,0:T(8,128)(2,1)S(1)} %all-to-all-done.1.pieces), custom_call_target="tpu_custom_call" | custom-call | bytes 8388608 | tf_op jit(solution)/shard_map/route/pallas_call | solution.py:343
  42.2 4.8 %all-to-all-done.hidden = bf16[16,4,896]{2,1,0:T(4,128)(2,1)S(1)} async-done(((bf16[16,4,896]{2,1,0:T(4,128)(2,1)}), bf16[16,4,896]{2,1,0:T(4,128)(2,1)S(1)}, u32[]{:S(2)}, u32[]{:S(2)}) %all-to-all-start) | async-done | bytes 114720 | tf_op jit(solution)/shard_map/all_to_all | solution.py:577
  47.0 3.7 %all-to-all-start.2 = ((bf16[16,80,512]{2,1,0:T(8,128)(2,1)}), bf16[16,80,512]{2,1,0:T(8,128)(2,1)S(1)}, u32[]{:S(2)}, u32[]{:S(2)}) async-start(bf16[16,80,512]{2,1,0:T(8,128)(2,1)} %get-tuple-element.21), calls=%async_computation.2 | async-start | bytes 2621440 | tf_op jit(solution)/shard_map/all_to_all | solution.py:577
  50.8 3.7 %expand.1 = (f32[16,2176]{1,0:T(8,128)S(1)}, bf16[16,2176]{1,0:T(8,128)(2,1)S(1)}) custom-call(bf16[16,4,896]{2,1,0:T(4,128)(2,1)S(1)} %all-to-all-done.hidden, bf16[16,64]{1,0:T(8,128)(2,1)S(1)} %get-tuple-element.18.choose, bf16[1,896]{1,0:T(2,128)(2,1)S(1)} %reshape.20.gain, bf16[1,896,2048]{2,1,0:T(8,128)(2,1)} %w_gate.1, bf16[1,896,2048]{2,1,0:T(8,128)(2,1)} %w_up.1), custom_call_target="tpu_custom_call" | custom-call | bytes 8388608 | tf_op jit(solution)/shard_map/expand/pallas_call | solution.py:435
  54.6 1.2 %collective-permute-done.4.arrived = bf16[16,2176]{1,0:T(8,128)(2,1)S(1)} collective-permute-done((bf16[16,2176]{1,0:T(8,128)(2,1)S(1)}, bf16[16,2176]{1,0:T(8,128)(2,1)S(1)}, u32[]{:S(2)}, u32[]{:S(2)}) %collective-permute-start.4) | collective-permute-done | bytes 69664 | tf_op jit(solution)/shard_map/ppermute | solution.py:567
  56.0 3.2 %collective-permute-start.7 = (bf16[16,2176]{1,0:T(8,128)(2,1)S(1)}, bf16[16,2176]{1,0:T(8,128)(2,1)S(1)}, u32[]{:S(2)}, u32[]{:S(2)}) collective-permute-start(bf16[16,2176]{1,0:T(8,128)(2,1)S(1)} %pair_sum.1.a), channel_id=1, source_target_pairs={{0,4},{1,5},{2,6},{3,7},{4,0},{5,1},{6,2},{7,3},{8,12},{9,13},{10,... | collective-permute-start | bytes 208904 | tf_op jit(solution)/shard_map/ppermute | solution.py:572
  59.2 1.1 %collective-permute-start.6 = (bf16[16,2176]{1,0:T(8,128)(2,1)S(1)}, bf16[16,2176]{1,0:T(8,128)(2,1)S(1)}, u32[]{:S(2)}, u32[]{:S(2)}) collective-permute-start(bf16[16,2176]{1,0:T(8,128)(2,1)S(1)} %pair_sum.1.a), channel_id=1, source_target_pairs={{0,6},{1,7},{2,0},{3,1},{4,2},{5,3},{6,4},{7,5},{8,14},{9,15},{10,... | collective-permute-start | bytes 208904 | tf_op jit(solution)/shard_map/ppermute | solution.py:572
  61.8 1.8 %collective-permute-done.6.c = bf16[16,2176]{1,0:T(8,128)(2,1)S(1)} collective-permute-done((bf16[16,2176]{1,0:T(8,128)(2,1)S(1)}, bf16[16,2176]{1,0:T(8,128)(2,1)S(1)}, u32[]{:S(2)}, u32[]{:S(2)}) %collective-permute-start.6) | collective-permute-done | bytes 69664 | tf_op jit(solution)/shard_map/ppermute | solution.py:572
  63.6 2.1 %collective-permute-done.5.b = bf16[16,2176]{1,0:T(8,128)(2,1)S(1)} collective-permute-done((bf16[16,2176]{1,0:T(8,128)(2,1)S(1)}, bf16[16,2176]{1,0:T(8,128)(2,1)S(1)}, u32[]{:S(2)}, u32[]{:S(2)}) %collective-permute-start.5) | collective-permute-done | bytes 69664 | tf_op jit(solution)/shard_map/ppermute | solution.py:572
  66.0 1.2 %collective-permute-done.8.other = bf16[16,1024]{1,0:T(8,128)(2,1)S(1)} collective-permute-done((bf16[16,1024]{1,0:T(8,128)(2,1)S(1)}, bf16[16,1024]{1,0:T(8,128)(2,1)S(1)}, u32[]{:S(2)}, u32[]{:S(2)}) %collective-permute-start.8) | collective-permute-done | bytes 32800 | tf_op jit(solution)/shard_map/ppermute | solution.py:567
  67.2 1.4 %down.1 = bf16[16,2,896]{2,1,0:T(2,128)(2,1)} custom-call(bf16[16,1024]{1,0:T(8,128)(2,1)S(1)} %activate.1.mine, bf16[16,1024]{1,0:T(8,128)(2,1)S(1)} %collective-permute-done.8.other, s32[1,64]{1,0:T(1,128)S(1)} %bitcast.9, bf16[1,2048,896]{2,1,0:T(8,128)(2,1)S(1)} %copy-done.1), custom_call_target="tpu_custom_call" | custom-call | bytes 4194304 | tf_op jit(solution)/shard_map/down/pallas_call | solution.py:499
  68.6 7.2 %all-to-all-start.3 = ((bf16[16,2,896]{2,1,0:T(2,128)(2,1)}), bf16[16,2,896]{2,1,0:T(2,128)(2,1)S(1)}, u32[]{:S(2)}, u32[]{:S(2)}) async-start(bf16[16,2,896]{2,1,0:T(2,128)(2,1)} %down.1), calls=%async_computation.3 | async-start | bytes 114688 | tf_op jit(solution)/shard_map/all_to_all | solution.py:577
  76.0 2.7 %keep.1 = (bf16[16,8,16,512]{3,2,1,0:T(8,128)(2,1)}, bf16[16,64,128]{2,1,0:T(8,128)(2,1)}) custom-call(s32[64]{0:T(128)S(1)} %copy-done.3, s32[64]{0:T(128)S(1)} %copy-done.7, s32[2,4]{1,0:T(2,128)S(1)} %bitcast.14, s32[64]{0:T(128)S(1)} %get-tuple-element.25.source, bf16[8,8,16,512]{3,2,1,0:T(8,128)(2,1)S(1)} %bitcast.7, bf16[8,64,128]{2,1,0:T(8,128)(2,1)S(1)} %copy-done.2, ...), custom_call_target="tpu_custom_call" | custom-call | bytes 8388608 | tf_op jit(solution)/shard_map/keep/pallas_call | solution.py:386
  78.8 4.6 %all-to-all-done.3.returned = bf16[16,2,896]{2,1,0:T(2,128)(2,1)S(1)} async-done(((bf16[16,2,896]{2,1,0:T(2,128)(2,1)}), bf16[16,2,896]{2,1,0:T(2,128)(2,1)S(1)}, u32[]{:S(2)}, u32[]{:S(2)}) %all-to-all-start.3) | async-done | bytes 57376 | tf_op jit(solution)/shard_map/all_to_all | solution.py:577
  (34 shorter events, 5.1 us)
Async XLA Ops:
  0.6 25.8 %copy-start.5 = (bf16[4,896]{1,0:T(4,128)(2,1)S(1)}, bf16[4,896]{1,0:T(4,128)(2,1)}, u32[]{:S(2)}) copy-start(bf16[4,896]{1,0:T(4,128)(2,1)} %residual.1) | copy-start | bytes 21508
  7.0 28.8 %all-to-all-start.1 = ((bf16[16,80,512]{2,1,0:T(8,128)(2,1)}), bf16[16,80,512]{2,1,0:T(8,128)(2,1)S(1)}, u32[]{:S(2)}, u32[]{:S(2)}) async-start(bf16[16,80,512]{2,1,0:T(8,128)(2,1)} %get-tuple-element.17), calls=%async_computation.1 | async-start | bytes 2621440 | tf_op jit(solution)/shard_map/all_to_all | solution.py:577
  14.9 1.3 %collective-permute-start = (bf16[128,256]{1,0:T(8,128)(2,1)S(1)}, bf16[128,256]{1,0:T(8,128)(2,1)S(1)}, u32[]{:S(2)}, u32[]{:S(2)}) collective-permute-start(bf16[128,256]{1,0:T(8,128)(2,1)S(1)} %get-tuple-element.16.first), channel_id=1, source_target_pairs={{0,1},{1,0},{2,3},{3,2},{4,5},{5,4},{6,7},{7,6},{8,9},{9,8},{10,11... | collective-permute-start | bytes 196616 | tf_op jit(solution)/shard_map/ppermute | solution.py:567
  16.6 22.6 %copy-start.3 = (s32[64]{0:T(128)S(1)}, s32[64]{0:T(128)}, u32[]{:S(2)}) copy-start(s32[64]{0:T(128)} %destiny.3) | copy-start | bytes 772
  16.6 5.8 %collective-permute-start.3 = (bf16[128,256]{1,0:T(8,128)(2,1)S(1)}, bf16[128,256]{1,0:T(8,128)(2,1)S(1)}, u32[]{:S(2)}, u32[]{:S(2)}) collective-permute-start(bf16[128,256]{1,0:T(8,128)(2,1)S(1)} %join_pair.1.a), channel_id=1, source_target_pairs={{0,4},{1,5},{2,6},{3,7},{4,0},{5,1},{6,2},{7,3},{8,12},{9,13},{10,... | collective-permute-start | bytes 196616 | tf_op jit(solution)/shard_map/ppermute | solution.py:572
  19.9 4.3 %collective-permute-start.2 = (bf16[128,256]{1,0:T(8,128)(2,1)S(1)}, bf16[128,256]{1,0:T(8,128)(2,1)S(1)}, u32[]{:S(2)}, u32[]{:S(2)}) collective-permute-start(bf16[128,256]{1,0:T(8,128)(2,1)S(1)} %join_pair.1.a), channel_id=1, source_target_pairs={{0,6},{1,7},{2,0},{3,1},{4,2},{5,3},{6,4},{7,5},{8,14},{9,15},{10,... | collective-permute-start | bytes 196616 | tf_op jit(solution)/shard_map/ppermute | solution.py:572
  20.9 5.5 %collective-permute-start.1 = (bf16[128,256]{1,0:T(8,128)(2,1)S(1)}, bf16[128,256]{1,0:T(8,128)(2,1)S(1)}, u32[]{:S(2)}, u32[]{:S(2)}) collective-permute-start(bf16[128,256]{1,0:T(8,128)(2,1)S(1)} %join_pair.1.a), channel_id=1, source_target_pairs={{0,2},{1,3},{2,4},{3,5},{4,6},{5,7},{6,0},{7,1},{8,10},{9,11},{10,... | collective-permute-start | bytes 196616 | tf_op jit(solution)/shard_map/ppermute | solution.py:572
  30.8 19.9 %copy-start.9 = (bf16[896]{0:T(1024)(128)(2,1)S(1)}, bf16[896]{0:T(1024)(128)(2,1)}, u32[]{:S(2)}) copy-start(bf16[896]{0:T(1024)(128)(2,1)} %param.30) | copy-start | bytes 5380
  35.7 11.3 %all-to-all-start = ((bf16[16,4,896]{2,1,0:T(4,128)(2,1)}), bf16[16,4,896]{2,1,0:T(4,128)(2,1)S(1)}, u32[]{:S(2)}, u32[]{:S(2)}) async-start(bf16[16,4,896]{2,1,0:T(4,128)(2,1)} %hidden.1), calls=%async_computation | async-start | bytes 229376 | tf_op jit(solution)/shard_map/all_to_all | solution.py:577
  47.0 21.6 %all-to-all-start.2 = ((bf16[16,80,512]{2,1,0:T(8,128)(2,1)}), bf16[16,80,512]{2,1,0:T(8,128)(2,1)S(1)}, u32[]{:S(2)}, u32[]{:S(2)}) async-start(bf16[16,80,512]{2,1,0:T(8,128)(2,1)} %get-tuple-element.21), calls=%async_computation.2 | async-start | bytes 2621440 | tf_op jit(solution)/shard_map/all_to_all | solution.py:577
  50.8 16.5 %copy-start.1 = (bf16[1,2048,896]{2,1,0:T(8,128)(2,1)S(1)}, bf16[1,2048,896]{2,1,0:T(8,128)(2,1)}, u32[]{:S(2)}) copy-start(bf16[1,2048,896]{2,1,0:T(8,128)(2,1)} %w_down.1) | copy-start | bytes 11010052
  54.4 21.3 %copy-start.4 = (s32[8,4]{0,1:T(4,128)S(1)}, s32[8,4]{0,1:T(4,128)}, u32[]{:S(2)}) copy-start(s32[8,4]{0,1:T(4,128)} %param.34) | copy-start | bytes 388
  54.4 21.3 %copy-start.8 = (f32[8,4]{0,1:T(4,128)S(1)}, f32[8,4]{0,1:T(4,128)}, u32[]{:S(2)}) copy-start(f32[8,4]{0,1:T(4,128)} %param.35) | copy-start | bytes 388
  54.4 21.6 %copy-start = (bf16[8,128,512]{2,1,0:T(8,128)(2,1)S(1)}, bf16[8,128,512]{2,1,0:T(8,128)(2,1)}, u32[]{:S(2)}) copy-start(bf16[8,128,512]{2,1,0:T(8,128)(2,1)} %param.18) | copy-start | bytes 3145732
  54.5 21.6 %copy-start.2 = (bf16[8,64,128]{2,1,0:T(8,128)(2,1)S(1)}, bf16[8,64,128]{2,1,0:T(8,128)(2,1)}, u32[]{:S(2)}) copy-start(bf16[8,64,128]{2,1,0:T(8,128)(2,1)} %rope.3) | copy-start | bytes 393220
  54.5 21.6 %copy-start.6 = (s32[4,2]{0,1:T(2,128)S(1)}, s32[4,2]{0,1:T(2,128)}, u32[]{:S(2)}) copy-start(s32[4,2]{0,1:T(2,128)} %param.20) | copy-start | bytes 100
  54.5 21.6 %copy-start.7 = (s32[64]{0:T(128)S(1)}, s32[64]{0:T(128)}, u32[]{:S(2)}) copy-start(s32[64]{0:T(128)} %lengths.3) | copy-start | bytes 772
  54.5 1.3 %collective-permute-start.4 = (bf16[16,2176]{1,0:T(8,128)(2,1)S(1)}, bf16[16,2176]{1,0:T(8,128)(2,1)S(1)}, u32[]{:S(2)}, u32[]{:S(2)}) collective-permute-start(bf16[16,2176]{1,0:T(8,128)(2,1)S(1)} %get-tuple-element.20), channel_id=1, source_target_pairs={{0,1},{1,0},{2,3},{3,2},{4,5},{5,4},{6,7},{7,6},{8,9},{9,8},{10,11... | collective-permute-start | bytes 208904 | tf_op jit(solution)/shard_map/ppermute | solution.py:567
  56.0 5.8 %collective-permute-start.7 = (bf16[16,2176]{1,0:T(8,128)(2,1)S(1)}, bf16[16,2176]{1,0:T(8,128)(2,1)S(1)}, u32[]{:S(2)}, u32[]{:S(2)}) collective-permute-start(bf16[16,2176]{1,0:T(8,128)(2,1)S(1)} %pair_sum.1.a), channel_id=1, source_target_pairs={{0,4},{1,5},{2,6},{3,7},{4,0},{5,1},{6,2},{7,3},{8,12},{9,13},{10,... | collective-permute-start | bytes 208904 | tf_op jit(solution)/shard_map/ppermute | solution.py:572
  59.2 4.5 %collective-permute-start.6 = (bf16[16,2176]{1,0:T(8,128)(2,1)S(1)}, bf16[16,2176]{1,0:T(8,128)(2,1)S(1)}, u32[]{:S(2)}, u32[]{:S(2)}) collective-permute-start(bf16[16,2176]{1,0:T(8,128)(2,1)S(1)} %pair_sum.1.a), channel_id=1, source_target_pairs={{0,6},{1,7},{2,0},{3,1},{4,2},{5,3},{6,4},{7,5},{8,14},{9,15},{10,... | collective-permute-start | bytes 208904 | tf_op jit(solution)/shard_map/ppermute | solution.py:572
  60.2 5.5 %collective-permute-start.5 = (bf16[16,2176]{1,0:T(8,128)(2,1)S(1)}, bf16[16,2176]{1,0:T(8,128)(2,1)S(1)}, u32[]{:S(2)}, u32[]{:S(2)}) collective-permute-start(bf16[16,2176]{1,0:T(8,128)(2,1)S(1)} %pair_sum.1.a), channel_id=1, source_target_pairs={{0,2},{1,3},{2,4},{3,5},{4,6},{5,7},{6,0},{7,1},{8,10},{9,11},{10,... | collective-permute-start | bytes 208904 | tf_op jit(solution)/shard_map/ppermute | solution.py:572
  65.9 1.3 %collective-permute-start.8 = (bf16[16,1024]{1,0:T(8,128)(2,1)S(1)}, bf16[16,1024]{1,0:T(8,128)(2,1)S(1)}, u32[]{:S(2)}, u32[]{:S(2)}) collective-permute-start(bf16[16,1024]{1,0:T(8,128)(2,1)S(1)} %activate.1.mine), channel_id=1, source_target_pairs={{0,1},{1,0},{2,3},{3,2},{4,5},{5,4},{6,7},{7,6},{8,9},{9,8},{10,11... | collective-permute-start | bytes 98312 | tf_op jit(solution)/shard_map/ppermute | solution.py:567
  68.6 14.8 %all-to-all-start.3 = ((bf16[16,2,896]{2,1,0:T(2,128)(2,1)}), bf16[16,2,896]{2,1,0:T(2,128)(2,1)S(1)}, u32[]{:S(2)}, u32[]{:S(2)}) async-start(bf16[16,2,896]{2,1,0:T(2,128)(2,1)} %down.1), calls=%async_computation.3 | async-start | bytes 114688 | tf_op jit(solution)/shard_map/all_to_all | solution.py:577

commit v3 on v2

--- a/solution.py
+++ b/solution.py
@@ -40,6 +40,9 @@
 EXPAND_COLS = 512
 SCALE = (HEAD_V + ROPE) ** -0.5
 
+ROTATED = [(i + GROUPS // 2) % GROUPS for i in range(GROUPS)]
+REVERSED = [GROUPS - 1 - i for i in range(GROUPS)]
+
 VM = pl.BlockSpec(memory_space=pltpu.VMEM)
 SM = pl.BlockSpec(memory_space=pltpu.SMEM)
 ANY = pl.BlockSpec(memory_space=pl.ANY)
@@ -107,52 +110,29 @@
     return summed, highest, normalizer
 
 
-def attend_kernel(
-    table,
-    lengths,
-    routes,
-    q_latent,
-    q_rope,
-    fresh_latent,
-    fresh_rope,
-    rope,
-    latent_hbm,
-    w_uv_hbm,
-    packed,
-    pieces,
-    latent,
-    w_uv,
-    tail,
-    wide,
-    narrow,
-    sems,
-    head_sems,
-    out_sems,
-):
-    group, lane = lax.axis_index("group"), lax.axis_index("lane")
-    loads, pages = [], []
+def spread_kernel(table, routes, rope_hbm, latent_hbm, pieces, table_out, rope, latent, tail, rope_sem, sems, out_sems):
+    rope_load = pltpu.make_async_copy(rope_hbm, rope, rope_sem)
+    rope_load.start()
+    loads = []
     for s in range(SEQ_G):
         for p in range(PSL):
             at = s * PSL + p
             loads.append(pltpu.make_async_copy(latent_hbm.at[table[p, s]], latent.at[at], sems.at[at]))
             loads[-1].start()
-    heads_per = HEADS // WEIGHT_CUTS
-    weights_in = []
-    for i in range(WEIGHT_CUTS):
-        part = pl.ds(i * heads_per, heads_per)
-        weights_in.append(pltpu.make_async_copy(w_uv_hbm.at[part], w_uv.at[part], head_sems.at[i]))
-        weights_in[-1].start()
+            table_out[p, s] = table[p, s]
     column = iota((NEW_G, LAT), 1)
     named = jnp.zeros((NEW_G, LAT), F32)
     for j in range(TOP):
         named = jnp.where(column == j, to_column(routes[j : j + 1, :].astype(F32)), named)
     named = jnp.broadcast_to(named[None], (CHUNKS, NEW_G, LAT))
+    rope_load.wait()
     for p in range(PSL):
         turned = [rope[table[p, s]].astype(F32).reshape(CHUNKS, 8, PAGE) for s in range(SEQ_G)]
         turned = jnp.concatenate(turned, axis=2)
         tail[p * CHUNKS : (p + 1) * CHUNKS] = jnp.concatenate([turned, named], axis=1).astype(BF16)
-    stores = [pltpu.make_async_copy(tail, pieces.at[:, pl.ds(SEQ_G * 16, 16), :], out_sems.at[SEQ_G * PSL])]
-    stores[0].start()
+    stores = []
+    stores.append(pltpu.make_async_copy(tail, pieces.at[:, pl.ds(SEQ_G * 16, 16), :], out_sems.at[SEQ_G * PSL]))
+    stores[-1].start()
     for s in range(SEQ_G):
         for p in range(PSL):
             at = s * PSL + p
@@ -165,13 +145,47 @@
                 )
             )
             stores[-1].start()
+    for store in stores:
+        store.wait()
+
+
+def spread(table, routes, rope, latent):
+    return call(
+        spread_kernel,
+        (pltpu.HBM((GROUPS, PIECE_ROWS, LAT), BF16), shape((PSL, SEQ_G), I32)),
+        [SM, VM, ANY, ANY],
+        (ANY, SM),
+        [
+            pltpu.VMEM((SEQ_G * PSL, ROPE, PAGE), BF16),
+            pltpu.VMEM((SEQ_G * PSL, CHUNKS, 16, LAT), BF16),
+            pltpu.VMEM((GROUPS, 16, LAT), BF16),
+            pltpu.SemaphoreType.DMA,
+            pltpu.SemaphoreType.DMA((SEQ_G * PSL,)),
+            pltpu.SemaphoreType.DMA((SEQ_G * PSL + 1,)),
+        ],
+        8,
+        "spread",
+        moved=16 * MIB,
+    )(*[in_hbm(x) for x in (table, routes, rope, latent)])
+
+
+def attend_kernel(
+    table, lengths, q_latent, q_rope, fresh_latent, fresh_rope, latent, rope, w_uv_hbm, packed, w_uv, wide, narrow, sems
+):
+    group, lane = lax.axis_index("group"), lax.axis_index("lane")
+    heads_per = HEADS // WEIGHT_CUTS
+    weights_in = []
+    for i in range(WEIGHT_CUTS):
+        part = pl.ds(i * heads_per, heads_per)
+        weights_in.append(pltpu.make_async_copy(w_uv_hbm.at[part], w_uv.at[part], sems.at[i]))
+        weights_in[-1].start()
     tops, norms = [], []
     for s in range(SEQ_G):
         length = lengths[group * SEQ_G + s]
         query, turned = q_latent[s], q_rope[s]
         pages, shown, scores = [], [], []
         for p in range(PSL):
-            tokens = latent[s * PSL + p].reshape(PAGE, LAT)
+            tokens = latent[table[p, s]]
             score = lax.dot_general(query, tokens, (((1,), (1,)), ((), ())), preferred_element_type=F32)
             score = score + jnp.dot(turned, rope[table[p, s]], preferred_element_type=F32)
             visible = (p * LANES + lane) < length
@@ -199,30 +213,24 @@
         row = jnp.concatenate([wide[c, rows, :] for c in range(LAT // 128)], axis=1).astype(BF16)
         narrow[rows, :] = jnp.dot(row, w_uv[h], preferred_element_type=F32)
     packed[...] = pack_rows(narrow[...], jnp.concatenate(tops, axis=0), jnp.concatenate(norms, axis=0))
-    for store in stores:
-        store.wait()
-
-
-def attend(table, lengths, routes, q_latent, q_rope, fresh_latent, fresh_rope, rope, latent, w_uv):
+
+
+def attend(table, lengths, q_latent, q_rope, fresh_latent, fresh_rope, latent, rope, w_uv):
     return call(
         attend_kernel,
-        (shape((SEQ_G * HEADS, 256), BF16), pltpu.HBM((GROUPS, PIECE_ROWS, LAT), BF16)),
-        [SM, SM] + [VM] * 6 + [ANY, ANY],
-        (VM, ANY),
+        shape((SEQ_G * HEADS, 256), BF16),
+        [SM, SM] + [VM] * 6 + [ANY],
+        VM,
         [
-            pltpu.VMEM((SEQ_G * PSL, CHUNKS, 16, LAT), BF16),
             pltpu.VMEM((HEADS, LAT, HEAD_V), BF16),
-            pltpu.VMEM((GROUPS, 16, LAT), BF16),
             pltpu.VMEM((LAT // 128, SEQ_G * HEADS, 128), F32),
             pltpu.VMEM((SEQ_G * HEADS, 128), F32),
-            pltpu.SemaphoreType.DMA((SEQ_G * PSL,)),
             pltpu.SemaphoreType.DMA((WEIGHT_CUTS,)),
-            pltpu.SemaphoreType.DMA((SEQ_G * PSL + 1,)),
         ],
-        16,
+        12,
         "attend",
         moved=8 * MIB,
-    )(*[in_hbm(x) for x in (table, lengths, routes, q_latent, q_rope, fresh_latent, fresh_rope, rope, latent, w_uv)])
+    )(table, lengths, q_latent, q_rope, fresh_latent, fresh_rope, latent, rope, in_hbm(w_uv))
 
 
 def join_kernel(first, second, packed):
@@ -233,22 +241,36 @@
     return call(join_kernel, shape(first.shape, BF16), [VM, VM], VM, [], 4, "join_pair", moved=4 * MIB)(first, second)
 
 
-def hidden_kernel(a, b, c, d, residual, w_out_hbm, copies, w_out, heads, sems):
-    depth = HEADS * HEAD_V // HIDDEN_CUTS
+def preload_kernel(weights, after, held, sems):
+    depth = weights.shape[0] // HIDDEN_CUTS
     loads = []
     for i in range(HIDDEN_CUTS):
         part = pl.ds(i * depth, depth)
-        loads.append(pltpu.make_async_copy(w_out_hbm.at[part, :], w_out.at[part, :], sems.at[i]))
+        loads.append(pltpu.make_async_copy(weights.at[part, :], held.at[part, :], sems.at[i]))
         loads[-1].start()
+    for load in loads:
+        load.wait()
+
+
+def preload(weights, after):
+    return call(
+        preload_kernel,
+        pltpu.VMEM(weights.shape, weights.dtype),
+        [ANY, ANY],
+        VM,
+        [pltpu.SemaphoreType.DMA((HIDDEN_CUTS,))],
+        4,
+        "preload",
+        moved=8 * MIB,
+    )(in_hbm(weights), after)
+
+
+def hidden_kernel(a, b, c, d, residual, w_out, copies, heads):
     summed, _, normalizer = join_rows([unpack_rows(x[...]) for x in (a, b, c, d)])
     heads[...] = summed / normalizer
-    hidden = residual[...].astype(F32)
-    per = HEADS // HIDDEN_CUTS
-    for i in range(HIDDEN_CUTS):
-        rows = [heads[pl.ds(h, SEQ_G, stride=HEADS), :] for h in range(i * per, (i + 1) * per)]
-        flat = jnp.concatenate(rows, axis=1).astype(BF16)
-        loads[i].wait()
-        hidden = hidden + jnp.dot(flat, w_out[i * depth : (i + 1) * depth, :], preferred_element_type=F32)
+    rows = [heads[pl.ds(h, SEQ_G, stride=HEADS), :] for h in range(HEADS)]
+    flat = jnp.concatenate(rows, axis=1).astype(BF16)
+    hidden = residual[...].astype(F32) + jnp.dot(flat, w_out[...], preferred_element_type=F32)
     hidden = hidden.astype(BF16)
     for g in range(GROUPS):
         copies[g] = hidden
@@ -258,17 +280,13 @@
     return call(
         hidden_kernel,
         pltpu.HBM((GROUPS, SEQ_G, WIDTH), BF16),
-        [VM] * 5 + [ANY],
+        [VM] * 6,
         VM,
-        [
-            pltpu.VMEM((HEADS * HEAD_V, WIDTH), BF16),
-            pltpu.VMEM((SEQ_G * HEADS, HEAD_V), F32),
-            pltpu.SemaphoreType.DMA((HIDDEN_CUTS,)),
-        ],
-        16,
+        [pltpu.VMEM((SEQ_G * HEADS, HEAD_V), F32)],
+        8,
         "hidden",
         moved=8 * MIB,
-    )(*parts, residual, in_hbm(w_out))
+    )(*parts, residual, w_out)
 
 
 def to_column(row):
@@ -291,8 +309,7 @@
     return slot, leaves
 
 
-def route_kernel(destiny, destiny_row, pieces, sent, choose, source, count, out, sem):
-    expert = lax.axis_index("group")
+def route_kernel(destiny, pieces, sent, named, source, count, sem):
     for i in range(GROUPS):
         count[i] = 0
     for i in range(SEQS):
@@ -307,18 +324,136 @@
             count[keeper] = rank + 1
             source[keeper * SEQ_G + rank] = q
             rows = pl.ds(pl.multiple_of(rank * 16, 16), 16)
-            out[keeper, rows, :] = pieces[g, s * 16 : (s + 1) * 16, :]
             cols = pl.ds(pl.multiple_of(rank * 128, 128), 128)
-            out[keeper, SEQ_G * 16 :, cols] = pieces[g, SEQ_G * 16 :, s * 128 : (s + 1) * 128]
-
-    copies = []
-    for i in range(4):
-        part = pl.ds(i * (GROUPS // 4), GROUPS // 4)
-        copies.append(pltpu.make_async_copy(out.at[part], sent.at[part], sem.at[i]))
-        copies[-1].start()
-    slot, leaves = slots_of(destiny_row[...].astype(F32))
+            last = pl.ds(SEQ_G * 16, 16)
+            pltpu.make_async_copy(
+                pieces.at[ROTATED[g], pl.ds(s * 16, 16), :], sent.at[keeper, rows, :], sem
+            ).start()
+            pltpu.make_async_copy(
+                pieces.at[ROTATED[g], last, pl.ds(s * 128, 128)], sent.at[keeper, last, cols], sem
+            ).start()
+
+    for g in range(GROUPS):
+        named[g] = pieces[ROTATED[g], SEQ_G * 16 :, 0:128]
+    half = pl.ds(0, GROUPS // 2)
+    pltpu.make_async_copy(pieces.at[half], sent.at[half], sem).wait()
+
+
+def route(destiny, pieces):
+    return call(
+        route_kernel,
+        (pltpu.HBM((GROUPS, PIECE_ROWS, LAT), BF16), shape((GROUPS, 16, 128), BF16), shape((SEQS,), I32)),
+        [SM, VM],
+        (ANY, VM, SM),
+        [pltpu.SMEM((GROUPS,), I32), pltpu.SemaphoreType.DMA],
+        8,
+        "route",
+        moved=8 * MIB,
+    )(destiny, pieces)
+
+
+def place_pages(pages, kept, kept_rope, zeros, sems, first):
+    zeros[...] = jnp.zeros_like(zeros)
+    waits = []
+    for i, (taken, turned, visible) in enumerate(pages):
+        copy = pltpu.make_async_copy(taken, kept.at[first + i], sems.at[i])
+        blank = pltpu.make_async_copy(zeros, kept.at[first + i], sems.at[i])
+        pl.when(visible)(copy.start)
+        pl.when(jnp.logical_not(visible))(blank.start)
+        waits.append(blank)
+        kept_rope[i] = jnp.where(visible, turned, 0.0).astype(BF16)
+    return waits
+
+
+def keep_own_kernel(
+    destiny, lengths, table, latent, rope, after, kept, kept_rope, token, zeros, rope_out, sems, rope_sem
+):
+    group, lane = lax.axis_index("group"), lax.axis_index("lane")
+    stays = destiny[group * SEQ_G] == group
+    pages = []
+    for s in range(SEQ_G):
+        for p in range(PSL):
+            page = table[p, s]
+            visible = stays & ((p * LANES + lane) < lengths[group * SEQ_G + s])
+            pages.append((latent.at[page], rope[page].astype(F32), visible))
+    waits = place_pages(pages, kept, rope_out, zeros, sems, 0)
+    turned = pltpu.make_async_copy(rope_out, kept_rope.at[pl.ds(0, SEQ_G * PSL)], rope_sem)
+    turned.start()
+    token[...] = jnp.zeros_like(token)
+    for wait in [*waits, turned]:
+        wait.wait()
+
+
+def keep_moved_kernel(
+    destiny, lengths, source, pieces, kept_in, kept_rope_in, kept, kept_rope, zeros, rope_out, sems, rope_sem
+):
+    group, lane = lax.axis_index("group"), lax.axis_index("lane")
+    stays = destiny[group * SEQ_G] == group
+    pages = []
+    for r in range(SEQ_G):
+        seq = source[group * SEQ_G + r]
+        for p in range(PSL):
+            at = ROTATED[p * CHUNKS]
+            turned = pieces[at : at + CHUNKS, SEQ_G * 16 :, r * 128 : (r + 1) * 128].astype(F32)[:, :8, :]
+            taken = pieces.at[pl.ds(at, CHUNKS), pl.ds(r * 16, 16), :]
+            pages.append((taken, turned.reshape(ROPE, PAGE), stays & ((p * LANES + lane) < lengths[seq])))
+    first = SEQ_G * PSL
+    waits = place_pages(pages, kept, rope_out, zeros, sems, first)
+    turned = pltpu.make_async_copy(rope_out, kept_rope.at[pl.ds(first, first)], rope_sem)
+    turned.start()
+    for wait in [*waits, turned]:
+        wait.wait()
+
+
+KEPT = (
+    shape((NEW_G * PSL, CHUNKS, 16, LAT), BF16),
+    shape((NEW_G * PSL, ROPE, PAGE), BF16),
+)
+KEEP_SCRATCH = [
+    pltpu.VMEM((CHUNKS, 16, LAT), BF16),
+    pltpu.VMEM((SEQ_G * PSL, ROPE, PAGE), BF16),
+    pltpu.SemaphoreType.DMA((SEQ_G * PSL,)),
+    pltpu.SemaphoreType.DMA,
+]
+
+
+def keep_own(destiny, lengths, table, latent, rope, after):
+    return call(
+        keep_own_kernel,
+        (*KEPT, shape((8, 128), F32)),
+        [SM, SM, SM, VM, VM, ANY],
+        (ANY, ANY, VM),
+        KEEP_SCRATCH,
+        4,
+        "keep_own",
+        moved=6 * MIB,
+    )(destiny, lengths, table, latent, rope, after)
+
+
+def keep_moved(destiny, lengths, source, pieces, kept, kept_rope):
+    return pl.pallas_call(
+        keep_moved_kernel,
+        out_shape=KEPT,
+        in_specs=[SM, SM, SM, VM, ANY, ANY],
+        out_specs=(ANY, ANY),
+        scratch_shapes=KEEP_SCRATCH,
+        input_output_aliases={4: 0, 5: 1},
+        compiler_params=pltpu.CompilerParams(vmem_limit_bytes=4 * MIB),
+        cost_estimate=pl.CostEstimate(flops=0, bytes_accessed=6 * MIB, transcendentals=0),
+        name="keep_moved",
+    )(destiny, lengths, source, pieces, kept, kept_rope)
+
+
+def gather_hidden(hidden, rows):
+    for g in range(GROUPS):
+        rows[g * SEQ_G : (g + 1) * SEQ_G, :] = hidden[GROUPS - 1 - g].astype(F32)
+    return rows[...].astype(BF16)
+
+
+def chosen(expert, destiny_row, named_rows):
+    slot, leaves = slots_of(destiny_row.astype(F32))
     new_group = jnp.floor(slot * (1.0 / NEW_G))
-    named = pieces[:, SEQ_G * 16 :, 0:128].astype(F32)[:, 8:, :].reshape(SLOTS, 128)
+    named = named_rows[...].astype(F32)[:, 8:, :].reshape(SLOTS, 128)
     lane = iota((SLOTS, 128), 1)
     hit = jnp.where((lane < TOP) & (named == expert.astype(F32)), 1.0, 0.0)
     hit = jnp.sum(hit, axis=1, keepdims=True)
@@ -334,74 +469,10 @@
         jnp.where(first & ((other // SEQ_G).astype(F32) < new_group), stays_col, 0.0), axis=0, keepdims=True
     )
     row = iota((ROWS, SEQS), 0).astype(F32)
-    choose[...] = jnp.where((row == keeper_rank * CAP + before) & (mine > 0.5), 1.0, 0.0).astype(BF16)
-    for copy in copies:
-        copy.wait()
-
-
-def route(destiny, destiny_row, pieces):
-    return call(
-        route_kernel,
-        (pltpu.HBM((GROUPS, PIECE_ROWS, LAT), BF16), shape((ROWS, SEQS), BF16), shape((SEQS,), I32)),
-        [SM, VM, VM],
-        (ANY, VM, SM),
-        [pltpu.SMEM((GROUPS,), I32), pltpu.VMEM((GROUPS, PIECE_ROWS, LAT), BF16), pltpu.SemaphoreType.DMA((4,))],
-        8,
-        "route",
-        moved=8 * MIB,
-    )(destiny, destiny_row, pieces)
-
-
-def keep_kernel(destiny, lengths, table, source, latent, rope, pieces, tails, kept, kept_rope, zeros, sems):
-    group, lane = lax.axis_index("group"), lax.axis_index("lane")
-    stays = destiny[group * SEQ_G] == group
-    zeros[...] = jnp.zeros_like(zeros)
-    waits = []
-    for i in range(NEW_G * PSL):
-        s, p = i // PSL, i % PSL
-        if s < SEQ_G:
-            seq = group * SEQ_G + s
-            taken = latent.at[table[p, s]]
-        else:
-            seq = source[group * SEQ_G + s - SEQ_G]
-            taken = pieces.at[pl.ds(p * CHUNKS, CHUNKS), pl.ds((s - SEQ_G) * 16, 16), :]
-        visible = stays & ((p * LANES + lane) < lengths[seq])
-        copy = pltpu.make_async_copy(taken, kept.at[i], sems.at[i])
-        blank = pltpu.make_async_copy(zeros, kept.at[i], sems.at[i])
-        pl.when(visible)(copy.start)
-        pl.when(jnp.logical_not(visible))(blank.start)
-        waits.append(blank)
-        if s < SEQ_G:
-            page = rope[table[p, s]].astype(F32)
-        else:
-            c = s - SEQ_G
-            page = tails[p * CHUNKS : (p + 1) * CHUNKS, SEQ_G * 16 :, c * 128 : (c + 1) * 128].astype(F32)
-            page = page[:, :8, :].reshape(ROPE, PAGE)
-        kept_rope[i] = jnp.where(visible, page, 0.0).astype(BF16)
-    for wait in waits:
-        wait.wait()
-
-
-def keep(destiny, lengths, table, source, latent, rope, pieces):
-    return call(
-        keep_kernel,
-        (shape((NEW_G * PSL, CHUNKS, 16, LAT), BF16), shape((NEW_G * PSL, ROPE, PAGE), BF16)),
-        [SM, SM, SM, SM, ANY, VM, ANY, VM],
-        (ANY, VM),
-        [pltpu.VMEM((CHUNKS, 16, LAT), BF16), pltpu.SemaphoreType.DMA((NEW_G * PSL,))],
-        6,
-        "keep",
-        moved=8 * MIB,
-    )(destiny, lengths, table, source, latent, rope, pieces, pieces)
-
-
-def gather_hidden(hidden, rows):
-    for g in range(GROUPS):
-        rows[g * SEQ_G : (g + 1) * SEQ_G, :] = hidden[g].astype(F32)
-    return rows[...].astype(BF16)
-
-
-def expand_kernel(hidden, choose, gain, w_gate, w_up, keep_half, send_half, rows, held, sems):
+    return jnp.where((row == keeper_rank * CAP + before) & (mine > 0.5), 1.0, 0.0).astype(BF16)
+
+
+def expand_kernel(hidden, named, destiny_row, gain, w_gate, w_up, keep_half, send_half, rows, held, sems):
     core = lax.rem(lax.axis_index("lane"), 2)
     loads = []
     for half in range(2):
@@ -412,7 +483,8 @@
                 at = len(loads)
                 loads.append(pltpu.make_async_copy(weights.at[0, :, cols], held.at[at], sems.at[at]))
                 loads[-1].start()
-    taken = jnp.dot(choose[...], gather_hidden(hidden, rows), preferred_element_type=F32)
+    choose = chosen(lax.axis_index("group"), destiny_row[...], named)
+    taken = jnp.dot(choose, gather_hidden(hidden, rows), preferred_element_type=F32)
     squares = jnp.sum(taken * taken, axis=1, keepdims=True)
     scaled = (taken * gain[...].astype(F32)).astype(BF16)
     lane = iota((ROWS, 128), 1)
@@ -430,12 +502,12 @@
             keep_half[:, cols] = made
 
 
-def expand(hidden, choose, gain, w_gate, w_up):
+def expand(hidden, named, destiny_row, gain, w_gate, w_up):
     cuts = 2 * FF // EXPAND_COLS
     return call(
         expand_kernel,
         (shape((ROWS, FF + 128), F32), shape((ROWS, FF + 128), BF16)),
-        [VM] * 3 + [ANY] * 2,
+        [VM] * 4 + [ANY] * 2,
         (VM, VM),
         [
             pltpu.VMEM((SEQS, WIDTH), F32),
@@ -445,7 +517,7 @@
         16,
         "expand",
         moved=8 * MIB,
-    )(hidden, choose, gain, in_hbm(w_gate), in_hbm(w_up))
+    )(hidden, named, destiny_row, gain, in_hbm(w_gate), in_hbm(w_up))
 
 
 def pair_kernel(kept, arrived, out):
@@ -460,7 +532,7 @@
     return call(pair_kernel, shape((ROWS, FF + 128), BF16), [VM, VM], VM, [], 4, "pair_sum", moved=4 * MIB)(kept, arrived)
 
 
-def activate_kernel(a, b, c, d, out):
+def activate_kernel(a, b, c, d, token, out):
     total = sum(x[...].astype(F32) for x in (a, b, c, d))
     squares = total[:, FF : FF + 1] + total[:, FF + 1 : FF + 2]
     factor = lax.rsqrt(squares / D + EPSILON)
@@ -469,8 +541,10 @@
     out[...] = (jax.nn.silu(gate) * up).astype(BF16)
 
 
-def activate(parts):
-    return call(activate_kernel, shape((ROWS, HALF), BF16), [VM] * 4, VM, [], 4, "activate", moved=4 * MIB)(*parts)
+def activate(parts, token):
+    return call(activate_kernel, shape((ROWS, HALF), BF16), [VM] * 4 + [ANY], VM, [], 4, "activate", moved=4 * MIB)(
+        *parts, token
+    )
 
 
 def down_kernel(mine, other, destiny_row, w_down, out, rows):
@@ -492,7 +566,7 @@
     matrix = jnp.where(iota((GROUPS * CAP, ROWS), 1).astype(F32) == wanted, present, 0.0).astype(BF16)
     rows[...] = jnp.dot(matrix, made, preferred_element_type=F32)
     for g in range(GROUPS):
-        out[g] = rows[g * CAP : (g + 1) * CAP, :].astype(BF16)
+        out[GROUPS - 1 - g] = rows[g * CAP : (g + 1) * CAP, :].astype(BF16)
 
 
 def down(mine, other, destiny_row, w_down):
@@ -542,7 +616,7 @@
 
 def finish_kernel(returned, own, combine, out, rows):
     for g in range(GROUPS):
-        rows[g * CAP : (g + 1) * CAP, :] = returned[g].astype(F32)
+        rows[g * CAP : (g + 1) * CAP, :] = returned[GROUPS - 1 - g].astype(F32)
     back = rows[...].astype(BF16)
     mixed = own[...]
     for term in split_terms(combine[...], 3):
@@ -569,12 +643,13 @@
 
 def around(value):
     return [value] + [
-        lax.ppermute(value, "lane", [(i, (i + 2 * step) % LANES) for i in range(LANES)]) for step in (1, 3, 2)
+        lax.ppermute(value, "lane", [(i, (i + 2 * step) % LANES) for i in range(LANES)]) for step in (2, 3, 1)
     ]
 
 
-def exchange(value):
-    return lax.all_to_all(value, "group", split_axis=0, concat_axis=0, tiled=True)
+def exchange(value, order=None):
+    lists = None if order is None else [order]
+    return lax.all_to_all(value, "group", split_axis=0, concat_axis=0, axis_index_groups=lists, tiled=True)
 
 
 def per_device(
@@ -602,27 +677,29 @@
     gain = norm_gain.reshape(1, WIDTH)
     page_table, routes, route_gates = page_table.T, routes.T, route_gates.T
 
-    packed, cut = attend(
-        page_table, seq_pages, routes, q_latent, q_rope, new_latent, new_rope, kv_rope, cut_latent, w_uv
-    )
-    scattered = exchange(cut)
+    cut, page_table = spread(page_table, routes, kv_rope, cut_latent)
+    scattered = exchange(cut, ROTATED)
+
+    packed = attend(page_table, seq_pages, q_latent, q_rope, new_latent, new_rope, kv_latent, kv_rope, w_uv)
     packed = join_pair(packed, swap_core(packed))
-    copies = hidden_rows(around(packed), residual_in, w_out)
-    hidden = exchange(copies)
-
-    forwarded, choose, source = route(destiny, destiny_row, scattered)
+    held = preload(w_out, packed)
+    copies = hidden_rows(around(packed), residual_in, held)
+    hidden = exchange(copies, REVERSED)
+
+    forwarded, named, source = route(destiny, scattered)
     gathered = exchange(forwarded)
 
-    keep_half, send_half = expand(hidden, choose, gain, w_gate, w_up)
+    keep_half, send_half = expand(hidden, named, destiny_row, gain, w_gate, w_up)
     total = pair_sum(keep_half, swap_core(send_half))
-    active = activate(around(total))
+    kept_latent, kept_rope, token = keep_own(destiny, seq_pages, page_table, cut_latent, kv_rope, total)
+    active = activate(around(total), token)
     made = down(active, swap_core(active), destiny_row, in_vmem(w_down))
     made, gathered = lax.optimization_barrier((made, gathered))
-    returned = exchange(made)
+    returned = exchange(made, REVERSED)
 
     own, combine = own_rows(hidden, destiny_row, routes, route_gates)
     layer_out = finish(returned, own, combine)
-    kept_latent, kept_rope = keep(destiny, seq_pages, page_table, source, cut_latent, kv_rope, gathered)
+    kept_latent, kept_rope = keep_moved(destiny, seq_pages, source, gathered, kept_latent, kept_rope)
     return layer_out, kept_latent.reshape(-1, PAGE, LAT), kept_rope
 
 

time: 84.6 us -> 80.1 us (0.947)
  waiting for transfers between devices: 27.1 us -> 12.8 us
  starting transfers between devices: 33.1 us -> 40 us
  Pallas kernels: 23 us -> 25.8 us
    all_to_all x4, waiting for transfers between devices: 14.4 us -> 4.89 us  [exchange(): lax.all_to_all(value, 'group', split_axis=0, concat_axis=0, axis_index_gr...]
    all_to_all x4, starting transfers between devices: 22.3 us -> 29.9 us  [exchange(): lax.all_to_all(value, 'group', split_axis=0, concat_axis=0, axis_index_gr...]
    ppermute x6, waiting for transfers between devices: 9.05 us -> 4.19 us  [around(): lax.ppermute(value, 'lane', [(i, (i + 2 * step) % LANES) for i in range(L...]
    pallas_call x5 -> x8, Pallas kernels: 16.5 us -> 19.2 us  [the longest x1 4.12 us: attend(): call(attend_kernel, shape((SEQ_G * HEADS, 256), BF16), [SM, SM] + [VM] *...]
  transfers between devices with their start and end apart: 13 -> 13, of which waited for: 12 -> 10; matrix products, arithmetic and copies ran while one was open for 0% -> 0% of each run, Pallas kernels for 19% -> 27%
where the time goes in v3:
time: 80.1 us; the launch traced here: 79.6 us
  starting transfers between devices  40 us (50%)
  Pallas kernels  25.8 us (32%)
  waiting for transfers between devices  12.8 us (16%)
  between operations  0.95 us (1%)
    all_to_all x4, starting transfers between devices, exchange(): lax.all_to_all(value, 'group', split_axis=0, concat_axis=0, axis_index_gr...  29.9 us
    ppermute x6, starting transfers between devices, around(): lax.ppermute(value, 'lane', [(i, (i + 2 * step) % LANES) for i in range(L...  9.91 us
    all_to_all x4, waiting for transfers between devices, exchange(): lax.all_to_all(value, 'group', split_axis=0, concat_axis=0, axis_index_gr...  4.89 us
    ppermute x6, waiting for transfers between devices, around(): lax.ppermute(value, 'lane', [(i, (i + 2 * step) % LANES) for i in range(L...  4.19 us
    pallas_call x1, Pallas kernels, attend(): call(attend_kernel, shape((SEQ_G * HEADS, 256), BF16), [SM, SM] + [VM] *...  4.12 us
    pallas_call x1, Pallas kernels, spread(): call(spread_kernel, (pltpu.HBM((GROUPS, PIECE_ROWS, LAT), BF16), shape((P...  3.89 us
    pallas_call x1, Pallas kernels, expand(): call(expand_kernel, (shape((ROWS, FF + 128), F32), shape((ROWS, FF + 128)...  3.75 us
    ppermute x3, waiting for transfers between devices, swap_core(): return lax.ppermute(value, 'lane', [(i, i ^ 1) for i in range(LANES)])  3.68 us
  transfers between devices with their start and end apart: 13, of which 10 were waited for; matrix products, arithmetic and copies ran while one was open for 0% of the time, Pallas kernels for 27%

profile of v3, /device:TPU:0, one launch (start us, length us, event | category | flops | bytes accessed | tf_op | source)
XLA Modules:
  0.0 79.6 jit_solution(6093123658392486072)
XLA Ops:
  0.7 3.9 %spread.1 = (bf16[16,80,512]{2,1,0:T(8,128)(2,1)}, s32[2,4]{1,0:T(2,128)S(1)}) custom-call(s32[2,4]{1,0:T(2,128)} %bitcast.15, s32[4,8]{1,0:T(4,128)} %bitcast.11, bf16[8,64,128]{2,1,0:T(8,128)(2,1)} %rope.3, bf16[8,8,16,512]{3,2,1,0:T(8,128)(2,1)} %bitcast.6), custom_call_target="tpu_custom_call" | custom-call | bytes 16777216 | tf_op jit(solution)/shard_map/spread/pallas_call | solution.py:153
  4.6 9.1 %all-to-all-start.1 = ((bf16[16,80,512]{2,1,0:T(8,128)(2,1)}), bf16[16,80,512]{2,1,0:T(8,128)(2,1)S(1)}, u32[]{:S(2)}, u32[]{:S(2)}) async-start(bf16[16,80,512]{2,1,0:T(8,128)(2,1)} %get-tuple-element.20), calls=%async_computation.1 | async-start | bytes 2621440 | tf_op jit(solution)/shard_map/all_to_all | solution.py:652
  13.7 4.1 %attend.1.first = bf16[128,256]{1,0:T(8,128)(2,1)S(1)} custom-call(s32[2,4]{1,0:T(2,128)S(1)} %get-tuple-element.19.table, s32[64]{0:T(128)S(1)} %copy-done.8, bf16[4,32,512]{2,1,0:T(8,128)(2,1)S(1)} %copy-done.3, bf16[4,32,64]{2,1,0:T(8,128)(2,1)S(1)} %copy-done.4, bf16[4,512]{1,0:T(4,128)(2,1)S(1)} %copy-done.9, bf16[4,64]{1,0:T(4,128)(2,1)S(1)} %copy-done.11, ...), custom_call_target="tpu_custom_call" | custom-call | bytes 8388608 | tf_op jit(solution)/shard_map/attend/pallas_call | solution.py:219
  18.0 1.2 %collective-permute-done.second = bf16[128,256]{1,0:T(8,128)(2,1)S(1)} collective-permute-done((bf16[128,256]{1,0:T(8,128)(2,1)S(1)}, bf16[128,256]{1,0:T(8,128)(2,1)S(1)}, u32[]{:S(2)}, u32[]{:S(2)}) %collective-permute-start) | collective-permute-done | bytes 65568 | tf_op jit(solution)/shard_map/ppermute | solution.py:641
  19.6 3.3 %collective-permute-start.1 = (bf16[128,256]{1,0:T(8,128)(2,1)S(1)}, bf16[128,256]{1,0:T(8,128)(2,1)S(1)}, u32[]{:S(2)}, u32[]{:S(2)}) collective-permute-start(bf16[128,256]{1,0:T(8,128)(2,1)S(1)} %join_pair.1.after.a), channel_id=1, source_target_pairs={{0,4},{1,5},{2,6},{3,7},{4,0},{5,1},{6,2},{7,3},{8,12},{9,13},{10,... | collective-permute-start | bytes 196616 | tf_op jit(solution)/shard_map/ppermute | solution.py:646
  22.8 1.1 %collective-permute-start.2 = (bf16[128,256]{1,0:T(8,128)(2,1)S(1)}, bf16[128,256]{1,0:T(8,128)(2,1)S(1)}, u32[]{:S(2)}, u32[]{:S(2)}) collective-permute-start(bf16[128,256]{1,0:T(8,128)(2,1)S(1)} %join_pair.1.after.a), channel_id=1, source_target_pairs={{0,6},{1,7},{2,0},{3,1},{4,2},{5,3},{6,4},{7,5},{8,14},{9,15},{10,... | collective-permute-start | bytes 196616 | tf_op jit(solution)/shard_map/ppermute | solution.py:646
  24.9 3.2 %preload.1.w_out = bf16[4096,896]{1,0:T(8,128)(2,1)S(1)} custom-call(bf16[4096,896]{1,0:T(8,128)(2,1)} %weights.1, bf16[128,256]{1,0:T(8,128)(2,1)S(1)} %join_pair.1.after.a), custom_call_target="tpu_custom_call" | custom-call | bytes 8388608 | tf_op jit(solution)/shard_map/preload/pallas_call | solution.py:256
  28.1 1.3 %collective-permute-done.3.d = bf16[128,256]{1,0:T(8,128)(2,1)S(1)} collective-permute-done((bf16[128,256]{1,0:T(8,128)(2,1)S(1)}, bf16[128,256]{1,0:T(8,128)(2,1)S(1)}, u32[]{:S(2)}, u32[]{:S(2)}) %collective-permute-start.3) | collective-permute-done | bytes 65568 | tf_op jit(solution)/shard_map/ppermute | solution.py:646
  29.4 2.1 %hidden.1 = bf16[16,4,896]{2,1,0:T(4,128)(2,1)} custom-call(bf16[128,256]{1,0:T(8,128)(2,1)S(1)} %join_pair.1.after.a, bf16[128,256]{1,0:T(8,128)(2,1)S(1)} %collective-permute-done.1.b, bf16[128,256]{1,0:T(8,128)(2,1)S(1)} %collective-permute-done.2.c, bf16[128,256]{1,0:T(8,128)(2,1)S(1)} %collective-permute-done.3.d, bf16[4,896]{1,0:T(4,128)(2,1)S(1)} %copy-done.7, ...), custom_call_target="tpu_custom_call" | custom-call | bytes 8388608 | tf_op jit(solution)/shard_map/hidden/pallas_call | solution.py:280
  31.9 7.3 %all-to-all-start = ((bf16[16,4,896]{2,1,0:T(4,128)(2,1)}), bf16[16,4,896]{2,1,0:T(4,128)(2,1)S(1)}, u32[]{:S(2)}, u32[]{:S(2)}) async-start(bf16[16,4,896]{2,1,0:T(4,128)(2,1)} %hidden.1), calls=%async_computation | async-start | bytes 229376 | tf_op jit(solution)/shard_map/all_to_all | solution.py:652
  39.2 2.4 %route.1 = (bf16[16,80,512]{2,1,0:T(8,128)(2,1)}, bf16[16,16,128]{2,1,0:T(8,128)(2,1)S(1)}, s32[64]{0:T(128)S(1)}) custom-call(s32[64]{0:T(128)S(1)} %copy-done.5, bf16[16,80,512]{2,1,0:T(8,128)(2,1)S(1)} %all-to-all-done.1.pieces), custom_call_target="tpu_custom_call" | custom-call | bytes 8388608 | tf_op jit(solution)/shard_map/route/pallas_call | solution.py:343
  41.6 1.8 %all-to-all-done.hidden = bf16[16,4,896]{2,1,0:T(4,128)(2,1)S(1)} async-done(((bf16[16,4,896]{2,1,0:T(4,128)(2,1)}), bf16[16,4,896]{2,1,0:T(4,128)(2,1)S(1)}, u32[]{:S(2)}, u32[]{:S(2)}) %all-to-all-start) | async-done | bytes 114720 | tf_op jit(solution)/shard_map/all_to_all | solution.py:652
  43.4 5.0 %all-to-all-start.2 = ((bf16[16,80,512]{2,1,0:T(8,128)(2,1)}), bf16[16,80,512]{2,1,0:T(8,128)(2,1)S(1)}, u32[]{:S(2)}, u32[]{:S(2)}) async-start(bf16[16,80,512]{2,1,0:T(8,128)(2,1)} %get-tuple-element.25), calls=%async_computation.2 | async-start | bytes 2621440 | tf_op jit(solution)/shard_map/all_to_all | solution.py:652
  48.5 3.8 %expand.1 = (f32[16,2176]{1,0:T(8,128)S(1)}, bf16[16,2176]{1,0:T(8,128)(2,1)S(1)}) custom-call(bf16[16,4,896]{2,1,0:T(4,128)(2,1)S(1)} %all-to-all-done.hidden, bf16[16,16,128]{2,1,0:T(8,128)(2,1)S(1)} %get-tuple-element.21.named, s32[1,64]{1,0:T(1,128)S(1)} %bitcast.8, bf16[1,896]{1,0:T(2,128)(2,1)S(1)} %reshape.20.gain, bf16[1,896,2048]{2,1,0:T(8,128)(2,1)} %w_gate.1, ...), custom_call_target="tpu_custom_call" | custom-call | bytes 8388608 | tf_op jit(solution)/shard_map/expand/pallas_call | solution.py:507
  52.4 1.2 %collective-permute-done.4.arrived = bf16[16,2176]{1,0:T(8,128)(2,1)S(1)} collective-permute-done((bf16[16,2176]{1,0:T(8,128)(2,1)S(1)}, bf16[16,2176]{1,0:T(8,128)(2,1)S(1)}, u32[]{:S(2)}, u32[]{:S(2)}) %collective-permute-start.4) | collective-permute-done | bytes 69664 | tf_op jit(solution)/shard_map/ppermute | solution.py:641
  53.8 2.6 %collective-permute-start.5 = (bf16[16,2176]{1,0:T(8,128)(2,1)S(1)}, bf16[16,2176]{1,0:T(8,128)(2,1)S(1)}, u32[]{:S(2)}, u32[]{:S(2)}) collective-permute-start(bf16[16,2176]{1,0:T(8,128)(2,1)S(1)} %pair_sum.1.after.a), channel_id=1, source_target_pairs={{0,4},{1,5},{2,6},{3,7},{4,0},{5,1},{6,2},{7,3},{8,12},{9,13},{10,... | collective-permute-start | bytes 208904 | tf_op jit(solution)/shard_map/ppermute | solution.py:646
  56.3 1.1 %collective-permute-start.6 = (bf16[16,2176]{1,0:T(8,128)(2,1)S(1)}, bf16[16,2176]{1,0:T(8,128)(2,1)S(1)}, u32[]{:S(2)}, u32[]{:S(2)}) collective-permute-start(bf16[16,2176]{1,0:T(8,128)(2,1)S(1)} %pair_sum.1.after.a), channel_id=1, source_target_pairs={{0,6},{1,7},{2,0},{3,1},{4,2},{5,3},{6,4},{7,5},{8,14},{9,15},{10,... | collective-permute-start | bytes 208904 | tf_op jit(solution)/shard_map/ppermute | solution.py:646
  58.4 1.6 %keep_own.1 = (bf16[16,8,16,512]{3,2,1,0:T(8,128)(2,1)}, bf16[16,64,128]{2,1,0:T(8,128)(2,1)}, f32[8,128]{1,0:T(8,128)S(1)}) custom-call(s32[64]{0:T(128)S(1)} %copy-done.5, s32[64]{0:T(128)S(1)} %copy-done.8, s32[2,4]{1,0:T(2,128)S(1)} %get-tuple-element.19.table, bf16[8,8,16,512]{3,2,1,0:T(8,128)(2,1)S(1)} %bitcast.7, bf16[8,64,128]{2,1,0:T(8,128)(2,1)S(1)} %copy-done.2, ...), custom_call_target="tpu_custom_call" | custom-call | bytes 6291456 | tf_op jit(solution)/shard_map/keep_own/pallas_call | solution.py:421
  60.8 2.1 %collective-permute-done.7.d = bf16[16,2176]{1,0:T(8,128)(2,1)S(1)} collective-permute-done((bf16[16,2176]{1,0:T(8,128)(2,1)S(1)}, bf16[16,2176]{1,0:T(8,128)(2,1)S(1)}, u32[]{:S(2)}, u32[]{:S(2)}) %collective-permute-start.7) | collective-permute-done | bytes 69664 | tf_op jit(solution)/shard_map/ppermute | solution.py:646
  63.2 1.2 %collective-permute-done.8.other = bf16[16,1024]{1,0:T(8,128)(2,1)S(1)} collective-permute-done((bf16[16,1024]{1,0:T(8,128)(2,1)S(1)}, bf16[16,1024]{1,0:T(8,128)(2,1)S(1)}, u32[]{:S(2)}, u32[]{:S(2)}) %collective-permute-start.8) | collective-permute-done | bytes 32800 | tf_op jit(solution)/shard_map/ppermute | solution.py:641
  64.4 1.4 %down.1 = bf16[16,2,896]{2,1,0:T(2,128)(2,1)} custom-call(bf16[16,1024]{1,0:T(8,128)(2,1)S(1)} %activate.1.mine, bf16[16,1024]{1,0:T(8,128)(2,1)S(1)} %collective-permute-done.8.other, s32[1,64]{1,0:T(1,128)S(1)} %bitcast.9, bf16[1,2048,896]{2,1,0:T(8,128)(2,1)S(1)} %copy-done.1), custom_call_target="tpu_custom_call" | custom-call | bytes 4194304 | tf_op jit(solution)/shard_map/down/pallas_call | solution.py:573
  66.2 8.5 %all-to-all-start.3 = ((bf16[16,2,896]{2,1,0:T(2,128)(2,1)}), bf16[16,2,896]{2,1,0:T(2,128)(2,1)S(1)}, u32[]{:S(2)}, u32[]{:S(2)}) async-start(bf16[16,2,896]{2,1,0:T(2,128)(2,1)} %down.1), calls=%async_computation.3 | async-start | bytes 114688 | tf_op jit(solution)/shard_map/all_to_all | solution.py:652
  74.9 1.7 %keep_moved.1 = (bf16[16,8,16,512]{3,2,1,0:T(8,128)(2,1)}, bf16[16,64,128]{2,1,0:T(8,128)(2,1)}) custom-call(s32[64]{0:T(128)S(1)} %copy-done.5, s32[64]{0:T(128)S(1)} %copy-done.8, s32[64]{0:T(128)S(1)} %get-tuple-element.29.source, bf16[16,80,512]{2,1,0:T(8,128)(2,1)S(1)} %all-to-all-done.2.pieces, ...), custom_call_target="tpu_custom_call", output_to_operand_aliasing={{0}: (4, {}), {1}: (5, {})} | custom-call | bytes 6291456 | tf_op jit(solution)/shard_map/keep_moved/pallas_call | solution.py:434
  76.6 2.3 %all-to-all-done.3.returned = bf16[16,2,896]{2,1,0:T(2,128)(2,1)S(1)} async-done(((bf16[16,2,896]{2,1,0:T(2,128)(2,1)}), bf16[16,2,896]{2,1,0:T(2,128)(2,1)S(1)}, u32[]{:S(2)}, u32[]{:S(2)}) %all-to-all-start.3) | async-done | bytes 57376 | tf_op jit(solution)/shard_map/all_to_all | solution.py:652
  (43 shorter events, 5.5 us)
Async XLA Ops:
  0.6 13.0 %copy-start = (bf16[8,128,512]{2,1,0:T(8,128)(2,1)S(1)}, bf16[8,128,512]{2,1,0:T(8,128)(2,1)}, u32[]{:S(2)}) copy-start(bf16[8,128,512]{2,1,0:T(8,128)(2,1)} %latent.1) | copy-start | bytes 3145732
  0.6 13.0 %copy-start.2 = (bf16[8,64,128]{2,1,0:T(8,128)(2,1)S(1)}, bf16[8,64,128]{2,1,0:T(8,128)(2,1)}, u32[]{:S(2)}) copy-start(bf16[8,64,128]{2,1,0:T(8,128)(2,1)} %rope.3) | copy-start | bytes 393220
  0.7 13.0 %copy-start.8 = (s32[64]{0:T(128)S(1)}, s32[64]{0:T(128)}, u32[]{:S(2)}) copy-start(s32[64]{0:T(128)} %lengths.5) | copy-start | bytes 772
  0.7 13.0 %copy-start.3 = (bf16[4,32,512]{2,1,0:T(8,128)(2,1)S(1)}, bf16[4,32,512]{2,1,0:T(8,128)(2,1)}, u32[]{:S(2)}) copy-start(bf16[4,32,512]{2,1,0:T(8,128)(2,1)} %q_latent.1) | copy-start | bytes 393220
  0.7 13.0 %copy-start.4 = (bf16[4,32,64]{2,1,0:T(8,128)(2,1)S(1)}, bf16[4,32,64]{2,1,0:T(8,128)(2,1)}, u32[]{:S(2)}) copy-start(bf16[4,32,64]{2,1,0:T(8,128)(2,1)} %q_rope.1) | copy-start | bytes 49156
  0.7 13.0 %copy-start.9 = (bf16[4,512]{1,0:T(4,128)(2,1)S(1)}, bf16[4,512]{1,0:T(4,128)(2,1)}, u32[]{:S(2)}) copy-start(bf16[4,512]{1,0:T(4,128)(2,1)} %fresh_latent.1) | copy-start | bytes 12292
  0.7 13.0 %copy-start.11 = (bf16[4,64]{1,0:T(4,128)(2,1)S(1)}, bf16[4,64]{1,0:T(4,128)(2,1)}, u32[]{:S(2)}) copy-start(bf16[4,64]{1,0:T(4,128)(2,1)} %fresh_rope.1) | copy-start | bytes 1540
  4.6 27.3 %all-to-all-start.1 = ((bf16[16,80,512]{2,1,0:T(8,128)(2,1)}), bf16[16,80,512]{2,1,0:T(8,128)(2,1)S(1)}, u32[]{:S(2)}, u32[]{:S(2)}) async-start(bf16[16,80,512]{2,1,0:T(8,128)(2,1)} %get-tuple-element.20), calls=%async_computation.1 | async-start | bytes 2621440 | tf_op jit(solution)/shard_map/all_to_all | solution.py:652
  17.9 1.3 %collective-permute-start = (bf16[128,256]{1,0:T(8,128)(2,1)S(1)}, bf16[128,256]{1,0:T(8,128)(2,1)S(1)}, u32[]{:S(2)}, u32[]{:S(2)}) collective-permute-start(bf16[128,256]{1,0:T(8,128)(2,1)S(1)} %attend.1.first), channel_id=1, source_target_pairs={{0,1},{1,0},{2,3},{3,2},{4,5},{5,4},{6,7},{7,6},{8,9},{9,8},{10,11... | collective-permute-start | bytes 196616 | tf_op jit(solution)/shard_map/ppermute | solution.py:641
  19.6 8.5 %collective-permute-start.1 = (bf16[128,256]{1,0:T(8,128)(2,1)S(1)}, bf16[128,256]{1,0:T(8,128)(2,1)S(1)}, u32[]{:S(2)}, u32[]{:S(2)}) collective-permute-start(bf16[128,256]{1,0:T(8,128)(2,1)S(1)} %join_pair.1.after.a), channel_id=1, source_target_pairs={{0,4},{1,5},{2,6},{3,7},{4,0},{5,1},{6,2},{7,3},{8,12},{9,13},{10,... | collective-permute-start | bytes 196616 | tf_op jit(solution)/shard_map/ppermute | solution.py:646
  22.8 5.2 %collective-permute-start.2 = (bf16[128,256]{1,0:T(8,128)(2,1)S(1)}, bf16[128,256]{1,0:T(8,128)(2,1)S(1)}, u32[]{:S(2)}, u32[]{:S(2)}) collective-permute-start(bf16[128,256]{1,0:T(8,128)(2,1)S(1)} %join_pair.1.after.a), channel_id=1, source_target_pairs={{0,6},{1,7},{2,0},{3,1},{4,2},{5,3},{6,4},{7,5},{8,14},{9,15},{10,... | collective-permute-start | bytes 196616 | tf_op jit(solution)/shard_map/ppermute | solution.py:646
  23.9 5.5 %collective-permute-start.3 = (bf16[128,256]{1,0:T(8,128)(2,1)S(1)}, bf16[128,256]{1,0:T(8,128)(2,1)S(1)}, u32[]{:S(2)}, u32[]{:S(2)}) collective-permute-start(bf16[128,256]{1,0:T(8,128)(2,1)S(1)} %join_pair.1.after.a), channel_id=1, source_target_pairs={{0,2},{1,3},{2,4},{3,5},{4,6},{5,7},{6,0},{7,1},{8,10},{9,11},{10,... | collective-permute-start | bytes 196616 | tf_op jit(solution)/shard_map/ppermute | solution.py:646
  31.5 17.0 %copy-start.12 = (bf16[896]{0:T(1024)(128)(2,1)S(1)}, bf16[896]{0:T(1024)(128)(2,1)}, u32[]{:S(2)}) copy-start(bf16[896]{0:T(1024)(128)(2,1)} %param.30) | copy-start | bytes 5380
  31.9 11.5 %all-to-all-start = ((bf16[16,4,896]{2,1,0:T(4,128)(2,1)}), bf16[16,4,896]{2,1,0:T(4,128)(2,1)S(1)}, u32[]{:S(2)}, u32[]{:S(2)}) async-start(bf16[16,4,896]{2,1,0:T(4,128)(2,1)} %hidden.1), calls=%async_computation | async-start | bytes 229376 | tf_op jit(solution)/shard_map/all_to_all | solution.py:652
  43.4 22.8 %all-to-all-start.2 = ((bf16[16,80,512]{2,1,0:T(8,128)(2,1)}), bf16[16,80,512]{2,1,0:T(8,128)(2,1)S(1)}, u32[]{:S(2)}, u32[]{:S(2)}) async-start(bf16[16,80,512]{2,1,0:T(8,128)(2,1)} %get-tuple-element.25), calls=%async_computation.2 | async-start | bytes 2621440 | tf_op jit(solution)/shard_map/all_to_all | solution.py:652
  48.5 15.9 %copy-start.1 = (bf16[1,2048,896]{2,1,0:T(8,128)(2,1)S(1)}, bf16[1,2048,896]{2,1,0:T(8,128)(2,1)}, u32[]{:S(2)}) copy-start(bf16[1,2048,896]{2,1,0:T(8,128)(2,1)} %w_down.1) | copy-start | bytes 11010052
  52.2 22.4 %copy-start.6 = (s32[8,4]{0,1:T(4,128)S(1)}, s32[8,4]{0,1:T(4,128)}, u32[]{:S(2)}) copy-start(s32[8,4]{0,1:T(4,128)} %param.34) | copy-start | bytes 388
  52.3 22.4 %copy-start.10 = (f32[8,4]{0,1:T(4,128)S(1)}, f32[8,4]{0,1:T(4,128)}, u32[]{:S(2)}) copy-start(f32[8,4]{0,1:T(4,128)} %param.35) | copy-start | bytes 388
  52.3 1.3 %collective-permute-start.4 = (bf16[16,2176]{1,0:T(8,128)(2,1)S(1)}, bf16[16,2176]{1,0:T(8,128)(2,1)S(1)}, u32[]{:S(2)}, u32[]{:S(2)}) collective-permute-start(bf16[16,2176]{1,0:T(8,128)(2,1)S(1)} %get-tuple-element.23), channel_id=1, source_target_pairs={{0,1},{1,0},{2,3},{3,2},{4,5},{5,4},{6,7},{7,6},{8,9},{9,8},{10,11... | collective-permute-start | bytes 208904 | tf_op jit(solution)/shard_map/ppermute | solution.py:641
  53.8 6.3 %collective-permute-start.5 = (bf16[16,2176]{1,0:T(8,128)(2,1)S(1)}, bf16[16,2176]{1,0:T(8,128)(2,1)S(1)}, u32[]{:S(2)}, u32[]{:S(2)}) collective-permute-start(bf16[16,2176]{1,0:T(8,128)(2,1)S(1)} %pair_sum.1.after.a), channel_id=1, source_target_pairs={{0,4},{1,5},{2,6},{3,7},{4,0},{5,1},{6,2},{7,3},{8,12},{9,13},{10,... | collective-permute-start | bytes 208904 | tf_op jit(solution)/shard_map/ppermute | solution.py:646
  56.3 4.5 %collective-permute-start.6 = (bf16[16,2176]{1,0:T(8,128)(2,1)S(1)}, bf16[16,2176]{1,0:T(8,128)(2,1)S(1)}, u32[]{:S(2)}, u32[]{:S(2)}) collective-permute-start(bf16[16,2176]{1,0:T(8,128)(2,1)S(1)} %pair_sum.1.after.a), channel_id=1, source_target_pairs={{0,6},{1,7},{2,0},{3,1},{4,2},{5,3},{6,4},{7,5},{8,14},{9,15},{10,... | collective-permute-start | bytes 208904 | tf_op jit(solution)/shard_map/ppermute | solution.py:646
  57.4 5.5 %collective-permute-start.7 = (bf16[16,2176]{1,0:T(8,128)(2,1)S(1)}, bf16[16,2176]{1,0:T(8,128)(2,1)S(1)}, u32[]{:S(2)}, u32[]{:S(2)}) collective-permute-start(bf16[16,2176]{1,0:T(8,128)(2,1)S(1)} %pair_sum.1.after.a), channel_id=1, source_target_pairs={{0,2},{1,3},{2,4},{3,5},{4,6},{5,7},{6,0},{7,1},{8,10},{9,11},{10,... | collective-permute-start | bytes 208904 | tf_op jit(solution)/shard_map/ppermute | solution.py:646
  63.1 1.3 %collective-permute-start.8 = (bf16[16,1024]{1,0:T(8,128)(2,1)S(1)}, bf16[16,1024]{1,0:T(8,128)(2,1)S(1)}, u32[]{:S(2)}, u32[]{:S(2)}) collective-permute-start(bf16[16,1024]{1,0:T(8,128)(2,1)S(1)} %activate.1.mine), channel_id=1, source_target_pairs={{0,1},{1,0},{2,3},{3,2},{4,5},{5,4},{6,7},{7,6},{8,9},{9,8},{10,11... | collective-permute-start | bytes 98312 | tf_op jit(solution)/shard_map/ppermute | solution.py:641
  66.2 12.7 %all-to-all-start.3 = ((bf16[16,2,896]{2,1,0:T(2,128)(2,1)}), bf16[16,2,896]{2,1,0:T(2,128)(2,1)S(1)}, u32[]{:S(2)}, u32[]{:S(2)}) async-start(bf16[16,2,896]{2,1,0:T(2,128)(2,1)} %down.1), calls=%async_computation.3 | async-start | bytes 114688 | tf_op jit(solution)/shard_map/all_to_all | solution.py:652
  (2 other events, 21.0 us)

commit v4 on v3

--- a/solution.py
+++ b/solution.py
@@ -110,41 +110,50 @@
     return summed, highest, normalizer
 
 
-def spread_kernel(table, routes, rope_hbm, latent_hbm, pieces, table_out, rope, latent, tail, rope_sem, sems, out_sems):
-    rope_load = pltpu.make_async_copy(rope_hbm, rope, rope_sem)
-    rope_load.start()
-    loads = []
+def spread_kernel(
+    table_hbm, routes_hbm, rope_hbm, latent_hbm, pieces, table_out, table, routes, rope, latent, tail, sems, out_sems
+):
+    loads = [
+        pltpu.make_async_copy(source, target, sems.at[i])
+        for i, (source, target) in enumerate(
+            [(table_hbm, table), (routes_hbm, routes), (rope_hbm, rope)]
+            + [(latent_hbm.at[pl.ds(2 * i, 2)], latent.at[pl.ds(2 * i, 2)]) for i in range(SEQ_G)]
+        )
+    ]
+    for load in loads:
+        load.start()
+    loads[0].wait()
     for s in range(SEQ_G):
         for p in range(PSL):
-            at = s * PSL + p
-            loads.append(pltpu.make_async_copy(latent_hbm.at[table[p, s]], latent.at[at], sems.at[at]))
-            loads[-1].start()
             table_out[p, s] = table[p, s]
+    for load in loads[3:]:
+        load.wait()
+    stores = []
+    for s in range(SEQ_G):
+        for p in range(PSL):
+            stores.append(
+                pltpu.make_async_copy(
+                    latent.at[table[p, s]],
+                    pieces.at[pl.ds(p * CHUNKS, CHUNKS), pl.ds(s * 16, 16), :],
+                    out_sems.at[s * PSL + p],
+                )
+            )
+            stores[-1].start()
+    loads[1].wait()
+    loads[2].wait()
     column = iota((NEW_G, LAT), 1)
     named = jnp.zeros((NEW_G, LAT), F32)
     for j in range(TOP):
         named = jnp.where(column == j, to_column(routes[j : j + 1, :].astype(F32)), named)
     named = jnp.broadcast_to(named[None], (CHUNKS, NEW_G, LAT))
-    rope_load.wait()
     for p in range(PSL):
         turned = [rope[table[p, s]].astype(F32).reshape(CHUNKS, 8, PAGE) for s in range(SEQ_G)]
         turned = jnp.concatenate(turned, axis=2)
         tail[p * CHUNKS : (p + 1) * CHUNKS] = jnp.concatenate([turned, named], axis=1).astype(BF16)
-    stores = []
-    stores.append(pltpu.make_async_copy(tail, pieces.at[:, pl.ds(SEQ_G * 16, 16), :], out_sems.at[SEQ_G * PSL]))
+    stores.append(
+        pltpu.make_async_copy(tail, pieces.at[:, pl.ds(SEQ_G * 16, 16), :], out_sems.at[SEQ_G * PSL])
+    )
     stores[-1].start()
-    for s in range(SEQ_G):
-        for p in range(PSL):
-            at = s * PSL + p
-            loads[at].wait()
-            stores.append(
-                pltpu.make_async_copy(
-                    latent.at[at],
-                    pieces.at[pl.ds(p * CHUNKS, CHUNKS), pl.ds(s * 16, 16), :],
-                    out_sems.at[at],
-                )
-            )
-            stores[-1].start()
     for store in stores:
         store.wait()
 
@@ -153,14 +162,15 @@
     return call(
         spread_kernel,
         (pltpu.HBM((GROUPS, PIECE_ROWS, LAT), BF16), shape((PSL, SEQ_G), I32)),
-        [SM, VM, ANY, ANY],
+        [ANY] * 4,
         (ANY, SM),
         [
+            pltpu.SMEM((PSL, SEQ_G), I32),
+            pltpu.VMEM((TOP, NEW_G), I32),
             pltpu.VMEM((SEQ_G * PSL, ROPE, PAGE), BF16),
             pltpu.VMEM((SEQ_G * PSL, CHUNKS, 16, LAT), BF16),
             pltpu.VMEM((GROUPS, 16, LAT), BF16),
-            pltpu.SemaphoreType.DMA,
-            pltpu.SemaphoreType.DMA((SEQ_G * PSL,)),
+            pltpu.SemaphoreType.DMA((3 + SEQ_G,)),
             pltpu.SemaphoreType.DMA((SEQ_G * PSL + 1,)),
         ],
         8,
@@ -472,41 +482,35 @@
     return jnp.where((row == keeper_rank * CAP + before) & (mine > 0.5), 1.0, 0.0).astype(BF16)
 
 
-def expand_kernel(hidden, named, destiny_row, gain, w_gate, w_up, keep_half, send_half, rows, held, sems):
-    core = lax.rem(lax.axis_index("lane"), 2)
+def expand_kernel(hidden, named, destiny_row, gain, w_gate, w_up, kept, sent, rows, held, sems):
     loads = []
-    for half in range(2):
-        first = (1 - core if half == 0 else core) * HALF
-        for weights in (w_gate, w_up):
-            for part in range(HALF // EXPAND_COLS):
-                cols = pl.ds(pl.multiple_of(first + part * EXPAND_COLS, EXPAND_COLS), EXPAND_COLS)
-                at = len(loads)
-                loads.append(pltpu.make_async_copy(weights.at[0, :, cols], held.at[at], sems.at[at]))
-                loads[-1].start()
+    for weights in (w_gate, w_up):
+        for part in range(FF // EXPAND_COLS):
+            cols = pl.ds(part * EXPAND_COLS, EXPAND_COLS)
+            at = len(loads)
+            loads.append(pltpu.make_async_copy(weights.at[0, :, cols], held.at[at], sems.at[at]))
+            loads[-1].start()
     choose = chosen(lax.axis_index("group"), destiny_row[...], named)
     taken = jnp.dot(choose, gather_hidden(hidden, rows), preferred_element_type=F32)
     squares = jnp.sum(taken * taken, axis=1, keepdims=True)
     scaled = (taken * gain[...].astype(F32)).astype(BF16)
     lane = iota((ROWS, 128), 1)
-    keep_half[:, FF:] = jnp.where(lane == 0, squares, 0.0)
+    kept[:, 2 * FF :] = jnp.where(lane == 0, squares, 0.0)
     high, low = split_terms(squares, 2)
-    send_half[:, FF:] = jnp.where(lane == 0, high, jnp.where(lane == 1, low, 0.0)).astype(BF16)
+    sent[:, 2 * FF :] = jnp.where(lane == 0, high, jnp.where(lane == 1, low, 0.0)).astype(BF16)
     for at, load in enumerate(loads):
         load.wait()
         made = jnp.dot(scaled, held[at], preferred_element_type=F32)
-        per_half = len(loads) // 2
-        cols = slice((at % per_half) * EXPAND_COLS, (at % per_half + 1) * EXPAND_COLS)
-        if at < per_half:
-            send_half[:, cols] = made.astype(BF16)
-        else:
-            keep_half[:, cols] = made
+        cols = slice(at * EXPAND_COLS, (at + 1) * EXPAND_COLS)
+        kept[:, cols] = made
+        sent[:, cols] = made.astype(BF16)
 
 
 def expand(hidden, named, destiny_row, gain, w_gate, w_up):
     cuts = 2 * FF // EXPAND_COLS
     return call(
         expand_kernel,
-        (shape((ROWS, FF + 128), F32), shape((ROWS, FF + 128), BF16)),
+        (shape((ROWS, 2 * FF + 128), F32), shape((ROWS, 2 * FF + 128), BF16)),
         [VM] * 4 + [ANY] * 2,
         (VM, VM),
         [
@@ -521,39 +525,28 @@
 
 
 def pair_kernel(kept, arrived, out):
-    out[:, :FF] = (kept[:, :FF] + arrived[:, :FF].astype(F32)).astype(BF16)
-    squares = kept[:, FF : FF + 1] + arrived[:, FF : FF + 1].astype(F32) + arrived[:, FF + 1 : FF + 2].astype(F32)
+    out[:, : 2 * FF] = (kept[:, : 2 * FF] + arrived[:, : 2 * FF].astype(F32)).astype(BF16)
+    tail = arrived[:, 2 * FF :].astype(F32)
+    squares = kept[:, 2 * FF : 2 * FF + 1] + tail[:, 0:1] + tail[:, 1:2]
     high, low = split_terms(squares, 2)
     lane = iota((ROWS, 128), 1)
-    out[:, FF:] = jnp.where(lane == 0, high, jnp.where(lane == 1, low, 0.0)).astype(BF16)
+    out[:, 2 * FF :] = jnp.where(lane == 0, high, jnp.where(lane == 1, low, 0.0)).astype(BF16)
 
 
 def pair_sum(kept, arrived):
-    return call(pair_kernel, shape((ROWS, FF + 128), BF16), [VM, VM], VM, [], 4, "pair_sum", moved=4 * MIB)(kept, arrived)
-
-
-def activate_kernel(a, b, c, d, token, out):
+    return call(pair_kernel, shape((ROWS, 2 * FF + 128), BF16), [VM, VM], VM, [], 4, "pair_sum", moved=4 * MIB)(
+        kept, arrived
+    )
+
+
+def down_kernel(a, b, c, d, token, destiny_row, w_down, out, rows):
     total = sum(x[...].astype(F32) for x in (a, b, c, d))
-    squares = total[:, FF : FF + 1] + total[:, FF + 1 : FF + 2]
+    squares = total[:, 2 * FF : 2 * FF + 1] + total[:, 2 * FF + 1 : 2 * FF + 2]
     factor = lax.rsqrt(squares / D + EPSILON)
-    gate = total[:, :HALF] * factor
-    up = total[:, HALF:FF] * factor
-    out[...] = (jax.nn.silu(gate) * up).astype(BF16)
-
-
-def activate(parts, token):
-    return call(activate_kernel, shape((ROWS, HALF), BF16), [VM] * 4 + [ANY], VM, [], 4, "activate", moved=4 * MIB)(
-        *parts, token
-    )
-
-
-def down_kernel(mine, other, destiny_row, w_down, out, rows):
-    core = lax.rem(lax.axis_index("lane"), 2)
-    here = pl.ds(pl.multiple_of(core * HALF, HALF), HALF)
-    there = pl.ds(pl.multiple_of((1 - core) * HALF, HALF), HALF)
-    made = jnp.dot(mine[...], w_down[0, here, :], preferred_element_type=F32)
-    made = made + jnp.dot(other[...], w_down[0, there, :], preferred_element_type=F32)
-    made = made.astype(BF16)
+    gate = total[:, :FF] * factor
+    up = total[:, FF : 2 * FF] * factor
+    active = (jax.nn.silu(gate) * up).astype(BF16)
+    made = jnp.dot(active, w_down[0], preferred_element_type=F32).astype(BF16)
     seq = iota((1, SEQS), 1)
     keeper = jnp.where(
         (destiny_row[...] == seq // SEQ_G) & (seq % SEQ_G == 0), 1.0, 0.0
@@ -569,17 +562,17 @@
         out[GROUPS - 1 - g] = rows[g * CAP : (g + 1) * CAP, :].astype(BF16)
 
 
-def down(mine, other, destiny_row, w_down):
+def down(parts, token, destiny_row, w_down):
     return call(
         down_kernel,
         shape((GROUPS, CAP, WIDTH), BF16),
-        [VM] * 4,
+        [VM] * 4 + [ANY, VM, VM],
         VM,
         [pltpu.VMEM((GROUPS * CAP, WIDTH), F32)],
         8,
         "down",
         moved=4 * MIB,
-    )(mine, other, destiny_row, w_down)
+    )(*parts, token, destiny_row, w_down)
 
 
 def own_kernel(hidden, destiny_row, routes, gates, own, combine, rows):
@@ -689,11 +682,10 @@
     forwarded, named, source = route(destiny, scattered)
     gathered = exchange(forwarded)
 
-    keep_half, send_half = expand(hidden, named, destiny_row, gain, w_gate, w_up)
-    total = pair_sum(keep_half, swap_core(send_half))
+    own_sums, sent_sums = expand(hidden, named, destiny_row, gain, w_gate, w_up)
+    total = pair_sum(own_sums, swap_core(sent_sums))
     kept_latent, kept_rope, token = keep_own(destiny, seq_pages, page_table, cut_latent, kv_rope, total)
-    active = activate(around(total), token)
-    made = down(active, swap_core(active), destiny_row, in_vmem(w_down))
+    made = down(around(total), token, destiny_row, in_vmem(w_down))
     made, gathered = lax.optimization_barrier((made, gathered))
     returned = exchange(made, REVERSED)
 

time: 80.1 us -> 79.3 us (0.990)
    ppermute x6, waiting for transfers between devices: 4.19 us -> 5.41 us  [around(): lax.ppermute(value, 'lane', [(i, (i + 2 * step) % LANES) for i in range(L...]
    ppermute x3 -> x2, waiting for transfers between devices: 3.68 us -> 2.58 us  [swap_core(): return lax.ppermute(value, 'lane', [(i, i ^ 1) for i in range(LANES)])]
    pallas_call x4 -> x3, Pallas kernels: 5.45 us -> 5.41 us  [the longest x1 3.75 us: expand(): call(expand_kernel, (shape((ROWS, 2 * FF + 128), F32), shape((ROWS, 2 * F...]
  transfers between devices with their start and end apart: 13 -> 12, of which waited for: 10 -> 10; matrix products, arithmetic and copies ran while one was open for 0% -> 0% of each run, Pallas kernels for 27% -> 27%
where the time goes in v4:
time: 79.3 us; the launch traced here: 78.9 us
  starting transfers between devices  39.9 us (50%)
  Pallas kernels  25 us (32%)
  waiting for transfers between devices  12.9 us (16%)
  between operations  0.93 us (1%)
    all_to_all x4, starting transfers between devices, exchange(): lax.all_to_all(value, 'group', split_axis=0, concat_axis=0, axis_index_gr...  29.9 us
    ppermute x6, starting transfers between devices, around(): lax.ppermute(value, 'lane', [(i, (i + 2 * step) % LANES) for i in range(L...  9.91 us
    ppermute x6, waiting for transfers between devices, around(): lax.ppermute(value, 'lane', [(i, (i + 2 * step) % LANES) for i in range(L...  5.41 us
    all_to_all x4, waiting for transfers between devices, exchange(): lax.all_to_all(value, 'group', split_axis=0, concat_axis=0, axis_index_gr...  4.93 us
    pallas_call x1, Pallas kernels, attend(): call(attend_kernel, shape((SEQ_G * HEADS, 256), BF16), [SM, SM] + [VM] *...  4.12 us
    pallas_call x1, Pallas kernels, expand(): call(expand_kernel, (shape((ROWS, 2 * FF + 128), F32), shape((ROWS, 2 * F...  3.75 us
    pallas_call x1, Pallas kernels, preload(): call(preload_kernel, pltpu.VMEM(weights.shape, weights.dtype), [ANY, ANY]...  3.17 us
    pallas_call x1, Pallas kernels, spread(): call(spread_kernel, (pltpu.HBM((GROUPS, PIECE_ROWS, LAT), BF16), shape((P...  3.14 us
  transfers between devices with their start and end apart: 12, of which 10 were waited for; matrix products, arithmetic and copies ran while one was open for 0% of the time, Pallas kernels for 27%

profile of v4, /device:TPU:0, one launch (start us, length us, event | category | flops | bytes accessed | tf_op | source)
XLA Modules:
  0.0 78.9 jit_solution(14109749488886094443)
XLA Ops:
  0.7 3.1 %spread.1 = (bf16[16,80,512]{2,1,0:T(8,128)(2,1)}, s32[2,4]{1,0:T(2,128)S(1)}) custom-call(s32[2,4]{1,0:T(2,128)} %bitcast.15, s32[4,8]{1,0:T(4,128)} %bitcast.11, bf16[8,64,128]{2,1,0:T(8,128)(2,1)} %rope.3, bf16[8,8,16,512]{3,2,1,0:T(8,128)(2,1)} %bitcast.6), custom_call_target="tpu_custom_call" | custom-call | bytes 16777216 | tf_op jit(solution)/shard_map/spread/pallas_call | solution.py:162
  3.9 9.1 %all-to-all-start.1 = ((bf16[16,80,512]{2,1,0:T(8,128)(2,1)}), bf16[16,80,512]{2,1,0:T(8,128)(2,1)S(1)}, u32[]{:S(2)}, u32[]{:S(2)}) async-start(bf16[16,80,512]{2,1,0:T(8,128)(2,1)} %get-tuple-element.20), calls=%async_computation.1 | async-start | bytes 2621440 | tf_op jit(solution)/shard_map/all_to_all | solution.py:645
  13.0 4.1 %attend.1.first = bf16[128,256]{1,0:T(8,128)(2,1)S(1)} custom-call(s32[2,4]{1,0:T(2,128)S(1)} %get-tuple-element.19.table, s32[64]{0:T(128)S(1)} %copy-done.8, bf16[4,32,512]{2,1,0:T(8,128)(2,1)S(1)} %copy-done.3, bf16[4,32,64]{2,1,0:T(8,128)(2,1)S(1)} %copy-done.4, bf16[4,512]{1,0:T(4,128)(2,1)S(1)} %copy-done.9, bf16[4,64]{1,0:T(4,128)(2,1)S(1)} %copy-done.11, ...), custom_call_target="tpu_custom_call" | custom-call | bytes 8388608 | tf_op jit(solution)/shard_map/attend/pallas_call | solution.py:229
  17.2 1.2 %collective-permute-done.second = bf16[128,256]{1,0:T(8,128)(2,1)S(1)} collective-permute-done((bf16[128,256]{1,0:T(8,128)(2,1)S(1)}, bf16[128,256]{1,0:T(8,128)(2,1)S(1)}, u32[]{:S(2)}, u32[]{:S(2)}) %collective-permute-start) | collective-permute-done | bytes 65568 | tf_op jit(solution)/shard_map/ppermute | solution.py:634
  18.8 3.3 %collective-permute-start.1 = (bf16[128,256]{1,0:T(8,128)(2,1)S(1)}, bf16[128,256]{1,0:T(8,128)(2,1)S(1)}, u32[]{:S(2)}, u32[]{:S(2)}) collective-permute-start(bf16[128,256]{1,0:T(8,128)(2,1)S(1)} %join_pair.1.after.a), channel_id=1, source_target_pairs={{0,4},{1,5},{2,6},{3,7},{4,0},{5,1},{6,2},{7,3},{8,12},{9,13},{10,... | collective-permute-start | bytes 196616 | tf_op jit(solution)/shard_map/ppermute | solution.py:639
  22.1 1.1 %collective-permute-start.2 = (bf16[128,256]{1,0:T(8,128)(2,1)S(1)}, bf16[128,256]{1,0:T(8,128)(2,1)S(1)}, u32[]{:S(2)}, u32[]{:S(2)}) collective-permute-start(bf16[128,256]{1,0:T(8,128)(2,1)S(1)} %join_pair.1.after.a), channel_id=1, source_target_pairs={{0,6},{1,7},{2,0},{3,1},{4,2},{5,3},{6,4},{7,5},{8,14},{9,15},{10,... | collective-permute-start | bytes 196616 | tf_op jit(solution)/shard_map/ppermute | solution.py:639
  24.1 3.2 %preload.1.w_out = bf16[4096,896]{1,0:T(8,128)(2,1)S(1)} custom-call(bf16[4096,896]{1,0:T(8,128)(2,1)} %weights.1, bf16[128,256]{1,0:T(8,128)(2,1)S(1)} %join_pair.1.after.a), custom_call_target="tpu_custom_call" | custom-call | bytes 8388608 | tf_op jit(solution)/shard_map/preload/pallas_call | solution.py:266
  27.3 1.3 %collective-permute-done.3.d = bf16[128,256]{1,0:T(8,128)(2,1)S(1)} collective-permute-done((bf16[128,256]{1,0:T(8,128)(2,1)S(1)}, bf16[128,256]{1,0:T(8,128)(2,1)S(1)}, u32[]{:S(2)}, u32[]{:S(2)}) %collective-permute-start.3) | collective-permute-done | bytes 65568 | tf_op jit(solution)/shard_map/ppermute | solution.py:639
  28.6 2.1 %hidden.1 = bf16[16,4,896]{2,1,0:T(4,128)(2,1)} custom-call(bf16[128,256]{1,0:T(8,128)(2,1)S(1)} %join_pair.1.after.a, bf16[128,256]{1,0:T(8,128)(2,1)S(1)} %collective-permute-done.1.b, bf16[128,256]{1,0:T(8,128)(2,1)S(1)} %collective-permute-done.2.c, bf16[128,256]{1,0:T(8,128)(2,1)S(1)} %collective-permute-done.3.d, bf16[4,896]{1,0:T(4,128)(2,1)S(1)} %copy-done.7, ...), custom_call_target="tpu_custom_call" | custom-call | bytes 8388608 | tf_op jit(solution)/shard_map/hidden/pallas_call | solution.py:290
  31.1 7.3 %all-to-all-start = ((bf16[16,4,896]{2,1,0:T(4,128)(2,1)}), bf16[16,4,896]{2,1,0:T(4,128)(2,1)S(1)}, u32[]{:S(2)}, u32[]{:S(2)}) async-start(bf16[16,4,896]{2,1,0:T(4,128)(2,1)} %hidden.1), calls=%async_computation | async-start | bytes 229376 | tf_op jit(solution)/shard_map/all_to_all | solution.py:645
  38.4 2.4 %route.1 = (bf16[16,80,512]{2,1,0:T(8,128)(2,1)}, bf16[16,16,128]{2,1,0:T(8,128)(2,1)S(1)}, s32[64]{0:T(128)S(1)}) custom-call(s32[64]{0:T(128)S(1)} %copy-done.5, bf16[16,80,512]{2,1,0:T(8,128)(2,1)S(1)} %all-to-all-done.1.pieces), custom_call_target="tpu_custom_call" | custom-call | bytes 8388608 | tf_op jit(solution)/shard_map/route/pallas_call | solution.py:353
  40.8 1.8 %all-to-all-done.hidden = bf16[16,4,896]{2,1,0:T(4,128)(2,1)S(1)} async-done(((bf16[16,4,896]{2,1,0:T(4,128)(2,1)}), bf16[16,4,896]{2,1,0:T(4,128)(2,1)S(1)}, u32[]{:S(2)}, u32[]{:S(2)}) %all-to-all-start) | async-done | bytes 114720 | tf_op jit(solution)/shard_map/all_to_all | solution.py:645
  42.7 5.0 %all-to-all-start.2 = ((bf16[16,80,512]{2,1,0:T(8,128)(2,1)}), bf16[16,80,512]{2,1,0:T(8,128)(2,1)S(1)}, u32[]{:S(2)}, u32[]{:S(2)}) async-start(bf16[16,80,512]{2,1,0:T(8,128)(2,1)} %get-tuple-element.25), calls=%async_computation.2 | async-start | bytes 2621440 | tf_op jit(solution)/shard_map/all_to_all | solution.py:645
  47.7 3.7 %expand.1 = (f32[16,4224]{1,0:T(8,128)S(1)}, bf16[16,4224]{1,0:T(8,128)(2,1)S(1)}) custom-call(bf16[16,4,896]{2,1,0:T(4,128)(2,1)S(1)} %all-to-all-done.hidden, bf16[16,16,128]{2,1,0:T(8,128)(2,1)S(1)} %get-tuple-element.21.named, s32[1,64]{1,0:T(1,128)S(1)} %bitcast.8, bf16[1,896]{1,0:T(2,128)(2,1)S(1)} %reshape.20.gain, bf16[1,896,2048]{2,1,0:T(8,128)(2,1)} %w_gate.1, ...), custom_call_target="tpu_custom_call" | custom-call | bytes 8388608 | tf_op jit(solution)/shard_map/expand/pallas_call | solution.py:511
  51.6 1.3 %collective-permute-done.4.arrived = bf16[16,4224]{1,0:T(8,128)(2,1)S(1)} collective-permute-done((bf16[16,4224]{1,0:T(8,128)(2,1)S(1)}, bf16[16,4224]{1,0:T(8,128)(2,1)S(1)}, u32[]{:S(2)}, u32[]{:S(2)}) %collective-permute-start.4) | collective-permute-done | bytes 135200 | tf_op jit(solution)/shard_map/ppermute | solution.py:634
  53.1 2.6 %collective-permute-start.5 = (bf16[16,4224]{1,0:T(8,128)(2,1)S(1)}, bf16[16,4224]{1,0:T(8,128)(2,1)S(1)}, u32[]{:S(2)}, u32[]{:S(2)}) collective-permute-start(bf16[16,4224]{1,0:T(8,128)(2,1)S(1)} %pair_sum.1.after.a), channel_id=1, source_target_pairs={{0,4},{1,5},{2,6},{3,7},{4,0},{5,1},{6,2},{7,3},{8,12},{9,13},{10,... | collective-permute-start | bytes 405512 | tf_op jit(solution)/shard_map/ppermute | solution.py:639
  55.7 1.1 %collective-permute-start.6 = (bf16[16,4224]{1,0:T(8,128)(2,1)S(1)}, bf16[16,4224]{1,0:T(8,128)(2,1)S(1)}, u32[]{:S(2)}, u32[]{:S(2)}) collective-permute-start(bf16[16,4224]{1,0:T(8,128)(2,1)S(1)} %pair_sum.1.after.a), channel_id=1, source_target_pairs={{0,6},{1,7},{2,0},{3,1},{4,2},{5,3},{6,4},{7,5},{8,14},{9,15},{10,... | collective-permute-start | bytes 405512 | tf_op jit(solution)/shard_map/ppermute | solution.py:639
  57.7 1.6 %keep_own.1 = (bf16[16,8,16,512]{3,2,1,0:T(8,128)(2,1)}, bf16[16,64,128]{2,1,0:T(8,128)(2,1)}, f32[8,128]{1,0:T(8,128)S(1)}) custom-call(s32[64]{0:T(128)S(1)} %copy-done.5, s32[64]{0:T(128)S(1)} %copy-done.8, s32[2,4]{1,0:T(2,128)S(1)} %get-tuple-element.19.table, bf16[8,8,16,512]{3,2,1,0:T(8,128)(2,1)S(1)} %bitcast.7, bf16[8,64,128]{2,1,0:T(8,128)(2,1)S(1)} %copy-done.2, ...), custom_call_target="tpu_custom_call" | custom-call | bytes 6291456 | tf_op jit(solution)/shard_map/keep_own/pallas_call | solution.py:431
  59.4 1.7 %collective-permute-done.5.b = bf16[16,4224]{1,0:T(8,128)(2,1)S(1)} collective-permute-done((bf16[16,4224]{1,0:T(8,128)(2,1)S(1)}, bf16[16,4224]{1,0:T(8,128)(2,1)S(1)}, u32[]{:S(2)}, u32[]{:S(2)}) %collective-permute-start.5) | collective-permute-done | bytes 135200 | tf_op jit(solution)/shard_map/ppermute | solution.py:639
  61.0 1.8 %collective-permute-done.6.c = bf16[16,4224]{1,0:T(8,128)(2,1)S(1)} collective-permute-done((bf16[16,4224]{1,0:T(8,128)(2,1)S(1)}, bf16[16,4224]{1,0:T(8,128)(2,1)S(1)}, u32[]{:S(2)}, u32[]{:S(2)}) %collective-permute-start.6) | collective-permute-done | bytes 135200 | tf_op jit(solution)/shard_map/ppermute | solution.py:639
  63.5 1.5 %down.1 = bf16[16,2,896]{2,1,0:T(2,128)(2,1)} custom-call(bf16[16,4224]{1,0:T(8,128)(2,1)S(1)} %pair_sum.1.after.a, bf16[16,4224]{1,0:T(8,128)(2,1)S(1)} %collective-permute-done.5.b, bf16[16,4224]{1,0:T(8,128)(2,1)S(1)} %collective-permute-done.6.c, bf16[16,4224]{1,0:T(8,128)(2,1)S(1)} %collective-permute-done.7.d, f32[8,128]{1,0:T(8,128)S(1)} %get-tuple-element.24.token, ...), custom_call_target="tpu_custom_call" | custom-call | bytes 4194304 | tf_op jit(solution)/shard_map/down/pallas_call | solution.py:566
  65.4 8.5 %all-to-all-start.3 = ((bf16[16,2,896]{2,1,0:T(2,128)(2,1)}), bf16[16,2,896]{2,1,0:T(2,128)(2,1)S(1)}, u32[]{:S(2)}, u32[]{:S(2)}) async-start(bf16[16,2,896]{2,1,0:T(2,128)(2,1)} %down.1), calls=%async_computation.3 | async-start | bytes 114688 | tf_op jit(solution)/shard_map/all_to_all | solution.py:645
  74.2 1.7 %keep_moved.1 = (bf16[16,8,16,512]{3,2,1,0:T(8,128)(2,1)}, bf16[16,64,128]{2,1,0:T(8,128)(2,1)}) custom-call(s32[64]{0:T(128)S(1)} %copy-done.5, s32[64]{0:T(128)S(1)} %copy-done.8, s32[64]{0:T(128)S(1)} %get-tuple-element.29.source, bf16[16,80,512]{2,1,0:T(8,128)(2,1)S(1)} %all-to-all-done.2.pieces, ...), custom_call_target="tpu_custom_call", output_to_operand_aliasing={{0}: (4, {}), {1}: (5, {})} | custom-call | bytes 6291456 | tf_op jit(solution)/shard_map/keep_moved/pallas_call | solution.py:444
  75.8 2.3 %all-to-all-done.3.returned = bf16[16,2,896]{2,1,0:T(2,128)(2,1)S(1)} async-done(((bf16[16,2,896]{2,1,0:T(2,128)(2,1)}), bf16[16,2,896]{2,1,0:T(2,128)(2,1)S(1)}, u32[]{:S(2)}, u32[]{:S(2)}) %all-to-all-start.3) | async-done | bytes 57376 | tf_op jit(solution)/shard_map/all_to_all | solution.py:645
  (40 shorter events, 5.1 us)
Async XLA Ops:
  0.6 12.3 %copy-start = (bf16[8,128,512]{2,1,0:T(8,128)(2,1)S(1)}, bf16[8,128,512]{2,1,0:T(8,128)(2,1)}, u32[]{:S(2)}) copy-start(bf16[8,128,512]{2,1,0:T(8,128)(2,1)} %latent.1) | copy-start | bytes 3145732
  0.6 12.3 %copy-start.2 = (bf16[8,64,128]{2,1,0:T(8,128)(2,1)S(1)}, bf16[8,64,128]{2,1,0:T(8,128)(2,1)}, u32[]{:S(2)}) copy-start(bf16[8,64,128]{2,1,0:T(8,128)(2,1)} %rope.3) | copy-start | bytes 393220
  0.7 12.3 %copy-start.8 = (s32[64]{0:T(128)S(1)}, s32[64]{0:T(128)}, u32[]{:S(2)}) copy-start(s32[64]{0:T(128)} %lengths.5) | copy-start | bytes 772
  0.7 12.3 %copy-start.3 = (bf16[4,32,512]{2,1,0:T(8,128)(2,1)S(1)}, bf16[4,32,512]{2,1,0:T(8,128)(2,1)}, u32[]{:S(2)}) copy-start(bf16[4,32,512]{2,1,0:T(8,128)(2,1)} %q_latent.1) | copy-start | bytes 393220
  0.7 12.3 %copy-start.4 = (bf16[4,32,64]{2,1,0:T(8,128)(2,1)S(1)}, bf16[4,32,64]{2,1,0:T(8,128)(2,1)}, u32[]{:S(2)}) copy-start(bf16[4,32,64]{2,1,0:T(8,128)(2,1)} %q_rope.1) | copy-start | bytes 49156
  0.7 12.3 %copy-start.9 = (bf16[4,512]{1,0:T(4,128)(2,1)S(1)}, bf16[4,512]{1,0:T(4,128)(2,1)}, u32[]{:S(2)}) copy-start(bf16[4,512]{1,0:T(4,128)(2,1)} %fresh_latent.1) | copy-start | bytes 12292
  0.7 12.3 %copy-start.11 = (bf16[4,64]{1,0:T(4,128)(2,1)S(1)}, bf16[4,64]{1,0:T(4,128)(2,1)}, u32[]{:S(2)}) copy-start(bf16[4,64]{1,0:T(4,128)(2,1)} %fresh_rope.1) | copy-start | bytes 1540
  3.9 27.3 %all-to-all-start.1 = ((bf16[16,80,512]{2,1,0:T(8,128)(2,1)}), bf16[16,80,512]{2,1,0:T(8,128)(2,1)S(1)}, u32[]{:S(2)}, u32[]{:S(2)}) async-start(bf16[16,80,512]{2,1,0:T(8,128)(2,1)} %get-tuple-element.20), calls=%async_computation.1 | async-start | bytes 2621440 | tf_op jit(solution)/shard_map/all_to_all | solution.py:645
  17.1 1.3 %collective-permute-start = (bf16[128,256]{1,0:T(8,128)(2,1)S(1)}, bf16[128,256]{1,0:T(8,128)(2,1)S(1)}, u32[]{:S(2)}, u32[]{:S(2)}) collective-permute-start(bf16[128,256]{1,0:T(8,128)(2,1)S(1)} %attend.1.first), channel_id=1, source_target_pairs={{0,1},{1,0},{2,3},{3,2},{4,5},{5,4},{6,7},{7,6},{8,9},{9,8},{10,11... | collective-permute-start | bytes 196616 | tf_op jit(solution)/shard_map/ppermute | solution.py:634
  18.8 8.5 %collective-permute-start.1 = (bf16[128,256]{1,0:T(8,128)(2,1)S(1)}, bf16[128,256]{1,0:T(8,128)(2,1)S(1)}, u32[]{:S(2)}, u32[]{:S(2)}) collective-permute-start(bf16[128,256]{1,0:T(8,128)(2,1)S(1)} %join_pair.1.after.a), channel_id=1, source_target_pairs={{0,4},{1,5},{2,6},{3,7},{4,0},{5,1},{6,2},{7,3},{8,12},{9,13},{10,... | collective-permute-start | bytes 196616 | tf_op jit(solution)/shard_map/ppermute | solution.py:639
  22.1 5.2 %collective-permute-start.2 = (bf16[128,256]{1,0:T(8,128)(2,1)S(1)}, bf16[128,256]{1,0:T(8,128)(2,1)S(1)}, u32[]{:S(2)}, u32[]{:S(2)}) collective-permute-start(bf16[128,256]{1,0:T(8,128)(2,1)S(1)} %join_pair.1.after.a), channel_id=1, source_target_pairs={{0,6},{1,7},{2,0},{3,1},{4,2},{5,3},{6,4},{7,5},{8,14},{9,15},{10,... | collective-permute-start | bytes 196616 | tf_op jit(solution)/shard_map/ppermute | solution.py:639
  23.1 5.5 %collective-permute-start.3 = (bf16[128,256]{1,0:T(8,128)(2,1)S(1)}, bf16[128,256]{1,0:T(8,128)(2,1)S(1)}, u32[]{:S(2)}, u32[]{:S(2)}) collective-permute-start(bf16[128,256]{1,0:T(8,128)(2,1)S(1)} %join_pair.1.after.a), channel_id=1, source_target_pairs={{0,2},{1,3},{2,4},{3,5},{4,6},{5,7},{6,0},{7,1},{8,10},{9,11},{10,... | collective-permute-start | bytes 196616 | tf_op jit(solution)/shard_map/ppermute | solution.py:639
  27.3 11.1 %copy-start.5 = (s32[64]{0:T(128)S(1)}, s32[64]{0:T(128)}, u32[]{:S(2)}) copy-start(s32[64]{0:T(128)} %destiny.5) | copy-start | bytes 772
  30.7 17.0 %copy-start.12 = (bf16[896]{0:T(1024)(128)(2,1)S(1)}, bf16[896]{0:T(1024)(128)(2,1)}, u32[]{:S(2)}) copy-start(bf16[896]{0:T(1024)(128)(2,1)} %param.30) | copy-start | bytes 5380
  31.1 11.5 %all-to-all-start = ((bf16[16,4,896]{2,1,0:T(4,128)(2,1)}), bf16[16,4,896]{2,1,0:T(4,128)(2,1)S(1)}, u32[]{:S(2)}, u32[]{:S(2)}) async-start(bf16[16,4,896]{2,1,0:T(4,128)(2,1)} %hidden.1), calls=%async_computation | async-start | bytes 229376 | tf_op jit(solution)/shard_map/all_to_all | solution.py:645
  42.7 22.8 %all-to-all-start.2 = ((bf16[16,80,512]{2,1,0:T(8,128)(2,1)}), bf16[16,80,512]{2,1,0:T(8,128)(2,1)S(1)}, u32[]{:S(2)}, u32[]{:S(2)}) async-start(bf16[16,80,512]{2,1,0:T(8,128)(2,1)} %get-tuple-element.25), calls=%async_computation.2 | async-start | bytes 2621440 | tf_op jit(solution)/shard_map/all_to_all | solution.py:645
  47.7 15.8 %copy-start.1 = (bf16[1,2048,896]{2,1,0:T(8,128)(2,1)S(1)}, bf16[1,2048,896]{2,1,0:T(8,128)(2,1)}, u32[]{:S(2)}) copy-start(bf16[1,2048,896]{2,1,0:T(8,128)(2,1)} %w_down.1) | copy-start | bytes 11010052
  51.5 22.4 %copy-start.6 = (s32[8,4]{0,1:T(4,128)S(1)}, s32[8,4]{0,1:T(4,128)}, u32[]{:S(2)}) copy-start(s32[8,4]{0,1:T(4,128)} %param.34) | copy-start | bytes 388
  51.5 22.4 %copy-start.10 = (f32[8,4]{0,1:T(4,128)S(1)}, f32[8,4]{0,1:T(4,128)}, u32[]{:S(2)}) copy-start(f32[8,4]{0,1:T(4,128)} %param.35) | copy-start | bytes 388
  51.5 1.4 %collective-permute-start.4 = (bf16[16,4224]{1,0:T(8,128)(2,1)S(1)}, bf16[16,4224]{1,0:T(8,128)(2,1)S(1)}, u32[]{:S(2)}, u32[]{:S(2)}) collective-permute-start(bf16[16,4224]{1,0:T(8,128)(2,1)S(1)} %get-tuple-element.23), channel_id=1, source_target_pairs={{0,1},{1,0},{2,3},{3,2},{4,5},{5,4},{6,7},{7,6},{8,9},{9,8},{10,11... | collective-permute-start | bytes 405512 | tf_op jit(solution)/shard_map/ppermute | solution.py:634
  53.1 7.9 %collective-permute-start.5 = (bf16[16,4224]{1,0:T(8,128)(2,1)S(1)}, bf16[16,4224]{1,0:T(8,128)(2,1)S(1)}, u32[]{:S(2)}, u32[]{:S(2)}) collective-permute-start(bf16[16,4224]{1,0:T(8,128)(2,1)S(1)} %pair_sum.1.after.a), channel_id=1, source_target_pairs={{0,4},{1,5},{2,6},{3,7},{4,0},{5,1},{6,2},{7,3},{8,12},{9,13},{10,... | collective-permute-start | bytes 405512 | tf_op jit(solution)/shard_map/ppermute | solution.py:639
  55.7 7.2 %collective-permute-start.6 = (bf16[16,4224]{1,0:T(8,128)(2,1)S(1)}, bf16[16,4224]{1,0:T(8,128)(2,1)S(1)}, u32[]{:S(2)}, u32[]{:S(2)}) collective-permute-start(bf16[16,4224]{1,0:T(8,128)(2,1)S(1)} %pair_sum.1.after.a), channel_id=1, source_target_pairs={{0,6},{1,7},{2,0},{3,1},{4,2},{5,3},{6,4},{7,5},{8,14},{9,15},{10,... | collective-permute-start | bytes 405512 | tf_op jit(solution)/shard_map/ppermute | solution.py:639
  56.7 6.7 %collective-permute-start.7 = (bf16[16,4224]{1,0:T(8,128)(2,1)S(1)}, bf16[16,4224]{1,0:T(8,128)(2,1)S(1)}, u32[]{:S(2)}, u32[]{:S(2)}) collective-permute-start(bf16[16,4224]{1,0:T(8,128)(2,1)S(1)} %pair_sum.1.after.a), channel_id=1, source_target_pairs={{0,2},{1,3},{2,4},{3,5},{4,6},{5,7},{6,0},{7,1},{8,10},{9,11},{10,... | collective-permute-start | bytes 405512 | tf_op jit(solution)/shard_map/ppermute | solution.py:639
  65.4 12.6 %all-to-all-start.3 = ((bf16[16,2,896]{2,1,0:T(2,128)(2,1)}), bf16[16,2,896]{2,1,0:T(2,128)(2,1)S(1)}, u32[]{:S(2)}, u32[]{:S(2)}) async-start(bf16[16,2,896]{2,1,0:T(2,128)(2,1)} %down.1), calls=%async_computation.3 | async-start | bytes 114688 | tf_op jit(solution)/shard_map/all_to_all | solution.py:645
  (1 other events, 9.8 us)

commit v5 on v4

--- a/solution.py
+++ b/solution.py
@@ -524,27 +524,42 @@
     )(hidden, named, destiny_row, gain, in_hbm(w_gate), in_hbm(w_up))
 
 
-def pair_kernel(kept, arrived, out):
-    out[:, : 2 * FF] = (kept[:, : 2 * FF] + arrived[:, : 2 * FF].astype(F32)).astype(BF16)
+def pair_kernel(kept, arrived, out, part, wide):
+    core = lax.rem(lax.axis_index("lane"), 2)
+    wide[...] = kept[:, : 2 * FF] + arrived[:, : 2 * FF].astype(F32)
+    out[:, : 2 * FF] = wide[...].astype(BF16)
+    part[:, :FF] = wide[:, pl.ds(pl.multiple_of(core * FF, FF), FF)].astype(BF16)
     tail = arrived[:, 2 * FF :].astype(F32)
     squares = kept[:, 2 * FF : 2 * FF + 1] + tail[:, 0:1] + tail[:, 1:2]
     high, low = split_terms(squares, 2)
     lane = iota((ROWS, 128), 1)
-    out[:, 2 * FF :] = jnp.where(lane == 0, high, jnp.where(lane == 1, low, 0.0)).astype(BF16)
+    last = jnp.where(lane == 0, high, jnp.where(lane == 1, low, 0.0)).astype(BF16)
+    out[:, 2 * FF :] = last
+    part[:, FF:] = last
 
 
 def pair_sum(kept, arrived):
-    return call(pair_kernel, shape((ROWS, 2 * FF + 128), BF16), [VM, VM], VM, [], 4, "pair_sum", moved=4 * MIB)(
-        kept, arrived
-    )
-
-
-def down_kernel(a, b, c, d, token, destiny_row, w_down, out, rows):
-    total = sum(x[...].astype(F32) for x in (a, b, c, d))
-    squares = total[:, 2 * FF : 2 * FF + 1] + total[:, 2 * FF + 1 : 2 * FF + 2]
+    return call(
+        pair_kernel,
+        (shape((ROWS, 2 * FF + 128), BF16), shape((ROWS, FF + 128), BF16)),
+        [VM, VM],
+        (VM, VM),
+        [pltpu.VMEM((ROWS, 2 * FF), F32)],
+        4,
+        "pair_sum",
+        moved=4 * MIB,
+    )(kept, arrived)
+
+
+def down_kernel(a, b, c, mine, other, token, destiny_row, w_down, out, rows):
+    core = lax.rem(lax.axis_index("lane"), 2)
+    total = sum(x[...].astype(F32) for x in (a, b, c))
+    here, there = mine[...].astype(F32), other[...].astype(F32)
+    last = total[:, 2 * FF :] + here[:, FF:]
+    squares = last[:, 0:1] + last[:, 1:2]
     factor = lax.rsqrt(squares / D + EPSILON)
-    gate = total[:, :FF] * factor
-    up = total[:, FF : 2 * FF] * factor
+    gate = (total[:, :FF] + jnp.where(core == 0, here[:, :FF], there[:, :FF])) * factor
+    up = (total[:, FF : 2 * FF] + jnp.where(core == 0, there[:, :FF], here[:, :FF])) * factor
     active = (jax.nn.silu(gate) * up).astype(BF16)
     made = jnp.dot(active, w_down[0], preferred_element_type=F32).astype(BF16)
     seq = iota((1, SEQS), 1)
@@ -566,7 +581,7 @@
     return call(
         down_kernel,
         shape((GROUPS, CAP, WIDTH), BF16),
-        [VM] * 4 + [ANY, VM, VM],
+        [VM] * 5 + [ANY, VM, VM],
         VM,
         [pltpu.VMEM((GROUPS * CAP, WIDTH), F32)],
         8,
@@ -634,10 +649,12 @@
     return lax.ppermute(value, "lane", [(i, i ^ 1) for i in range(LANES)])
 
 
+def along_y(value, step):
+    return lax.ppermute(value, "lane", [(i, (i + 2 * step) % LANES) for i in range(LANES)])
+
+
 def around(value):
-    return [value] + [
-        lax.ppermute(value, "lane", [(i, (i + 2 * step) % LANES) for i in range(LANES)]) for step in (2, 3, 1)
-    ]
+    return [value] + [along_y(value, step) for step in (2, 3, 1)]
 
 
 def exchange(value, order=None):
@@ -683,9 +700,11 @@
     gathered = exchange(forwarded)
 
     own_sums, sent_sums = expand(hidden, named, destiny_row, gain, w_gate, w_up)
-    total = pair_sum(own_sums, swap_core(sent_sums))
+    total, part = pair_sum(own_sums, swap_core(sent_sums))
     kept_latent, kept_rope, token = keep_own(destiny, seq_pages, page_table, cut_latent, kv_rope, total)
-    made = down(around(total), token, destiny_row, in_vmem(w_down))
+    far = along_y(part, 2)
+    sums = (total, along_y(total, 3), along_y(total, 1), far, swap_core(far))
+    made = down(sums, token, destiny_row, in_vmem(w_down))
     made, gathered = lax.optimization_barrier((made, gathered))
     returned = exchange(made, REVERSED)
 

time: 79.3 us -> 78.9 us (level)
    ppermute x2 -> x3, waiting for transfers between devices: 2.58 us -> 2.58 us  [swap_core(): return lax.ppermute(value, 'lane', [(i, i ^ 1) for i in range(LANES)])]
  transfers between devices with their start and end apart: 12 -> 13, of which waited for: 10 -> 10; matrix products, arithmetic and copies ran while one was open for 0% -> 0% of each run, Pallas kernels for 27% -> 27%
where the time goes in v5:
time: 78.9 us; the launch traced here: 78.5 us
  starting transfers between devices  39.6 us (50%)
  Pallas kernels  25.1 us (32%)
  waiting for transfers between devices  12.8 us (16%)
  between operations  0.93 us (1%)
    all_to_all x4, starting transfers between devices, exchange(): lax.all_to_all(value, 'group', split_axis=0, concat_axis=0, axis_index_gr...  29.5 us
    ppermute x6, starting transfers between devices, along_y(): lax.ppermute(value, 'lane', [(i, (i + 2 * step) % LANES) for i in range(L...  9.96 us
    all_to_all x4, waiting for transfers between devices, exchange(): lax.all_to_all(value, 'group', split_axis=0, concat_axis=0, axis_index_gr...  5.3 us
    ppermute x6, waiting for transfers between devices, along_y(): lax.ppermute(value, 'lane', [(i, (i + 2 * step) % LANES) for i in range(L...  4.96 us
    pallas_call x1, Pallas kernels, attend(): call(attend_kernel, shape((SEQ_G * HEADS, 256), BF16), [SM, SM] + [VM] *...  4.12 us
    pallas_call x1, Pallas kernels, expand(): call(expand_kernel, (shape((ROWS, 2 * FF + 128), F32), shape((ROWS, 2 * F...  3.75 us
    pallas_call x1, Pallas kernels, preload(): call(preload_kernel, pltpu.VMEM(weights.shape, weights.dtype), [ANY, ANY]...  3.17 us
    pallas_call x1, Pallas kernels, spread(): call(spread_kernel, (pltpu.HBM((GROUPS, PIECE_ROWS, LAT), BF16), shape((P...  3.14 us
  transfers between devices with their start and end apart: 13, of which 10 were waited for; matrix products, arithmetic and copies ran while one was open for 0% of the time, Pallas kernels for 27%

profile of v5, /device:TPU:0, one launch (start us, length us, event | category | flops | bytes accessed | tf_op | source)
XLA Modules:
  0.0 78.5 jit_solution(11912350666286104377)
XLA Ops:
  0.7 3.1 %spread.1 = (bf16[16,80,512]{2,1,0:T(8,128)(2,1)}, s32[2,4]{1,0:T(2,128)S(1)}) custom-call(s32[2,4]{1,0:T(2,128)} %bitcast.15, s32[4,8]{1,0:T(4,128)} %bitcast.11, bf16[8,64,128]{2,1,0:T(8,128)(2,1)} %rope.3, bf16[8,8,16,512]{3,2,1,0:T(8,128)(2,1)} %bitcast.6), custom_call_target="tpu_custom_call" | custom-call | bytes 16777216 | tf_op jit(solution)/shard_map/spread/pallas_call | solution.py:162
  3.9 9.1 %all-to-all-start.1 = ((bf16[16,80,512]{2,1,0:T(8,128)(2,1)}), bf16[16,80,512]{2,1,0:T(8,128)(2,1)S(1)}, u32[]{:S(2)}, u32[]{:S(2)}) async-start(bf16[16,80,512]{2,1,0:T(8,128)(2,1)} %get-tuple-element.22), calls=%async_computation.1 | async-start | bytes 2621440 | tf_op jit(solution)/shard_map/all_to_all | solution.py:662
  13.0 4.1 %attend.1.first = bf16[128,256]{1,0:T(8,128)(2,1)S(1)} custom-call(s32[2,4]{1,0:T(2,128)S(1)} %get-tuple-element.21.table, s32[64]{0:T(128)S(1)} %copy-done.8, bf16[4,32,512]{2,1,0:T(8,128)(2,1)S(1)} %copy-done.3, bf16[4,32,64]{2,1,0:T(8,128)(2,1)S(1)} %copy-done.4, bf16[4,512]{1,0:T(4,128)(2,1)S(1)} %copy-done.9, bf16[4,64]{1,0:T(4,128)(2,1)S(1)} %copy-done.11, ...), custom_call_target="tpu_custom_call" | custom-call | bytes 8388608 | tf_op jit(solution)/shard_map/attend/pallas_call | solution.py:229
  17.2 1.2 %collective-permute-done.second = bf16[128,256]{1,0:T(8,128)(2,1)S(1)} collective-permute-done((bf16[128,256]{1,0:T(8,128)(2,1)S(1)}, bf16[128,256]{1,0:T(8,128)(2,1)S(1)}, u32[]{:S(2)}, u32[]{:S(2)}) %collective-permute-start) | collective-permute-done | bytes 65568 | tf_op jit(solution)/shard_map/ppermute | solution.py:649
  18.8 3.3 %collective-permute-start.1 = (bf16[128,256]{1,0:T(8,128)(2,1)S(1)}, bf16[128,256]{1,0:T(8,128)(2,1)S(1)}, u32[]{:S(2)}, u32[]{:S(2)}) collective-permute-start(bf16[128,256]{1,0:T(8,128)(2,1)S(1)} %join_pair.1.after.a), channel_id=1, source_target_pairs={{0,4},{1,5},{2,6},{3,7},{4,0},{5,1},{6,2},{7,3},{8,12},{9,13},{10,... | collective-permute-start | bytes 196616 | tf_op jit(solution)/shard_map/ppermute | solution.py:653
  22.1 1.1 %collective-permute-start.2 = (bf16[128,256]{1,0:T(8,128)(2,1)S(1)}, bf16[128,256]{1,0:T(8,128)(2,1)S(1)}, u32[]{:S(2)}, u32[]{:S(2)}) collective-permute-start(bf16[128,256]{1,0:T(8,128)(2,1)S(1)} %join_pair.1.after.a), channel_id=1, source_target_pairs={{0,6},{1,7},{2,0},{3,1},{4,2},{5,3},{6,4},{7,5},{8,14},{9,15},{10,... | collective-permute-start | bytes 196616 | tf_op jit(solution)/shard_map/ppermute | solution.py:653
  24.1 3.2 %preload.1.w_out = bf16[4096,896]{1,0:T(8,128)(2,1)S(1)} custom-call(bf16[4096,896]{1,0:T(8,128)(2,1)} %weights.1, bf16[128,256]{1,0:T(8,128)(2,1)S(1)} %join_pair.1.after.a), custom_call_target="tpu_custom_call" | custom-call | bytes 8388608 | tf_op jit(solution)/shard_map/preload/pallas_call | solution.py:266
  27.3 1.3 %collective-permute-done.3.d = bf16[128,256]{1,0:T(8,128)(2,1)S(1)} collective-permute-done((bf16[128,256]{1,0:T(8,128)(2,1)S(1)}, bf16[128,256]{1,0:T(8,128)(2,1)S(1)}, u32[]{:S(2)}, u32[]{:S(2)}) %collective-permute-start.3) | collective-permute-done | bytes 65568 | tf_op jit(solution)/shard_map/ppermute | solution.py:653
  28.6 2.1 %hidden.1 = bf16[16,4,896]{2,1,0:T(4,128)(2,1)} custom-call(bf16[128,256]{1,0:T(8,128)(2,1)S(1)} %join_pair.1.after.a, bf16[128,256]{1,0:T(8,128)(2,1)S(1)} %collective-permute-done.1.b, bf16[128,256]{1,0:T(8,128)(2,1)S(1)} %collective-permute-done.2.c, bf16[128,256]{1,0:T(8,128)(2,1)S(1)} %collective-permute-done.3.d, bf16[4,896]{1,0:T(4,128)(2,1)S(1)} %copy-done.7, ...), custom_call_target="tpu_custom_call" | custom-call | bytes 8388608 | tf_op jit(solution)/shard_map/hidden/pallas_call | solution.py:290
  31.1 7.3 %all-to-all-start = ((bf16[16,4,896]{2,1,0:T(4,128)(2,1)}), bf16[16,4,896]{2,1,0:T(4,128)(2,1)S(1)}, u32[]{:S(2)}, u32[]{:S(2)}) async-start(bf16[16,4,896]{2,1,0:T(4,128)(2,1)} %hidden.1), calls=%async_computation | async-start | bytes 229376 | tf_op jit(solution)/shard_map/all_to_all | solution.py:662
  38.4 2.4 %route.1 = (bf16[16,80,512]{2,1,0:T(8,128)(2,1)}, bf16[16,16,128]{2,1,0:T(8,128)(2,1)S(1)}, s32[64]{0:T(128)S(1)}) custom-call(s32[64]{0:T(128)S(1)} %copy-done.5, bf16[16,80,512]{2,1,0:T(8,128)(2,1)S(1)} %all-to-all-done.1.pieces), custom_call_target="tpu_custom_call" | custom-call | bytes 8388608 | tf_op jit(solution)/shard_map/route/pallas_call | solution.py:353
  40.9 1.8 %all-to-all-done.hidden = bf16[16,4,896]{2,1,0:T(4,128)(2,1)S(1)} async-done(((bf16[16,4,896]{2,1,0:T(4,128)(2,1)}), bf16[16,4,896]{2,1,0:T(4,128)(2,1)S(1)}, u32[]{:S(2)}, u32[]{:S(2)}) %all-to-all-start) | async-done | bytes 114720 | tf_op jit(solution)/shard_map/all_to_all | solution.py:662
  42.7 5.0 %all-to-all-start.2 = ((bf16[16,80,512]{2,1,0:T(8,128)(2,1)}), bf16[16,80,512]{2,1,0:T(8,128)(2,1)S(1)}, u32[]{:S(2)}, u32[]{:S(2)}) async-start(bf16[16,80,512]{2,1,0:T(8,128)(2,1)} %get-tuple-element.29), calls=%async_computation.2 | async-start | bytes 2621440 | tf_op jit(solution)/shard_map/all_to_all | solution.py:662
  47.7 3.7 %expand.1 = (f32[16,4224]{1,0:T(8,128)S(1)}, bf16[16,4224]{1,0:T(8,128)(2,1)S(1)}) custom-call(bf16[16,4,896]{2,1,0:T(4,128)(2,1)S(1)} %all-to-all-done.hidden, bf16[16,16,128]{2,1,0:T(8,128)(2,1)S(1)} %get-tuple-element.23.named, s32[1,64]{1,0:T(1,128)S(1)} %bitcast.8, bf16[1,896]{1,0:T(2,128)(2,1)S(1)} %reshape.20.gain, bf16[1,896,2048]{2,1,0:T(8,128)(2,1)} %w_gate.1, ...), custom_call_target="tpu_custom_call" | custom-call | bytes 8388608 | tf_op jit(solution)/shard_map/expand/pallas_call | solution.py:511
  51.6 1.3 %collective-permute-done.4.arrived = bf16[16,4224]{1,0:T(8,128)(2,1)S(1)} collective-permute-done((bf16[16,4224]{1,0:T(8,128)(2,1)S(1)}, bf16[16,4224]{1,0:T(8,128)(2,1)S(1)}, u32[]{:S(2)}, u32[]{:S(2)}) %collective-permute-start.4) | collective-permute-done | bytes 135200 | tf_op jit(solution)/shard_map/ppermute | solution.py:649
  53.1 2.6 %collective-permute-start.7 = (bf16[16,2176]{1,0:T(8,128)(2,1)S(1)}, bf16[16,2176]{1,0:T(8,128)(2,1)S(1)}, u32[]{:S(2)}, u32[]{:S(2)}) collective-permute-start(bf16[16,2176]{1,0:T(8,128)(2,1)S(1)} %get-tuple-element.27), channel_id=1, source_target_pairs={{0,4},{1,5},{2,6},{3,7},{4,0},{5,1},{6,2},{7,3},{8,12},{9,13},{10,... | collective-permute-start | bytes 208904 | tf_op jit(solution)/shard_map/ppermute | solution.py:653
  55.7 1.1 %collective-permute-start.5 = (bf16[16,4224]{1,0:T(8,128)(2,1)S(1)}, bf16[16,4224]{1,0:T(8,128)(2,1)S(1)}, u32[]{:S(2)}, u32[]{:S(2)}) collective-permute-start(bf16[16,4224]{1,0:T(8,128)(2,1)S(1)} %get-tuple-element.26.after.a), channel_id=1, source_target_pairs={{0,6},{1,7},{2,0},{3,1},{4,2},{5,3},{6,4},{7,5},{8,14},{9,15},{10,... | collective-permute-start | bytes 405512 | tf_op jit(solution)/shard_map/ppermute | solution.py:653
  57.8 1.3 %collective-permute-done.7.mine = bf16[16,2176]{1,0:T(8,128)(2,1)S(1)} collective-permute-done((bf16[16,2176]{1,0:T(8,128)(2,1)S(1)}, bf16[16,2176]{1,0:T(8,128)(2,1)S(1)}, u32[]{:S(2)}, u32[]{:S(2)}) %collective-permute-start.7) | collective-permute-done | bytes 69664 | tf_op jit(solution)/shard_map/ppermute | solution.py:653
  59.1 1.7 %keep_own.1 = (bf16[16,8,16,512]{3,2,1,0:T(8,128)(2,1)}, bf16[16,64,128]{2,1,0:T(8,128)(2,1)}, f32[8,128]{1,0:T(8,128)S(1)}) custom-call(s32[64]{0:T(128)S(1)} %copy-done.5, s32[64]{0:T(128)S(1)} %copy-done.8, s32[2,4]{1,0:T(2,128)S(1)} %get-tuple-element.21.table, bf16[8,8,16,512]{3,2,1,0:T(8,128)(2,1)S(1)} %bitcast.7, bf16[8,64,128]{2,1,0:T(8,128)(2,1)S(1)} %copy-done.2, ...), custom_call_target="tpu_custom_call" | custom-call | bytes 6291456 | tf_op jit(solution)/shard_map/keep_own/pallas_call | solution.py:431
  61.6 1.5 %collective-permute-done.6.c = bf16[16,4224]{1,0:T(8,128)(2,1)S(1)} collective-permute-done((bf16[16,4224]{1,0:T(8,128)(2,1)S(1)}, bf16[16,4224]{1,0:T(8,128)(2,1)S(1)}, u32[]{:S(2)}, u32[]{:S(2)}) %collective-permute-start.6) | collective-permute-done | bytes 135200 | tf_op jit(solution)/shard_map/ppermute | solution.py:653
  63.1 1.5 %down.1 = bf16[16,2,896]{2,1,0:T(2,128)(2,1)} custom-call(bf16[16,4224]{1,0:T(8,128)(2,1)S(1)} %get-tuple-element.26.after.a, bf16[16,4224]{1,0:T(8,128)(2,1)S(1)} %collective-permute-done.5.b, bf16[16,4224]{1,0:T(8,128)(2,1)S(1)} %collective-permute-done.6.c, bf16[16,2176]{1,0:T(8,128)(2,1)S(1)} %collective-permute-done.7.mine, ...), custom_call_target="tpu_custom_call" | custom-call | bytes 4194304 | tf_op jit(solution)/shard_map/down/pallas_call | solution.py:581
  65.4 8.1 %all-to-all-start.3 = ((bf16[16,2,896]{2,1,0:T(2,128)(2,1)}), bf16[16,2,896]{2,1,0:T(2,128)(2,1)S(1)}, u32[]{:S(2)}, u32[]{:S(2)}) async-start(bf16[16,2,896]{2,1,0:T(2,128)(2,1)} %down.1), calls=%async_computation.3 | async-start | bytes 114688 | tf_op jit(solution)/shard_map/all_to_all | solution.py:662
  73.8 1.7 %keep_moved.1 = (bf16[16,8,16,512]{3,2,1,0:T(8,128)(2,1)}, bf16[16,64,128]{2,1,0:T(8,128)(2,1)}) custom-call(s32[64]{0:T(128)S(1)} %copy-done.5, s32[64]{0:T(128)S(1)} %copy-done.8, s32[64]{0:T(128)S(1)} %get-tuple-element.33.source, bf16[16,80,512]{2,1,0:T(8,128)(2,1)S(1)} %all-to-all-done.2.pieces, ...), custom_call_target="tpu_custom_call", output_to_operand_aliasing={{0}: (4, {}), {1}: (5, {})} | custom-call | bytes 6291456 | tf_op jit(solution)/shard_map/keep_moved/pallas_call | solution.py:444
  75.4 2.3 %all-to-all-done.3.returned = bf16[16,2,896]{2,1,0:T(2,128)(2,1)S(1)} async-done(((bf16[16,2,896]{2,1,0:T(2,128)(2,1)}), bf16[16,2,896]{2,1,0:T(2,128)(2,1)S(1)}, u32[]{:S(2)}, u32[]{:S(2)}) %all-to-all-start.3) | async-done | bytes 57376 | tf_op jit(solution)/shard_map/all_to_all | solution.py:662
  (42 shorter events, 5.8 us)
Async XLA Ops:
  0.6 12.3 %copy-start = (bf16[8,128,512]{2,1,0:T(8,128)(2,1)S(1)}, bf16[8,128,512]{2,1,0:T(8,128)(2,1)}, u32[]{:S(2)}) copy-start(bf16[8,128,512]{2,1,0:T(8,128)(2,1)} %latent.1) | copy-start | bytes 3145732
  0.6 12.3 %copy-start.2 = (bf16[8,64,128]{2,1,0:T(8,128)(2,1)S(1)}, bf16[8,64,128]{2,1,0:T(8,128)(2,1)}, u32[]{:S(2)}) copy-start(bf16[8,64,128]{2,1,0:T(8,128)(2,1)} %rope.3) | copy-start | bytes 393220
  0.7 12.3 %copy-start.8 = (s32[64]{0:T(128)S(1)}, s32[64]{0:T(128)}, u32[]{:S(2)}) copy-start(s32[64]{0:T(128)} %lengths.5) | copy-start | bytes 772
  0.7 12.3 %copy-start.3 = (bf16[4,32,512]{2,1,0:T(8,128)(2,1)S(1)}, bf16[4,32,512]{2,1,0:T(8,128)(2,1)}, u32[]{:S(2)}) copy-start(bf16[4,32,512]{2,1,0:T(8,128)(2,1)} %q_latent.1) | copy-start | bytes 393220
  0.7 12.3 %copy-start.4 = (bf16[4,32,64]{2,1,0:T(8,128)(2,1)S(1)}, bf16[4,32,64]{2,1,0:T(8,128)(2,1)}, u32[]{:S(2)}) copy-start(bf16[4,32,64]{2,1,0:T(8,128)(2,1)} %q_rope.1) | copy-start | bytes 49156
  0.7 12.3 %copy-start.9 = (bf16[4,512]{1,0:T(4,128)(2,1)S(1)}, bf16[4,512]{1,0:T(4,128)(2,1)}, u32[]{:S(2)}) copy-start(bf16[4,512]{1,0:T(4,128)(2,1)} %fresh_latent.1) | copy-start | bytes 12292
  0.7 12.3 %copy-start.11 = (bf16[4,64]{1,0:T(4,128)(2,1)S(1)}, bf16[4,64]{1,0:T(4,128)(2,1)}, u32[]{:S(2)}) copy-start(bf16[4,64]{1,0:T(4,128)(2,1)} %fresh_rope.1) | copy-start | bytes 1540
  3.9 27.3 %all-to-all-start.1 = ((bf16[16,80,512]{2,1,0:T(8,128)(2,1)}), bf16[16,80,512]{2,1,0:T(8,128)(2,1)S(1)}, u32[]{:S(2)}, u32[]{:S(2)}) async-start(bf16[16,80,512]{2,1,0:T(8,128)(2,1)} %get-tuple-element.22), calls=%async_computation.1 | async-start | bytes 2621440 | tf_op jit(solution)/shard_map/all_to_all | solution.py:662
  17.1 1.3 %collective-permute-start = (bf16[128,256]{1,0:T(8,128)(2,1)S(1)}, bf16[128,256]{1,0:T(8,128)(2,1)S(1)}, u32[]{:S(2)}, u32[]{:S(2)}) collective-permute-start(bf16[128,256]{1,0:T(8,128)(2,1)S(1)} %attend.1.first), channel_id=1, source_target_pairs={{0,1},{1,0},{2,3},{3,2},{4,5},{5,4},{6,7},{7,6},{8,9},{9,8},{10,11... | collective-permute-start | bytes 196616 | tf_op jit(solution)/shard_map/ppermute | solution.py:649
  18.8 8.5 %collective-permute-start.1 = (bf16[128,256]{1,0:T(8,128)(2,1)S(1)}, bf16[128,256]{1,0:T(8,128)(2,1)S(1)}, u32[]{:S(2)}, u32[]{:S(2)}) collective-permute-start(bf16[128,256]{1,0:T(8,128)(2,1)S(1)} %join_pair.1.after.a), channel_id=1, source_target_pairs={{0,4},{1,5},{2,6},{3,7},{4,0},{5,1},{6,2},{7,3},{8,12},{9,13},{10,... | collective-permute-start | bytes 196616 | tf_op jit(solution)/shard_map/ppermute | solution.py:653
  22.1 5.2 %collective-permute-start.2 = (bf16[128,256]{1,0:T(8,128)(2,1)S(1)}, bf16[128,256]{1,0:T(8,128)(2,1)S(1)}, u32[]{:S(2)}, u32[]{:S(2)}) collective-permute-start(bf16[128,256]{1,0:T(8,128)(2,1)S(1)} %join_pair.1.after.a), channel_id=1, source_target_pairs={{0,6},{1,7},{2,0},{3,1},{4,2},{5,3},{6,4},{7,5},{8,14},{9,15},{10,... | collective-permute-start | bytes 196616 | tf_op jit(solution)/shard_map/ppermute | solution.py:653
  23.1 5.5 %collective-permute-start.3 = (bf16[128,256]{1,0:T(8,128)(2,1)S(1)}, bf16[128,256]{1,0:T(8,128)(2,1)S(1)}, u32[]{:S(2)}, u32[]{:S(2)}) collective-permute-start(bf16[128,256]{1,0:T(8,128)(2,1)S(1)} %join_pair.1.after.a), channel_id=1, source_target_pairs={{0,2},{1,3},{2,4},{3,5},{4,6},{5,7},{6,0},{7,1},{8,10},{9,11},{10,... | collective-permute-start | bytes 196616 | tf_op jit(solution)/shard_map/ppermute | solution.py:653
  30.7 17.0 %copy-start.12 = (bf16[896]{0:T(1024)(128)(2,1)S(1)}, bf16[896]{0:T(1024)(128)(2,1)}, u32[]{:S(2)}) copy-start(bf16[896]{0:T(1024)(128)(2,1)} %param.30) | copy-start | bytes 5380
  31.1 11.5 %all-to-all-start = ((bf16[16,4,896]{2,1,0:T(4,128)(2,1)}), bf16[16,4,896]{2,1,0:T(4,128)(2,1)S(1)}, u32[]{:S(2)}, u32[]{:S(2)}) async-start(bf16[16,4,896]{2,1,0:T(4,128)(2,1)} %hidden.1), calls=%async_computation | async-start | bytes 229376 | tf_op jit(solution)/shard_map/all_to_all | solution.py:662
  42.7 22.8 %all-to-all-start.2 = ((bf16[16,80,512]{2,1,0:T(8,128)(2,1)}), bf16[16,80,512]{2,1,0:T(8,128)(2,1)S(1)}, u32[]{:S(2)}, u32[]{:S(2)}) async-start(bf16[16,80,512]{2,1,0:T(8,128)(2,1)} %get-tuple-element.29), calls=%async_computation.2 | async-start | bytes 2621440 | tf_op jit(solution)/shard_map/all_to_all | solution.py:662
  47.7 15.4 %copy-start.1 = (bf16[1,2048,896]{2,1,0:T(8,128)(2,1)S(1)}, bf16[1,2048,896]{2,1,0:T(8,128)(2,1)}, u32[]{:S(2)}) copy-start(bf16[1,2048,896]{2,1,0:T(8,128)(2,1)} %w_down.1) | copy-start | bytes 11010052
  51.5 22.0 %copy-start.6 = (s32[8,4]{0,1:T(4,128)S(1)}, s32[8,4]{0,1:T(4,128)}, u32[]{:S(2)}) copy-start(s32[8,4]{0,1:T(4,128)} %param.34) | copy-start | bytes 388
  51.5 22.0 %copy-start.10 = (f32[8,4]{0,1:T(4,128)S(1)}, f32[8,4]{0,1:T(4,128)}, u32[]{:S(2)}) copy-start(f32[8,4]{0,1:T(4,128)} %param.35) | copy-start | bytes 388
  51.5 1.4 %collective-permute-start.4 = (bf16[16,4224]{1,0:T(8,128)(2,1)S(1)}, bf16[16,4224]{1,0:T(8,128)(2,1)S(1)}, u32[]{:S(2)}, u32[]{:S(2)}) collective-permute-start(bf16[16,4224]{1,0:T(8,128)(2,1)S(1)} %get-tuple-element.25), channel_id=1, source_target_pairs={{0,1},{1,0},{2,3},{3,2},{4,5},{5,4},{6,7},{7,6},{8,9},{9,8},{10,11... | collective-permute-start | bytes 405512 | tf_op jit(solution)/shard_map/ppermute | solution.py:649
  53.1 6.0 %collective-permute-start.7 = (bf16[16,2176]{1,0:T(8,128)(2,1)S(1)}, bf16[16,2176]{1,0:T(8,128)(2,1)S(1)}, u32[]{:S(2)}, u32[]{:S(2)}) collective-permute-start(bf16[16,2176]{1,0:T(8,128)(2,1)S(1)} %get-tuple-element.27), channel_id=1, source_target_pairs={{0,4},{1,5},{2,6},{3,7},{4,0},{5,1},{6,2},{7,3},{8,12},{9,13},{10,... | collective-permute-start | bytes 208904 | tf_op jit(solution)/shard_map/ppermute | solution.py:653
  55.7 5.9 %collective-permute-start.5 = (bf16[16,4224]{1,0:T(8,128)(2,1)S(1)}, bf16[16,4224]{1,0:T(8,128)(2,1)S(1)}, u32[]{:S(2)}, u32[]{:S(2)}) collective-permute-start(bf16[16,4224]{1,0:T(8,128)(2,1)S(1)} %get-tuple-element.26.after.a), channel_id=1, source_target_pairs={{0,6},{1,7},{2,0},{3,1},{4,2},{5,3},{6,4},{7,5},{8,14},{9,15},{10,... | collective-permute-start | bytes 405512 | tf_op jit(solution)/shard_map/ppermute | solution.py:653
  56.8 6.3 %collective-permute-start.6 = (bf16[16,4224]{1,0:T(8,128)(2,1)S(1)}, bf16[16,4224]{1,0:T(8,128)(2,1)S(1)}, u32[]{:S(2)}, u32[]{:S(2)}) collective-permute-start(bf16[16,4224]{1,0:T(8,128)(2,1)S(1)} %get-tuple-element.26.after.a), channel_id=1, source_target_pairs={{0,2},{1,3},{2,4},{3,5},{4,6},{5,7},{6,0},{7,1},{8,10},{9,11},{10,... | collective-permute-start | bytes 405512 | tf_op jit(solution)/shard_map/ppermute | solution.py:653
  59.1 4.0 %collective-permute-start.8 = (bf16[16,2176]{1,0:T(8,128)(2,1)S(1)}, bf16[16,2176]{1,0:T(8,128)(2,1)S(1)}, u32[]{:S(2)}, u32[]{:S(2)}) collective-permute-start(bf16[16,2176]{1,0:T(8,128)(2,1)S(1)} %collective-permute-done.7.mine), channel_id=1, source_target_pairs={{0,1},{1,0},{2,3},{3,2},{4,5},{5,4},{6,7},{7,6},{8,9},{9,8},{10,11... | collective-permute-start | bytes 208904 | tf_op jit(solution)/shard_map/ppermute | solution.py:649
  65.4 12.3 %all-to-all-start.3 = ((bf16[16,2,896]{2,1,0:T(2,128)(2,1)}), bf16[16,2,896]{2,1,0:T(2,128)(2,1)S(1)}, u32[]{:S(2)}, u32[]{:S(2)}) async-start(bf16[16,2,896]{2,1,0:T(2,128)(2,1)} %down.1), calls=%async_computation.3 | async-start | bytes 114688 | tf_op jit(solution)/shard_map/all_to_all | solution.py:662
  (2 other events, 21.0 us)

commit v6 on v5

--- a/solution.py
+++ b/solution.py
@@ -376,7 +376,7 @@
 
 
 def keep_own_kernel(
-    destiny, lengths, table, latent, rope, after, kept, kept_rope, token, zeros, rope_out, sems, rope_sem
+    destiny, lengths, table, latent, rope, after, kept, kept_rope, zeros, rope_out, sems, rope_sem
 ):
     group, lane = lax.axis_index("group"), lax.axis_index("lane")
     stays = destiny[group * SEQ_G] == group
@@ -389,7 +389,6 @@
     waits = place_pages(pages, kept, rope_out, zeros, sems, 0)
     turned = pltpu.make_async_copy(rope_out, kept_rope.at[pl.ds(0, SEQ_G * PSL)], rope_sem)
     turned.start()
-    token[...] = jnp.zeros_like(token)
     for wait in [*waits, turned]:
         wait.wait()
 
@@ -430,9 +429,9 @@
 def keep_own(destiny, lengths, table, latent, rope, after):
     return call(
         keep_own_kernel,
-        (*KEPT, shape((8, 128), F32)),
+        KEPT,
         [SM, SM, SM, VM, VM, ANY],
-        (ANY, ANY, VM),
+        (ANY, ANY),
         KEEP_SCRATCH,
         4,
         "keep_own",
@@ -551,7 +550,7 @@
     )(kept, arrived)
 
 
-def down_kernel(a, b, c, mine, other, token, destiny_row, w_down, out, rows):
+def down_kernel(a, b, c, mine, other, destiny_row, w_down, out, rows):
     core = lax.rem(lax.axis_index("lane"), 2)
     total = sum(x[...].astype(F32) for x in (a, b, c))
     here, there = mine[...].astype(F32), other[...].astype(F32)
@@ -577,17 +576,17 @@
         out[GROUPS - 1 - g] = rows[g * CAP : (g + 1) * CAP, :].astype(BF16)
 
 
-def down(parts, token, destiny_row, w_down):
+def down(parts, destiny_row, w_down):
     return call(
         down_kernel,
         shape((GROUPS, CAP, WIDTH), BF16),
-        [VM] * 5 + [ANY, VM, VM],
+        [VM] * 7,
         VM,
         [pltpu.VMEM((GROUPS * CAP, WIDTH), F32)],
         8,
         "down",
         moved=4 * MIB,
-    )(*parts, token, destiny_row, w_down)
+    )(*parts, destiny_row, w_down)
 
 
 def own_kernel(hidden, destiny_row, routes, gates, own, combine, rows):
@@ -606,13 +605,14 @@
     later = (iota((NEW_G, NEW_G), 1) < iota((NEW_G, NEW_G), 0)).astype(F32)
     before = jnp.dot(later, hits, preferred_element_type=F32)
     want = (iota((NEW_G, GROUPS * CAP), 1) % CAP).astype(F32)
-    combine[...] = jnp.where(before == want, weight, 0.0)
+    terms = split_terms(jnp.where(before == want, weight, 0.0), 3)
+    combine[...] = jnp.concatenate(terms, axis=0)
 
 
 def own_rows(hidden, destiny_row, routes, gates):
     return call(
         own_kernel,
-        (shape((NEW_G, WIDTH), F32), shape((NEW_G, GROUPS * CAP), F32)),
+        (shape((NEW_G, WIDTH), F32), shape((3 * NEW_G, GROUPS * CAP), F32)),
         [VM] * 4,
         (VM, VM),
         [pltpu.VMEM((SEQS, WIDTH), F32)],
@@ -626,9 +626,10 @@
     for g in range(GROUPS):
         rows[g * CAP : (g + 1) * CAP, :] = returned[GROUPS - 1 - g].astype(F32)
     back = rows[...].astype(BF16)
+    terms = jnp.dot(combine[...].astype(BF16), back, preferred_element_type=F32)
     mixed = own[...]
-    for term in split_terms(combine[...], 3):
-        mixed = mixed + jnp.dot(term.astype(BF16), back, preferred_element_type=F32)
+    for i in range(3):
+        mixed = mixed + terms[i * NEW_G : (i + 1) * NEW_G, :]
     out[...] = mixed.astype(BF16)
 
 
@@ -701,15 +702,15 @@
 
     own_sums, sent_sums = expand(hidden, named, destiny_row, gain, w_gate, w_up)
     total, part = pair_sum(own_sums, swap_core(sent_sums))
-    kept_latent, kept_rope, token = keep_own(destiny, seq_pages, page_table, cut_latent, kv_rope, total)
     far = along_y(part, 2)
     sums = (total, along_y(total, 3), along_y(total, 1), far, swap_core(far))
-    made = down(sums, token, destiny_row, in_vmem(w_down))
+    made = down(sums, destiny_row, in_vmem(w_down))
     made, gathered = lax.optimization_barrier((made, gathered))
     returned = exchange(made, REVERSED)
 
     own, combine = own_rows(hidden, destiny_row, routes, route_gates)
     layer_out = finish(returned, own, combine)
+    kept_latent, kept_rope = keep_own(destiny, seq_pages, page_table, cut_latent, kv_rope, made)
     kept_latent, kept_rope = keep_moved(destiny, seq_pages, source, gathered, kept_latent, kept_rope)
     return layer_out, kept_latent.reshape(-1, PAGE, LAT), kept_rope
 

time: 78.9 us -> 78.9 us (level)
    all_to_all x4, waiting for transfers between devices: 5.3 us -> 3.64 us  [exchange(): lax.all_to_all(value, 'group', split_axis=0, concat_axis=0, axis_index_gr...]
    ppermute x6, waiting for transfers between devices: 4.96 us -> 6.61 us  [along_y(): lax.ppermute(value, 'lane', [(i, (i + 2 * step) % LANES) for i in range(L...]
where the time goes in v6:
time: 78.9 us; the launch traced here: 78.5 us
  starting transfers between devices  39.6 us (50%)
  Pallas kernels  25 us (32%)
  waiting for transfers between devices  12.8 us (16%)
  between operations  0.93 us (1%)
    all_to_all x4, starting transfers between devices, exchange(): lax.all_to_all(value, 'group', split_axis=0, concat_axis=0, axis_index_gr...  29.5 us
    ppermute x6, starting transfers between devices, along_y(): lax.ppermute(value, 'lane', [(i, (i + 2 * step) % LANES) for i in range(L...  9.96 us
    ppermute x6, waiting for transfers between devices, along_y(): lax.ppermute(value, 'lane', [(i, (i + 2 * step) % LANES) for i in range(L...  6.61 us
    pallas_call x1, Pallas kernels, attend(): call(attend_kernel, shape((SEQ_G * HEADS, 256), BF16), [SM, SM] + [VM] *...  4.12 us
    pallas_call x1, Pallas kernels, expand(): call(expand_kernel, (shape((ROWS, 2 * FF + 128), F32), shape((ROWS, 2 * F...  3.75 us
    all_to_all x4, waiting for transfers between devices, exchange(): lax.all_to_all(value, 'group', split_axis=0, concat_axis=0, axis_index_gr...  3.64 us
    pallas_call x1, Pallas kernels, preload(): call(preload_kernel, pltpu.VMEM(weights.shape, weights.dtype), [ANY, ANY]...  3.17 us
    pallas_call x1, Pallas kernels, spread(): call(spread_kernel, (pltpu.HBM((GROUPS, PIECE_ROWS, LAT), BF16), shape((P...  3.14 us
  transfers between devices with their start and end apart: 13, of which 10 were waited for; matrix products, arithmetic and copies ran while one was open for 0% of the time, Pallas kernels for 27%

profile of v6, /device:TPU:0, one launch (start us, length us, event | category | flops | bytes accessed | tf_op | source)
XLA Modules:
  0.0 78.5 jit_solution(5698619072348127135)
XLA Ops:
  0.7 3.1 %spread.1 = (bf16[16,80,512]{2,1,0:T(8,128)(2,1)}, s32[2,4]{1,0:T(2,128)S(1)}) custom-call(s32[2,4]{1,0:T(2,128)} %bitcast.15, s32[4,8]{1,0:T(4,128)} %bitcast.11, bf16[8,64,128]{2,1,0:T(8,128)(2,1)} %rope.3, bf16[8,8,16,512]{3,2,1,0:T(8,128)(2,1)} %bitcast.6), custom_call_target="tpu_custom_call" | custom-call | bytes 16777216 | tf_op jit(solution)/shard_map/spread/pallas_call | solution.py:162
  3.9 9.1 %all-to-all-start.1 = ((bf16[16,80,512]{2,1,0:T(8,128)(2,1)}), bf16[16,80,512]{2,1,0:T(8,128)(2,1)S(1)}, u32[]{:S(2)}, u32[]{:S(2)}) async-start(bf16[16,80,512]{2,1,0:T(8,128)(2,1)} %get-tuple-element.21), calls=%async_computation.1 | async-start | bytes 2621440 | tf_op jit(solution)/shard_map/all_to_all | solution.py:663
  13.0 4.1 %attend.1.first = bf16[128,256]{1,0:T(8,128)(2,1)S(1)} custom-call(s32[2,4]{1,0:T(2,128)S(1)} %get-tuple-element.20.table, s32[64]{0:T(128)S(1)} %copy-done.8, bf16[4,32,512]{2,1,0:T(8,128)(2,1)S(1)} %copy-done.3, bf16[4,32,64]{2,1,0:T(8,128)(2,1)S(1)} %copy-done.4, bf16[4,512]{1,0:T(4,128)(2,1)S(1)} %copy-done.9, bf16[4,64]{1,0:T(4,128)(2,1)S(1)} %copy-done.11, ...), custom_call_target="tpu_custom_call" | custom-call | bytes 8388608 | tf_op jit(solution)/shard_map/attend/pallas_call | solution.py:229
  17.2 1.2 %collective-permute-done.second = bf16[128,256]{1,0:T(8,128)(2,1)S(1)} collective-permute-done((bf16[128,256]{1,0:T(8,128)(2,1)S(1)}, bf16[128,256]{1,0:T(8,128)(2,1)S(1)}, u32[]{:S(2)}, u32[]{:S(2)}) %collective-permute-start) | collective-permute-done | bytes 65568 | tf_op jit(solution)/shard_map/ppermute | solution.py:650
  18.8 3.3 %collective-permute-start.1 = (bf16[128,256]{1,0:T(8,128)(2,1)S(1)}, bf16[128,256]{1,0:T(8,128)(2,1)S(1)}, u32[]{:S(2)}, u32[]{:S(2)}) collective-permute-start(bf16[128,256]{1,0:T(8,128)(2,1)S(1)} %join_pair.1.after.a), channel_id=1, source_target_pairs={{0,4},{1,5},{2,6},{3,7},{4,0},{5,1},{6,2},{7,3},{8,12},{9,13},{10,... | collective-permute-start | bytes 196616 | tf_op jit(solution)/shard_map/ppermute | solution.py:654
  22.1 1.1 %collective-permute-start.2 = (bf16[128,256]{1,0:T(8,128)(2,1)S(1)}, bf16[128,256]{1,0:T(8,128)(2,1)S(1)}, u32[]{:S(2)}, u32[]{:S(2)}) collective-permute-start(bf16[128,256]{1,0:T(8,128)(2,1)S(1)} %join_pair.1.after.a), channel_id=1, source_target_pairs={{0,6},{1,7},{2,0},{3,1},{4,2},{5,3},{6,4},{7,5},{8,14},{9,15},{10,... | collective-permute-start | bytes 196616 | tf_op jit(solution)/shard_map/ppermute | solution.py:654
  24.1 3.2 %preload.1.w_out = bf16[4096,896]{1,0:T(8,128)(2,1)S(1)} custom-call(bf16[4096,896]{1,0:T(8,128)(2,1)} %weights.1, bf16[128,256]{1,0:T(8,128)(2,1)S(1)} %join_pair.1.after.a), custom_call_target="tpu_custom_call" | custom-call | bytes 8388608 | tf_op jit(solution)/shard_map/preload/pallas_call | solution.py:266
  27.3 1.3 %collective-permute-done.3.d = bf16[128,256]{1,0:T(8,128)(2,1)S(1)} collective-permute-done((bf16[128,256]{1,0:T(8,128)(2,1)S(1)}, bf16[128,256]{1,0:T(8,128)(2,1)S(1)}, u32[]{:S(2)}, u32[]{:S(2)}) %collective-permute-start.3) | collective-permute-done | bytes 65568 | tf_op jit(solution)/shard_map/ppermute | solution.py:654
  28.6 2.1 %hidden.1 = bf16[16,4,896]{2,1,0:T(4,128)(2,1)} custom-call(bf16[128,256]{1,0:T(8,128)(2,1)S(1)} %join_pair.1.after.a, bf16[128,256]{1,0:T(8,128)(2,1)S(1)} %collective-permute-done.1.b, bf16[128,256]{1,0:T(8,128)(2,1)S(1)} %collective-permute-done.2.c, bf16[128,256]{1,0:T(8,128)(2,1)S(1)} %collective-permute-done.3.d, bf16[4,896]{1,0:T(4,128)(2,1)S(1)} %copy-done.7, ...), custom_call_target="tpu_custom_call" | custom-call | bytes 8388608 | tf_op jit(solution)/shard_map/hidden/pallas_call | solution.py:290
  31.1 7.3 %all-to-all-start = ((bf16[16,4,896]{2,1,0:T(4,128)(2,1)}), bf16[16,4,896]{2,1,0:T(4,128)(2,1)S(1)}, u32[]{:S(2)}, u32[]{:S(2)}) async-start(bf16[16,4,896]{2,1,0:T(4,128)(2,1)} %hidden.1), calls=%async_computation | async-start | bytes 229376 | tf_op jit(solution)/shard_map/all_to_all | solution.py:663
  38.4 2.4 %route.1 = (bf16[16,80,512]{2,1,0:T(8,128)(2,1)}, bf16[16,16,128]{2,1,0:T(8,128)(2,1)S(1)}, s32[64]{0:T(128)S(1)}) custom-call(s32[64]{0:T(128)S(1)} %copy-done.5, bf16[16,80,512]{2,1,0:T(8,128)(2,1)S(1)} %all-to-all-done.1.pieces), custom_call_target="tpu_custom_call" | custom-call | bytes 8388608 | tf_op jit(solution)/shard_map/route/pallas_call | solution.py:353
  40.9 1.8 %all-to-all-done.hidden = bf16[16,4,896]{2,1,0:T(4,128)(2,1)S(1)} async-done(((bf16[16,4,896]{2,1,0:T(4,128)(2,1)}), bf16[16,4,896]{2,1,0:T(4,128)(2,1)S(1)}, u32[]{:S(2)}, u32[]{:S(2)}) %all-to-all-start) | async-done | bytes 114720 | tf_op jit(solution)/shard_map/all_to_all | solution.py:663
  42.7 5.0 %all-to-all-start.2 = ((bf16[16,80,512]{2,1,0:T(8,128)(2,1)}), bf16[16,80,512]{2,1,0:T(8,128)(2,1)S(1)}, u32[]{:S(2)}, u32[]{:S(2)}) async-start(bf16[16,80,512]{2,1,0:T(8,128)(2,1)} %get-tuple-element.27), calls=%async_computation.2 | async-start | bytes 2621440 | tf_op jit(solution)/shard_map/all_to_all | solution.py:663
  47.7 3.7 %expand.1 = (f32[16,4224]{1,0:T(8,128)S(1)}, bf16[16,4224]{1,0:T(8,128)(2,1)S(1)}) custom-call(bf16[16,4,896]{2,1,0:T(4,128)(2,1)S(1)} %all-to-all-done.hidden, bf16[16,16,128]{2,1,0:T(8,128)(2,1)S(1)} %get-tuple-element.22.named, s32[1,64]{1,0:T(1,128)S(1)} %bitcast.8, bf16[1,896]{1,0:T(2,128)(2,1)S(1)} %reshape.20.gain, bf16[1,896,2048]{2,1,0:T(8,128)(2,1)} %w_gate.1, ...), custom_call_target="tpu_custom_call" | custom-call | bytes 8388608 | tf_op jit(solution)/shard_map/expand/pallas_call | solution.py:510
  51.6 1.3 %collective-permute-done.4.arrived = bf16[16,4224]{1,0:T(8,128)(2,1)S(1)} collective-permute-done((bf16[16,4224]{1,0:T(8,128)(2,1)S(1)}, bf16[16,4224]{1,0:T(8,128)(2,1)S(1)}, u32[]{:S(2)}, u32[]{:S(2)}) %collective-permute-start.4) | collective-permute-done | bytes 135200 | tf_op jit(solution)/shard_map/ppermute | solution.py:650
  53.1 2.6 %collective-permute-start.7 = (bf16[16,2176]{1,0:T(8,128)(2,1)S(1)}, bf16[16,2176]{1,0:T(8,128)(2,1)S(1)}, u32[]{:S(2)}, u32[]{:S(2)}) collective-permute-start(bf16[16,2176]{1,0:T(8,128)(2,1)S(1)} %get-tuple-element.26), channel_id=1, source_target_pairs={{0,4},{1,5},{2,6},{3,7},{4,0},{5,1},{6,2},{7,3},{8,12},{9,13},{10,... | collective-permute-start | bytes 208904 | tf_op jit(solution)/shard_map/ppermute | solution.py:654
  55.7 1.1 %collective-permute-start.5 = (bf16[16,4224]{1,0:T(8,128)(2,1)S(1)}, bf16[16,4224]{1,0:T(8,128)(2,1)S(1)}, u32[]{:S(2)}, u32[]{:S(2)}) collective-permute-start(bf16[16,4224]{1,0:T(8,128)(2,1)S(1)} %get-tuple-element.25.a), channel_id=1, source_target_pairs={{0,6},{1,7},{2,0},{3,1},{4,2},{5,3},{6,4},{7,5},{8,14},{9,15},{10,... | collective-permute-start | bytes 405512 | tf_op jit(solution)/shard_map/ppermute | solution.py:654
  57.8 1.3 %collective-permute-done.7.mine = bf16[16,2176]{1,0:T(8,128)(2,1)S(1)} collective-permute-done((bf16[16,2176]{1,0:T(8,128)(2,1)S(1)}, bf16[16,2176]{1,0:T(8,128)(2,1)S(1)}, u32[]{:S(2)}, u32[]{:S(2)}) %collective-permute-start.7) | collective-permute-done | bytes 69664 | tf_op jit(solution)/shard_map/ppermute | solution.py:654
  59.1 2.5 %collective-permute-done.5.b = bf16[16,4224]{1,0:T(8,128)(2,1)S(1)} collective-permute-done((bf16[16,4224]{1,0:T(8,128)(2,1)S(1)}, bf16[16,4224]{1,0:T(8,128)(2,1)S(1)}, u32[]{:S(2)}, u32[]{:S(2)}) %collective-permute-start.5) | collective-permute-done | bytes 135200 | tf_op jit(solution)/shard_map/ppermute | solution.py:654
  61.6 1.5 %collective-permute-done.6.c = bf16[16,4224]{1,0:T(8,128)(2,1)S(1)} collective-permute-done((bf16[16,4224]{1,0:T(8,128)(2,1)S(1)}, bf16[16,4224]{1,0:T(8,128)(2,1)S(1)}, u32[]{:S(2)}, u32[]{:S(2)}) %collective-permute-start.6) | collective-permute-done | bytes 135200 | tf_op jit(solution)/shard_map/ppermute | solution.py:654
  63.1 1.5 %down.1.after = bf16[16,2,896]{2,1,0:T(2,128)(2,1)} custom-call(bf16[16,4224]{1,0:T(8,128)(2,1)S(1)} %get-tuple-element.25.a, bf16[16,4224]{1,0:T(8,128)(2,1)S(1)} %collective-permute-done.5.b, bf16[16,4224]{1,0:T(8,128)(2,1)S(1)} %collective-permute-done.6.c, bf16[16,2176]{1,0:T(8,128)(2,1)S(1)} %collective-permute-done.7.mine, ...), custom_call_target="tpu_custom_call" | custom-call | bytes 4194304 | tf_op jit(solution)/shard_map/down/pallas_call | solution.py:580
  65.4 8.1 %all-to-all-start.3 = ((bf16[16,2,896]{2,1,0:T(2,128)(2,1)}), bf16[16,2,896]{2,1,0:T(2,128)(2,1)S(1)}, u32[]{:S(2)}, u32[]{:S(2)}) async-start(bf16[16,2,896]{2,1,0:T(2,128)(2,1)} %down.1.after), calls=%async_computation.3 | async-start | bytes 114688 | tf_op jit(solution)/shard_map/all_to_all | solution.py:663
  73.8 1.7 %keep_own.1 = (bf16[16,8,16,512]{3,2,1,0:T(8,128)(2,1)}, bf16[16,64,128]{2,1,0:T(8,128)(2,1)}) custom-call(s32[64]{0:T(128)S(1)} %copy-done.5, s32[64]{0:T(128)S(1)} %copy-done.8, s32[2,4]{1,0:T(2,128)S(1)} %get-tuple-element.20.table, bf16[8,8,16,512]{3,2,1,0:T(8,128)(2,1)S(1)} %bitcast.7, bf16[8,64,128]{2,1,0:T(8,128)(2,1)S(1)} %copy-done.2, ...), custom_call_target="tpu_custom_call" | custom-call | bytes 6291456 | tf_op jit(solution)/shard_map/keep_own/pallas_call | solution.py:430
  75.4 1.6 %keep_moved.1 = (bf16[16,8,16,512]{3,2,1,0:T(8,128)(2,1)}, bf16[16,64,128]{2,1,0:T(8,128)(2,1)}) custom-call(s32[64]{0:T(128)S(1)} %copy-done.5, s32[64]{0:T(128)S(1)} %copy-done.8, s32[64]{0:T(128)S(1)} %get-tuple-element.31.source, bf16[16,80,512]{2,1,0:T(8,128)(2,1)S(1)} %all-to-all-done.2.pieces, ...), custom_call_target="tpu_custom_call", output_to_operand_aliasing={{0}: (4, {}), {1}: (5, {})} | custom-call | bytes 6291456 | tf_op jit(solution)/shard_map/keep_moved/pallas_call | solution.py:443
  (42 shorter events, 5.5 us)
Async XLA Ops:
  0.6 12.3 %copy-start = (bf16[8,128,512]{2,1,0:T(8,128)(2,1)S(1)}, bf16[8,128,512]{2,1,0:T(8,128)(2,1)}, u32[]{:S(2)}) copy-start(bf16[8,128,512]{2,1,0:T(8,128)(2,1)} %latent.1) | copy-start | bytes 3145732
  0.6 12.3 %copy-start.2 = (bf16[8,64,128]{2,1,0:T(8,128)(2,1)S(1)}, bf16[8,64,128]{2,1,0:T(8,128)(2,1)}, u32[]{:S(2)}) copy-start(bf16[8,64,128]{2,1,0:T(8,128)(2,1)} %rope.3) | copy-start | bytes 393220
  0.7 12.3 %copy-start.8 = (s32[64]{0:T(128)S(1)}, s32[64]{0:T(128)}, u32[]{:S(2)}) copy-start(s32[64]{0:T(128)} %lengths.5) | copy-start | bytes 772
  0.7 12.3 %copy-start.3 = (bf16[4,32,512]{2,1,0:T(8,128)(2,1)S(1)}, bf16[4,32,512]{2,1,0:T(8,128)(2,1)}, u32[]{:S(2)}) copy-start(bf16[4,32,512]{2,1,0:T(8,128)(2,1)} %q_latent.1) | copy-start | bytes 393220
  0.7 12.3 %copy-start.4 = (bf16[4,32,64]{2,1,0:T(8,128)(2,1)S(1)}, bf16[4,32,64]{2,1,0:T(8,128)(2,1)}, u32[]{:S(2)}) copy-start(bf16[4,32,64]{2,1,0:T(8,128)(2,1)} %q_rope.1) | copy-start | bytes 49156
  0.7 12.3 %copy-start.9 = (bf16[4,512]{1,0:T(4,128)(2,1)S(1)}, bf16[4,512]{1,0:T(4,128)(2,1)}, u32[]{:S(2)}) copy-start(bf16[4,512]{1,0:T(4,128)(2,1)} %fresh_latent.1) | copy-start | bytes 12292
  0.7 12.3 %copy-start.11 = (bf16[4,64]{1,0:T(4,128)(2,1)S(1)}, bf16[4,64]{1,0:T(4,128)(2,1)}, u32[]{:S(2)}) copy-start(bf16[4,64]{1,0:T(4,128)(2,1)} %fresh_rope.1) | copy-start | bytes 1540
  3.9 27.3 %all-to-all-start.1 = ((bf16[16,80,512]{2,1,0:T(8,128)(2,1)}), bf16[16,80,512]{2,1,0:T(8,128)(2,1)S(1)}, u32[]{:S(2)}, u32[]{:S(2)}) async-start(bf16[16,80,512]{2,1,0:T(8,128)(2,1)} %get-tuple-element.21), calls=%async_computation.1 | async-start | bytes 2621440 | tf_op jit(solution)/shard_map/all_to_all | solution.py:663
  17.1 1.3 %collective-permute-start = (bf16[128,256]{1,0:T(8,128)(2,1)S(1)}, bf16[128,256]{1,0:T(8,128)(2,1)S(1)}, u32[]{:S(2)}, u32[]{:S(2)}) collective-permute-start(bf16[128,256]{1,0:T(8,128)(2,1)S(1)} %attend.1.first), channel_id=1, source_target_pairs={{0,1},{1,0},{2,3},{3,2},{4,5},{5,4},{6,7},{7,6},{8,9},{9,8},{10,11... | collective-permute-start | bytes 196616 | tf_op jit(solution)/shard_map/ppermute | solution.py:650
  18.8 8.5 %collective-permute-start.1 = (bf16[128,256]{1,0:T(8,128)(2,1)S(1)}, bf16[128,256]{1,0:T(8,128)(2,1)S(1)}, u32[]{:S(2)}, u32[]{:S(2)}) collective-permute-start(bf16[128,256]{1,0:T(8,128)(2,1)S(1)} %join_pair.1.after.a), channel_id=1, source_target_pairs={{0,4},{1,5},{2,6},{3,7},{4,0},{5,1},{6,2},{7,3},{8,12},{9,13},{10,... | collective-permute-start | bytes 196616 | tf_op jit(solution)/shard_map/ppermute | solution.py:654
  22.1 5.2 %collective-permute-start.2 = (bf16[128,256]{1,0:T(8,128)(2,1)S(1)}, bf16[128,256]{1,0:T(8,128)(2,1)S(1)}, u32[]{:S(2)}, u32[]{:S(2)}) collective-permute-start(bf16[128,256]{1,0:T(8,128)(2,1)S(1)} %join_pair.1.after.a), channel_id=1, source_target_pairs={{0,6},{1,7},{2,0},{3,1},{4,2},{5,3},{6,4},{7,5},{8,14},{9,15},{10,... | collective-permute-start | bytes 196616 | tf_op jit(solution)/shard_map/ppermute | solution.py:654
  23.1 5.5 %collective-permute-start.3 = (bf16[128,256]{1,0:T(8,128)(2,1)S(1)}, bf16[128,256]{1,0:T(8,128)(2,1)S(1)}, u32[]{:S(2)}, u32[]{:S(2)}) collective-permute-start(bf16[128,256]{1,0:T(8,128)(2,1)S(1)} %join_pair.1.after.a), channel_id=1, source_target_pairs={{0,2},{1,3},{2,4},{3,5},{4,6},{5,7},{6,0},{7,1},{8,10},{9,11},{10,... | collective-permute-start | bytes 196616 | tf_op jit(solution)/shard_map/ppermute | solution.py:654
  30.7 17.0 %copy-start.12 = (bf16[896]{0:T(1024)(128)(2,1)S(1)}, bf16[896]{0:T(1024)(128)(2,1)}, u32[]{:S(2)}) copy-start(bf16[896]{0:T(1024)(128)(2,1)} %param.30) | copy-start | bytes 5380
  31.1 11.5 %all-to-all-start = ((bf16[16,4,896]{2,1,0:T(4,128)(2,1)}), bf16[16,4,896]{2,1,0:T(4,128)(2,1)S(1)}, u32[]{:S(2)}, u32[]{:S(2)}) async-start(bf16[16,4,896]{2,1,0:T(4,128)(2,1)} %hidden.1), calls=%async_computation | async-start | bytes 229376 | tf_op jit(solution)/shard_map/all_to_all | solution.py:663
  42.7 22.8 %all-to-all-start.2 = ((bf16[16,80,512]{2,1,0:T(8,128)(2,1)}), bf16[16,80,512]{2,1,0:T(8,128)(2,1)S(1)}, u32[]{:S(2)}, u32[]{:S(2)}) async-start(bf16[16,80,512]{2,1,0:T(8,128)(2,1)} %get-tuple-element.27), calls=%async_computation.2 | async-start | bytes 2621440 | tf_op jit(solution)/shard_map/all_to_all | solution.py:663
  47.7 15.4 %copy-start.1 = (bf16[1,2048,896]{2,1,0:T(8,128)(2,1)S(1)}, bf16[1,2048,896]{2,1,0:T(8,128)(2,1)}, u32[]{:S(2)}) copy-start(bf16[1,2048,896]{2,1,0:T(8,128)(2,1)} %w_down.1) | copy-start | bytes 11010052
  51.5 22.0 %copy-start.6 = (s32[8,4]{0,1:T(4,128)S(1)}, s32[8,4]{0,1:T(4,128)}, u32[]{:S(2)}) copy-start(s32[8,4]{0,1:T(4,128)} %param.34) | copy-start | bytes 388
  51.5 22.0 %copy-start.10 = (f32[8,4]{0,1:T(4,128)S(1)}, f32[8,4]{0,1:T(4,128)}, u32[]{:S(2)}) copy-start(f32[8,4]{0,1:T(4,128)} %param.35) | copy-start | bytes 388
  51.5 1.4 %collective-permute-start.4 = (bf16[16,4224]{1,0:T(8,128)(2,1)S(1)}, bf16[16,4224]{1,0:T(8,128)(2,1)S(1)}, u32[]{:S(2)}, u32[]{:S(2)}) collective-permute-start(bf16[16,4224]{1,0:T(8,128)(2,1)S(1)} %get-tuple-element.24), channel_id=1, source_target_pairs={{0,1},{1,0},{2,3},{3,2},{4,5},{5,4},{6,7},{7,6},{8,9},{9,8},{10,11... | collective-permute-start | bytes 405512 | tf_op jit(solution)/shard_map/ppermute | solution.py:650
  53.1 6.0 %collective-permute-start.7 = (bf16[16,2176]{1,0:T(8,128)(2,1)S(1)}, bf16[16,2176]{1,0:T(8,128)(2,1)S(1)}, u32[]{:S(2)}, u32[]{:S(2)}) collective-permute-start(bf16[16,2176]{1,0:T(8,128)(2,1)S(1)} %get-tuple-element.26), channel_id=1, source_target_pairs={{0,4},{1,5},{2,6},{3,7},{4,0},{5,1},{6,2},{7,3},{8,12},{9,13},{10,... | collective-permute-start | bytes 208904 | tf_op jit(solution)/shard_map/ppermute | solution.py:654
  55.7 5.9 %collective-permute-start.5 = (bf16[16,4224]{1,0:T(8,128)(2,1)S(1)}, bf16[16,4224]{1,0:T(8,128)(2,1)S(1)}, u32[]{:S(2)}, u32[]{:S(2)}) collective-permute-start(bf16[16,4224]{1,0:T(8,128)(2,1)S(1)} %get-tuple-element.25.a), channel_id=1, source_target_pairs={{0,6},{1,7},{2,0},{3,1},{4,2},{5,3},{6,4},{7,5},{8,14},{9,15},{10,... | collective-permute-start | bytes 405512 | tf_op jit(solution)/shard_map/ppermute | solution.py:654
  56.8 6.3 %collective-permute-start.6 = (bf16[16,4224]{1,0:T(8,128)(2,1)S(1)}, bf16[16,4224]{1,0:T(8,128)(2,1)S(1)}, u32[]{:S(2)}, u32[]{:S(2)}) collective-permute-start(bf16[16,4224]{1,0:T(8,128)(2,1)S(1)} %get-tuple-element.25.a), channel_id=1, source_target_pairs={{0,2},{1,3},{2,4},{3,5},{4,6},{5,7},{6,0},{7,1},{8,10},{9,11},{10,... | collective-permute-start | bytes 405512 | tf_op jit(solution)/shard_map/ppermute | solution.py:654
  59.1 4.0 %collective-permute-start.8 = (bf16[16,2176]{1,0:T(8,128)(2,1)S(1)}, bf16[16,2176]{1,0:T(8,128)(2,1)S(1)}, u32[]{:S(2)}, u32[]{:S(2)}) collective-permute-start(bf16[16,2176]{1,0:T(8,128)(2,1)S(1)} %collective-permute-done.7.mine), channel_id=1, source_target_pairs={{0,1},{1,0},{2,3},{3,2},{4,5},{5,4},{6,7},{7,6},{8,9},{9,8},{10,11... | collective-permute-start | bytes 208904 | tf_op jit(solution)/shard_map/ppermute | solution.py:650
  65.4 12.2 %all-to-all-start.3 = ((bf16[16,2,896]{2,1,0:T(2,128)(2,1)}), bf16[16,2,896]{2,1,0:T(2,128)(2,1)S(1)}, u32[]{:S(2)}, u32[]{:S(2)}) async-start(bf16[16,2,896]{2,1,0:T(2,128)(2,1)} %down.1.after), calls=%async_computation.3 | async-start | bytes 114688 | tf_op jit(solution)/shard_map/all_to_all | solution.py:663
  (2 other events, 21.0 us)
